TPU v7x, 32 devices: a whole 2x2x4 slice. The times are simulated.
32 devices in a mesh: dp: 16 (over z, y, x), tensor: 2 (over core).
Axes of the slice: x: 2, y: 2, z: 4, core: 2. Of those that a mesh axis runs over, the one named last changes fastest.
Arguments:
- tokens: bfloat16 [16384, 768], P(('dp', 'tensor')), may hold values from -6 to 6
- segment_ids: int32 [16384], P(('dp', 'tensor')), may hold values from 0 to 11, as said below
- w_query: bfloat16 [768, 768], P(None, 'tensor'), may hold values from -0.21875 to 0.21875
- w_key: bfloat16 [768, 768], P(None, 'tensor'), may hold values from -0.21875 to 0.21875
- w_value: bfloat16 [768, 768], P(None, 'tensor'), may hold values from -0.21875 to 0.21875
- b_query: float32 [768], P('tensor'), may hold values from -3 to 3
- b_value: float32 [768], P('tensor'), may hold values from -3 to 3
- w_out: bfloat16 [768, 768], P('tensor'), may hold values from -0.625 to 0.625
- b_out: float32 [768], replicated, may hold values from -3 to 3
- gain_attn: float32 [768], replicated, may hold values from 0.5 to 1.5
- shift_attn: float32 [768], replicated, may hold values from -3 to 3
- w_up: bfloat16 [768, 3072], P(None, 'tensor'), may hold values from -0.21875 to 0.21875
- b_up: float32 [3072], P('tensor'), may hold values from -3 to 3
- w_down: bfloat16 [3072, 768], P('tensor'), may hold values from -0.109375 to 0.109375
- b_down: float32 [768], replicated, may hold values from -3 to 3
- gain_ffn: float32 [768], replicated, may hold values from 0.5 to 1.5
- shift_ffn: float32 [768], replicated, may hold values from -2 to 2
- cotangent: bfloat16 [16384, 768], P(('dp', 'tensor')), may hold values from -7.5 to 7.5
Outputs:
- mixed: bfloat16 [16384, 768], P(('dp', 'tensor'))
- grad_tokens: float32 [16384, 768], P(('dp', 'tensor'))
- grad_w_query: float32 [768, 768], P(None, 'tensor')
- grad_w_key: float32 [768, 768], P(None, 'tensor')
- grad_w_value: float32 [768, 768], P(None, 'tensor')
- grad_b_query: float32 [768], P('tensor')
- grad_b_value: float32 [768], P('tensor')
- grad_w_out: float32 [768, 768], P('tensor')
- grad_b_out: float32 [768], replicated
- grad_gain_attn: float32 [768], replicated
- grad_shift_attn: float32 [768], replicated
- grad_w_up: float32 [768, 3072], P(None, 'tensor')
- grad_b_up: float32 [3072], P('tensor')
- grad_w_down: float32 [3072, 768], P('tensor')
- grad_b_down: float32 [768], replicated
- grad_gain_ffn: float32 [768], replicated
- grad_shift_ffn: float32 [768], replicated
Inputs may be any that keep to these rules, and one draw needn't show every extreme that they name: `segment_ids`: within each row of 1024 tokens the numbers start at 0 and never fall; equal numbers in one row mark one sentence or the row's trailing padding, which is never empty.
All inputs are finite; a program needn't handle non-finite values.
Results may differ from a plain program's by a relative error of at most 0.014.
Values may be sent and summed in bfloat16 or wider, within the bound.
No kernel may reach another device: no remote copies, remote signals or barrier semaphores. Data moves between devices by JAX's collectives and lax.ppermute only.
A program may use at most 128 MiB of HBM per device.

v0:
```python
from functools import partial

import jax
import jax.numpy as jnp
from jax import lax
from jax.sharding import PartitionSpec as P

HD = 64
LEN = 1024


EPSILON = 1e-05
MASKED = -1e30


def normalize_parts(hidden):
    average = jnp.mean(hidden, axis=-1, keepdims=True)
    centred = hidden - average
    spread = jnp.mean(centred * centred, axis=-1, keepdims=True)
    inverse = lax.rsqrt(spread + EPSILON)
    return (centred * inverse, inverse)


def normalize_back(grad_out, normed, inverse, gain):
    scaled = grad_out * gain
    first_mean = jnp.mean(scaled, axis=-1, keepdims=True)
    second_mean = jnp.mean(scaled * normed, axis=-1, keepdims=True)
    return inverse * (scaled - first_mean - normed * second_mean)


def exact_gelu(values):
    return jax.nn.gelu(values, approximate=False)


def masked_scores(queries, keys_all, query_seg, key_seg, factor):
    scores = (
        jnp.einsum("qhd,khd->hqk", queries, keys_all, preferred_element_type=jnp.float32) * factor
    )
    allowed = query_seg[:, None] == key_seg[None, :]
    return jnp.where(allowed[None], scores, MASKED)


def forward_block(queries, query_seg, keys_all, values_all, key_seg, factor):
    scores = masked_scores(queries, keys_all, query_seg, key_seg, factor)
    row_max = jnp.max(scores, axis=-1, keepdims=True)
    exponent = jnp.exp(scores - row_max)
    totals = jnp.sum(exponent, axis=-1, keepdims=True)
    attend = (exponent / totals).astype(jnp.bfloat16)
    context = jnp.einsum("hqk,khd->qhd", attend, values_all, preferred_element_type=jnp.float32)
    return (context, (row_max + jnp.log(totals))[..., 0])


def backward_block(carry, member, keys_all, values_all, key_seg, factor):
    grad_keys, grad_values = carry
    queries, query_seg, grad_context, log_total = member
    scores = masked_scores(queries, keys_all, query_seg, key_seg, factor)
    attend = jnp.exp(scores - log_total[..., None])
    grad_attend = jnp.einsum(
        "qhd,khd->hqk", grad_context, values_all, preferred_element_type=jnp.float32
    )
    inner = jnp.sum(attend * grad_attend, axis=-1, keepdims=True)
    grad_scores = (attend * (grad_attend - inner)).astype(jnp.bfloat16)
    grad_queries = (
        jnp.einsum("hqk,khd->qhd", grad_scores, keys_all, preferred_element_type=jnp.float32)
        * factor
    )
    grad_keys = (
        grad_keys
        + jnp.einsum("hqk,qhd->khd", grad_scores, queries, preferred_element_type=jnp.float32)
        * factor
    )
    grad_values = grad_values + jnp.einsum(
        "hqk,qhd->khd",
        attend.astype(jnp.bfloat16),
        grad_context,
        preferred_element_type=jnp.float32,
    )
    return ((grad_keys, grad_values), grad_queries)


def attention_forward(queries, keys_all, values_all, segments, block_rows, factor):
    heads_here = queries.shape[1]
    blocks = LEN // block_rows

    def one_block(member):
        return forward_block(member[0], member[1], keys_all, values_all, segments, factor)

    contexts, logs = lax.map(
        one_block,
        (queries.reshape(blocks, block_rows, heads_here, HD), segments.reshape(blocks, block_rows)),
    )
    return (contexts.reshape(LEN, heads_here * HD), logs)


def attention_backward(
    queries, keys_all, values_all, segments, grad_context, logs, block_rows, factor
):
    heads_here = queries.shape[1]
    blocks = LEN // block_rows
    stepper = partial(
        backward_block, keys_all=keys_all, values_all=values_all, key_seg=segments, factor=factor
    )
    starting = (
        jnp.zeros((LEN, heads_here, HD), jnp.float32),
        jnp.zeros((LEN, heads_here, HD), jnp.float32),
    )
    pieces = (
        queries.reshape(blocks, block_rows, heads_here, HD),
        segments.reshape(blocks, block_rows),
        grad_context.reshape(blocks, block_rows, heads_here, HD),
        logs,
    )
    (grad_keys, grad_values), grad_queries = lax.scan(stepper, starting, pieces)
    width = heads_here * HD
    return (
        grad_queries.reshape(LEN, width),
        grad_keys.reshape(LEN, width),
        grad_values.reshape(LEN, width),
    )


def shards(
    tokens,
    segment_ids,
    w_query,
    w_key,
    w_value,
    b_query,
    b_value,
    w_out,
    b_out,
    gain_attn,
    shift_attn,
    w_up,
    b_up,
    w_down,
    b_down,
    gain_ffn,
    shift_ffn,
    cotangent,
):
    factor = HD ** (-0.5)
    block_rows = min(512, LEN)
    inputs_all, segments_all = (
        lax.all_gather(tokens, "tensor", axis=0, tiled=True),
        lax.all_gather(segment_ids, "tensor", axis=0, tiled=True),
    )
    full_rows = inputs_all.shape[0]
    row_count = full_rows // LEN
    heads_here = w_query.shape[1] // HD
    width = heads_here * HD
    query_low = (jnp.dot(inputs_all, w_query, preferred_element_type=jnp.float32) + b_query).astype(
        jnp.bfloat16
    )
    key_low = jnp.dot(inputs_all, w_key, preferred_element_type=jnp.float32).astype(jnp.bfloat16)
    value_low = (jnp.dot(inputs_all, w_value, preferred_element_type=jnp.float32) + b_value).astype(
        jnp.bfloat16
    )
    query_rows = query_low.reshape(row_count, LEN, heads_here, HD)
    key_rows = key_low.reshape(row_count, LEN, heads_here, HD)
    value_rows = value_low.reshape(row_count, LEN, heads_here, HD)
    segment_rows = segments_all.reshape(row_count, LEN)

    def forward_row(member):
        return attention_forward(member[0], member[1], member[2], member[3], block_rows, factor)

    context_rows, log_rows = lax.map(forward_row, (query_rows, key_rows, value_rows, segment_rows))
    context_low = context_rows.reshape(full_rows, width).astype(jnp.bfloat16)
    hidden_one = (
        tokens.astype(jnp.float32)
        + lax.psum_scatter(
            jnp.dot(context_low, w_out, preferred_element_type=jnp.float32),
            "tensor",
            scatter_dimension=0,
            tiled=True,
        )
        + b_out
    )
    normed_one, inverse_one = normalize_parts(hidden_one)
    after_attn = normed_one * gain_attn + shift_attn
    after_all = lax.all_gather(after_attn.astype(jnp.bfloat16), "tensor", axis=0, tiled=True)
    upper = jnp.dot(after_all, w_up, preferred_element_type=jnp.float32) + b_up
    activated = exact_gelu(upper).astype(jnp.bfloat16)
    hidden_two = (
        after_attn
        + lax.psum_scatter(
            jnp.dot(activated, w_down, preferred_element_type=jnp.float32),
            "tensor",
            scatter_dimension=0,
            tiled=True,
        )
        + b_down
    )
    normed_two, inverse_two = normalize_parts(hidden_two)
    mixed = (normed_two * gain_ffn + shift_ffn).astype(jnp.bfloat16)
    outer = cotangent.astype(jnp.float32)
    grad_gain_ffn = jnp.sum(outer * normed_two, axis=0)
    grad_shift_ffn = jnp.sum(outer, axis=0)
    grad_two = normalize_back(outer, normed_two, inverse_two, gain_ffn)
    grad_b_down = jnp.sum(grad_two, axis=0)
    grad_two_all = lax.all_gather(grad_two.astype(jnp.bfloat16), "tensor", axis=0, tiled=True)
    upper_again = jnp.dot(after_all, w_up, preferred_element_type=jnp.float32) + b_up
    activated_f, gelu_pull = jax.vjp(exact_gelu, upper_again)
    activated_again = activated_f.astype(jnp.bfloat16)
    grad_w_down = jnp.einsum(
        "tf,td->fd", activated_again, grad_two_all, preferred_element_type=jnp.float32
    )
    grad_activated = jnp.einsum(
        "td,fd->tf", grad_two_all, w_down, preferred_element_type=jnp.float32
    )
    grad_upper = gelu_pull(grad_activated)[0].astype(jnp.bfloat16)
    grad_b_up = jnp.sum(grad_upper.astype(jnp.float32), axis=0)
    grad_w_up = jnp.einsum("td,tf->df", after_all, grad_upper, preferred_element_type=jnp.float32)
    grad_after = (
        lax.psum_scatter(
            jnp.einsum("tf,df->td", grad_upper, w_up, preferred_element_type=jnp.float32),
            "tensor",
            scatter_dimension=0,
            tiled=True,
        )
        + grad_two
    )
    grad_gain_attn = jnp.sum(grad_after * normed_one, axis=0)
    grad_shift_attn = jnp.sum(grad_after, axis=0)
    grad_one = normalize_back(grad_after, normed_one, inverse_one, gain_attn)
    grad_b_out = jnp.sum(grad_one, axis=0)
    grad_one_all = lax.all_gather(grad_one.astype(jnp.bfloat16), "tensor", axis=0, tiled=True)
    grad_w_out = jnp.einsum(
        "tc,td->cd", context_low, grad_one_all, preferred_element_type=jnp.float32
    )
    grad_context = jnp.einsum(
        "td,cd->tc", grad_one_all, w_out, preferred_element_type=jnp.float32
    ).astype(jnp.bfloat16)
    grad_context_rows = grad_context.reshape(row_count, LEN, heads_here, HD)

    def backward_row(member):
        return attention_backward(
            member[0], member[1], member[2], member[3], member[4], member[5], block_rows, factor
        )

    grad_query_rows, grad_key_rows, grad_value_rows = lax.map(
        backward_row, (query_rows, key_rows, value_rows, segment_rows, grad_context_rows, log_rows)
    )
    grad_query = grad_query_rows.reshape(full_rows, width).astype(jnp.bfloat16)
    grad_key = grad_key_rows.reshape(full_rows, width).astype(jnp.bfloat16)
    grad_value = grad_value_rows.reshape(full_rows, width).astype(jnp.bfloat16)
    grad_b_query = jnp.sum(grad_query.astype(jnp.float32), axis=0)
    grad_b_value = jnp.sum(grad_value.astype(jnp.float32), axis=0)
    grad_w_query = jnp.einsum(
        "td,tc->dc", inputs_all, grad_query, preferred_element_type=jnp.float32
    )
    grad_w_key = jnp.einsum("td,tc->dc", inputs_all, grad_key, preferred_element_type=jnp.float32)
    grad_w_value = jnp.einsum(
        "td,tc->dc", inputs_all, grad_value, preferred_element_type=jnp.float32
    )
    part_query = jnp.einsum("tc,dc->td", grad_query, w_query, preferred_element_type=jnp.float32)
    part_key = jnp.einsum("tc,dc->td", grad_key, w_key, preferred_element_type=jnp.float32)
    part_value = jnp.einsum("tc,dc->td", grad_value, w_value, preferred_element_type=jnp.float32)
    grad_tokens = (
        lax.psum_scatter(
            (part_query + part_key + part_value).astype(jnp.bfloat16),
            "tensor",
            scatter_dimension=0,
            tiled=True,
        ).astype(jnp.float32)
        + grad_one
    )
    grad_b_out, grad_gain_attn, grad_shift_attn, grad_b_down, grad_gain_ffn, grad_shift_ffn = (
        lax.psum(
            (
                grad_b_out,
                grad_gain_attn,
                grad_shift_attn,
                grad_b_down,
                grad_gain_ffn,
                grad_shift_ffn,
            ),
            ("dp", "tensor"),
        )
    )
    (
        grad_w_query,
        grad_w_key,
        grad_w_value,
        grad_b_query,
        grad_b_value,
        grad_w_out,
        grad_w_up,
        grad_b_up,
        grad_w_down,
    ) = lax.psum(
        (
            grad_w_query,
            grad_w_key,
            grad_w_value,
            grad_b_query,
            grad_b_value,
            grad_w_out,
            grad_w_up,
            grad_b_up,
            grad_w_down,
        ),
        "dp",
    )
    return (
        mixed,
        grad_tokens,
        grad_w_query,
        grad_w_key,
        grad_w_value,
        grad_b_query,
        grad_b_value,
        grad_w_out,
        grad_b_out,
        grad_gain_attn,
        grad_shift_attn,
        grad_w_up,
        grad_b_up,
        grad_w_down,
        grad_b_down,
        grad_gain_ffn,
        grad_shift_ffn,
    )


def solution(mesh):
    placed = (
        P(("dp", "tensor"), None),
        P(("dp", "tensor")),
        P(None, "tensor"),
        P(None, "tensor"),
        P(None, "tensor"),
        P("tensor"),
        P("tensor"),
        P("tensor", None),
        P(),
        P(),
        P(),
        P(None, "tensor"),
        P("tensor"),
        P("tensor", None),
        P(),
        P(),
        P(),
        P(("dp", "tensor"), None),
    )
    return jax.shard_map(
        shards,
        mesh=mesh,
        in_specs=placed,
        out_specs=(
            P(("dp", "tensor"), None),
            P(("dp", "tensor"), None),
            P(None, "tensor"),
            P(None, "tensor"),
            P(None, "tensor"),
            P("tensor"),
            P("tensor"),
            P("tensor", None),
            P(),
            P(),
            P(),
            P(None, "tensor"),
            P("tensor"),
            P("tensor", None),
            P(),
            P(),
            P(),
        ),
        check_vma=False,
    )
```

profile of v0, /device:TPU:0, one launch (start us, length us, event | category | flops | bytes accessed | tf_op | source)
XLA Modules:
  0.0 708.4 jit_solution(13895730562728678954)
XLA Ops:
  10.1 12.1 %all-gather.6.cloned.1.call-done = bf16[1024,768]{1,0:T(8,128)(2,1)} async-done(((bf16[512,768]{1,0:T(8,128)(2,1)}), bf16[1024,768]{1,0:T(8,128)(2,1)}) %all-gather.6.cloned.1.call-update) | async-done | bytes 1572880 | tf_op jit(solution)/shard_map/all_gather | solution.py:145
  22.1 3.5 add_convert_fusion.4
  28.5 2.3 copy.52
  30.7 2.4 convolution_convert_fusion.1
  35.8 25.5 %while.47 = (s32[]{:T(128)}, bf16[2,512,6,64]{1,3,2,0:T(8,128)(2,1)}, f32[2,6,512]{2,1,0:T(8,128)S(1)}, s32[2,512]{1,0:T(2,128)S(1)}, s32[1024]{0:T(1024)S(1)}, ...) while((s32[]{:T(128)}, ...), condition=%wide.region_3.4_spmd, body=%wide.region_0.3_spmd.sunk | while | flops 843576320 | bytes 52164808 | solution.py:88
  36.2 3.4 fusion.124
  39.6 3.6 fusion.125
  43.2 4.4 fusion.126
  48.9 3.4 fusion.124
  52.3 3.6 fusion.125
  56.0 4.4 fusion.126
  64.3 2.7 fusion.55
  67.1 12.2 %reduce-scatter.5.cloned.1.call-done = f32[512,768]{1,0:T(8,128)} async-done(((f32[1024,768]{1,0:T(8,128)}), f32[512,768]{1,0:T(8,128)}) %reduce-scatter.5.cloned.1.call-update) | async-done | bytes 1572880 | tf_op jit(solution)/shard_map/reduce_scatter | solution.py:171
  83.8 10.9 %all-gather.8.cloned.1.call-done = bf16[1024,768]{1,0:T(8,128)(2,1)} async-done(((bf16[512,768]{1,0:T(8,128)(2,1)}), bf16[1024,768]{1,0:T(8,128)(2,1)}) %all-gather.8.cloned.1.call-update) | async-done | bytes 1572880 | tf_op jit(solution)/shard_map/all_gather | solution.py:181
  94.7 18.3 %multiply_convert_fusion.1 = (bf16[1024,1536]{1,0:T(8,128)(2,1)S(1)}, f32[1024,1536]{1,0:T(8,128)}, f32[1024,1536]{1,0:T(8,128)}) fusion(f32[1536]{0:T(1024)S(1)} %copy-done.56, bf16[1024,768]{1,0:T(8,128)(2,1)} %all-gather.8.cloned.1.call-done, bf16[768,1536]{1,0:T(8,128)(2,1)S(1)} %copy-done), kind=kOutput, calls=%fused_computation.51 | convolution fusion | flops 2519728128 | bytes 19666944 | tf_op jit(solution)/shard_map/dot_general | solution.py:182
  114.6 4.3 fusion.56
  119.0 12.2 %reduce-scatter.7.cloned.1.call-done = f32[512,768]{1,0:T(8,128)} async-done(((f32[1024,768]{1,0:T(8,128)}), f32[512,768]{1,0:T(8,128)}) %reduce-scatter.7.cloned.1.call-update) | async-done | bytes 1572880 | tf_op jit(solution)/shard_map/reduce_scatter | solution.py:186
  131.1 2.5 fusion.52
  135.3 2.1 fusion.49
  140.1 10.7 %all-gather.10.cloned.1.call-done = bf16[1024,768]{1,0:T(8,128)(2,1)} async-done(((bf16[512,768]{1,0:T(8,128)(2,1)}), bf16[1024,768]{1,0:T(8,128)(2,1)}) %all-gather.10.cloned.1.call-update) | async-done | bytes 1572880 | tf_op jit(solution)/shard_map/all_gather | solution.py:201
  150.7 10.8 %convert_reduce_fusion = (f32[1536]{0:T(1024)}, bf16[1024,1536]{1,0:T(8,128)(2,1)S(1)}) fusion(f32[1024,1536]{1,0:T(8,128)} %get-tuple-element.392, f32[1024,1536]{1,0:T(8,128)} %get-tuple-element.400, f32[1536]{0:T(1024)S(1)} %copy-done.56, bf16[1024,768]{1,0:T(8,128)(2,1)} %all-gather.10.cloned.1.call-done, bf16[1536,768]{1,0:T(8,128)(2,1)} %param.35), kind=kOutput, calls=%fused_computation.49 | convolution fusion | flops 2442656256 | bytes 19673088 | tf_op jit(solution)/shard_map/td,fd->tf/dot_general | solution.py:208
  163.2 4.3 fusion.57
  167.5 12.2 %reduce-scatter.9.cloned.1.call-done = f32[512,768]{1,0:T(8,128)} async-done(((f32[1024,768]{1,0:T(8,128)}), f32[512,768]{1,0:T(8,128)}) %reduce-scatter.9.cloned.1.call-update) | async-done | bytes 1572880 | tf_op jit(solution)/shard_map/reduce_scatter | solution.py:215
  179.7 3.3 multiply_reduce_fusion.1
  186.4 11.1 %all-gather.12.cloned.1.call-done = bf16[1024,768]{1,0:T(8,128)(2,1)} async-done(((bf16[512,768]{1,0:T(8,128)(2,1)}), bf16[1024,768]{1,0:T(8,128)(2,1)}) %all-gather.12.cloned.1.call-update) | async-done | bytes 1572880 | tf_op jit(solution)/shard_map/all_gather | solution.py:227
  197.4 3.3 convolution_convert_fusion
  203.6 2.1 copy.56
  206.6 49.3 %while.48 = (s32[]{:T(128)}, f32[1024,6,64]{0,2,1:T(8,128)S(1)}, f32[1024,6,64]{0,2,1:T(8,128)}, bf16[2,512,6,64]{1,3,2,0:T(8,128)(2,1)}, bf16[2,512,6,64]{1,3,2...) while((s32[]{:T(128)}, f32[1024,6,64]{0,2,1:T(8,128)S(1)}, ...), condition=%wide.region_17.18_spmd.clone, body=%wide.region_15.17_spmd.clone.sunk | while | flops 2063135744 | bytes 135895408 | solution.py:113
  207.2 3.0 fusion.136
  210.2 3.5 bitcast_add_fusion.5
  213.8 7.1 %multiply_reduce_fusion.7 = (f32[6,512]{1,0:T(8,128)S(1)}, f32[6,512,1024]{2,1,0:T(8,128)}) fusion(f32[6,512,1024]{2,1,0:T(8,128)S(1)} %fusion.136, f32[6,512]{1,0:T(8,128)S(1)} %dynamic-slice_bitcast_fusion.2, pred[512,1024]{1,0:T(8,128)(4,1)S(1)} %broadcast_compare_fusion.5, bf16[1024,6,64]{0,2,1:T(8,128)(2,1)S(1)} %copy-done.6, ...), kind=kOutput, calls=%fused_computation.18.clone.1 | convolution fusion | flops 418378752 | bytes 26898436 | tf_op jit(solution)/shard_map/while/body/eval_jaxpr/while/body/eval_jaxpr/qhd,khd->hqk/dot_general | solution.py:58
  220.9 6.9 multiply_convert_fusion.3
  231.7 3.0 fusion.136
  234.7 3.5 bitcast_add_fusion.5
  238.3 7.1 %multiply_reduce_fusion.7 = (f32[6,512]{1,0:T(8,128)S(1)}, f32[6,512,1024]{2,1,0:T(8,128)}) fusion(f32[6,512,1024]{2,1,0:T(8,128)S(1)} %fusion.136, f32[6,512]{1,0:T(8,128)S(1)} %dynamic-slice_bitcast_fusion.2, pred[512,1024]{1,0:T(8,128)(4,1)S(1)} %broadcast_compare_fusion.5, bf16[1024,6,64]{0,2,1:T(8,128)(2,1)S(1)} %copy-done.6, ...), kind=kOutput, calls=%fused_computation.18.clone.1 | convolution fusion | flops 418378752 | bytes 26898436 | tf_op jit(solution)/shard_map/while/body/eval_jaxpr/while/body/eval_jaxpr/qhd,khd->hqk/dot_general | solution.py:58
  245.4 6.9 multiply_convert_fusion.3
  256.1 2.3 copy.57
  261.2 2.3 add_convert_fusion.1
  263.6 7.4 %fusion.62 = f32[1536,768]{1,0:T(8,128)} fusion(bf16[1024,1536]{1,0:T(8,128)(2,1)} %copy-done.58, bf16[1024,768]{1,0:T(8,128)(2,1)} %all-gather.10.cloned.1.call-done), kind=kOutput, calls=%fused_computation.119 | convolution fusion | flops 2415919104 | bytes 9437184 | tf_op jit(solution)/shard_map/tf,td->fd/dot_general | solution.py:205
  271.0 4.4 fusion.61
  283.3 44.6 %all-reduce = (f32[768]{0:T(1024)}, f32[768]{0:T(1024)}, f32[768]{0:T(1024)}, f32[768]{0:T(1024)}, f32[768]{0:T(1024)}, /*index=5*/f32[768]{0:T(1024)}) all-reduce(f32[768]{0:T(1024)S(1)} %copy-done.42, f32[768]{0:T(1024)S(1)} %copy-done.46, f32[768]{0:T(1024)S(1)} %copy-done.47, ...), channel_id=1, replica_groups=mesh['dp'=16,'tensor'=2] {'dp','tensor'}, use_global_device_ids=true, to_apply=%region_28.29 | all-reduce | flops 4608 | bytes 36864 | tf_op jit(solution)/shard_map/psum | solution.py:269
  328.2 79.8 %all-reduce.1 = (f32[384]{0:T(512)}, f32[384]{0:T(512)}, f32[1536]{0:T(1024)}) all-reduce(f32[384]{0:T(512)S(1)} %reduce_sum.184, f32[384]{0:T(512)S(1)} %reduce_sum.186, f32[1536]{0:T(1024)S(1)} %copy-done.48), channel_id=1, replica_groups=mesh['dp'=16,'tensor'=2] {'dp'}, use_global_device_ids=true, to_apply=%region_23.24 | all-reduce | flops 2304 | bytes 18432 | tf_op jit(solution)/shard_map/psum | solution.py:291
  408.1 2.4 convert_add_fusion
  410.5 275.4 %all-reduce.5.cloned.1.call-done = (f32[768,384]{0,1:T(8,128)}, f32[768,384]{0,1:T(8,128)}, f32[768,384]{0,1:T(8,128)}, f32[384,768]{1,0:T(8,128)}, f32[768,1536]{1,0:T(8,128)}, /*index=5*/f32[1536,768]{1,0:T(8,128)}) async-done(((f32[768,384]{0,1:T(8,128)}, f32[768,384]{0,1:T(8,128)}, f32[768,384]{0,1:T(8,128)}, f32[384,768]{1,0:T(8,128)}, f32[768,1536]{1,0:T(8,128)}, /*index=5*/f32[1536,768]{1,0:T(8,128)}), ...) | async-done | bytes 14155792 | tf_op jit(solution)/shard_map/psum | solution.py:291
  685.9 2.8 copy.58
  688.7 2.7 copy.59
  693.8 5.5 copy.97
  699.3 2.2 copy.98
  (221 shorter events, 54.2 us)
Async XLA Ops:
  7.2 87.5 %copy-start = (bf16[768,1536]{1,0:T(8,128)(2,1)S(1)}, bf16[768,1536]{1,0:T(8,128)(2,1)}, u32[]{:S(2)}) copy-start(bf16[768,1536]{1,0:T(8,128)(2,1)} %param.33) | copy-start | bytes 7077892
  7.2 14.9 %all-gather.6.cloned.1.call-start = ((), (), s32[]{:S(2)}) async-start(), calls=%async_computation.4 | async-start | bytes 2359296 | tf_op jit(solution)/shard_map/all_gather | solution.py:145
  7.9 71.3 %reduce-scatter.5.cloned.1.call-start = ((), (), s32[]{:S(2)}) async-start(), calls=%async_computation.5 | async-start | bytes 4718592 | tf_op jit(solution)/shard_map/reduce_scatter | solution.py:171
  27.0 6.1 copy-start.57
  28.5 4.6 copy-start.37
  28.5 4.6 copy-start.53
  39.5 3.7 copy-start.5
  39.5 3.7 copy-start.16
  52.3 3.7 copy-start.5
  52.3 3.7 copy-start.16
  61.3 3.0 copy-start.33
  64.3 14.9 %copy-start.49 = (f32[768]{0:T(1024)S(1)}, f32[768]{0:T(1024)}, u32[]{:S(2)}) copy-start(f32[768]{0:T(1024)} %param.30) | copy-start | bytes 9220
  67.1 15.3 %copy-start.39 = (f32[768]{0:T(1024)S(1)}, f32[768]{0:T(1024)}, u32[]{:S(2)}) copy-start(f32[768]{0:T(1024)} %param.31) | copy-start | bytes 9220
  67.1 15.3 %copy-start.43 = (f32[768]{0:T(1024)S(1)}, f32[768]{0:T(1024)}, u32[]{:S(2)}) copy-start(f32[768]{0:T(1024)} %param.32) | copy-start | bytes 9220
  67.1 27.6 %all-gather.8.cloned.1.call-start = ((), (), s32[]{:S(2)}) async-start(), calls=%async_computation.6 | async-start | bytes 2359296 | tf_op jit(solution)/shard_map/all_gather | solution.py:181
  81.2 13.5 %copy-start.56 = (f32[1536]{0:T(1024)S(1)}, f32[1536]{0:T(1024)}, u32[]{:S(2)}) copy-start(f32[1536]{0:T(1024)} %param.34) | copy-start | bytes 18436
  83.5 47.6 %reduce-scatter.7.cloned.1.call-start = ((), (), s32[]{:S(2)}) async-start(), calls=%async_computation.7 | async-start | bytes 4718592 | tf_op jit(solution)/shard_map/reduce_scatter | solution.py:186
  94.7 19.9 %copy-start.52 = (bf16[1536,768]{1,0:T(8,128)(2,1)S(1)}, bf16[1536,768]{1,0:T(8,128)(2,1)}, u32[]{:S(2)}) copy-start(bf16[1536,768]{1,0:T(8,128)(2,1)} %param.35) | copy-start | bytes 7077892
  118.9 12.2 %copy-start.50 = (f32[768]{0:T(1024)S(1)}, f32[768]{0:T(1024)}, u32[]{:S(2)}) copy-start(f32[768]{0:T(1024)} %param.36) | copy-start | bytes 9220
  118.9 15.1 %copy-start.44 = (f32[768]{0:T(1024)S(1)}, f32[768]{0:T(1024)}, u32[]{:S(2)}) copy-start(f32[768]{0:T(1024)} %param.37) | copy-start | bytes 9220
  118.9 31.8 %all-gather.10.cloned.1.call-start = ((), (), s32[]{:S(2)}) async-start(), calls=%async_computation.8 | async-start | bytes 2359296 | tf_op jit(solution)/shard_map/all_gather | solution.py:201
  139.6 40.1 %reduce-scatter.9.cloned.1.call-start = ((), (), s32[]{:S(2)}) async-start(), calls=%async_computation.9 | async-start | bytes 4718592 | tf_op jit(solution)/shard_map/reduce_scatter | solution.py:215
  167.5 12.3 %copy-start.4 = (f32[512,768]{1,0:T(8,128)S(1)}, f32[512,768]{1,0:T(8,128)}, u32[]{:S(2)}) copy-start(f32[512,768]{1,0:T(8,128)} %copy-done.3) | copy-start | bytes 4718596
  167.5 29.9 %all-gather.12.cloned.1.call-start = ((), (), s32[]{:S(2)}) async-start(), calls=%async_computation.10 | async-start | bytes 2359296 | tf_op jit(solution)/shard_map/all_gather | solution.py:227
  183.1 14.4 %copy-start.34 = (bf16[384,768]{1,0:T(8,128)(2,1)S(1)}, bf16[384,768]{1,0:T(8,128)(2,1)}, u32[]{:S(2)}) copy-start(bf16[384,768]{1,0:T(8,128)(2,1)} %param.29) | copy-start | bytes 1769476
  186.3 221.8 %reduce-scatter.11.cloned.1.call-start = ((), (), s32[]{:S(2)}) async-start(), calls=%async_computation.11 | async-start | bytes 2359296 | tf_op jit(solution)/shard_map/reduce_scatter | solution.py:260
  207.2 3.0 copy-start.10
  207.2 3.0 copy-start.28
  210.2 3.5 copy-start.6
  213.8 7.1 %copy-start.29 = (f32[1024,6,64]{0,2,1:T(8,128)}, f32[1024,6,64]{0,2,1:T(8,128)S(1)}, u32[]{:S(2)}) copy-start(f32[1024,6,64]{0,2,1:T(8,128)S(1)} %bitcast_add_fusion.5) | copy-start | bytes 4718596 | tf_op jit(solution)/shard_map/while/body/eval_jaxpr/while
  220.9 6.9 copy-start.11
  234.7 3.5 copy-start.6
  238.3 7.1 %copy-start.29 = (f32[1024,6,64]{0,2,1:T(8,128)}, f32[1024,6,64]{0,2,1:T(8,128)S(1)}, u32[]{:S(2)}) copy-start(f32[1024,6,64]{0,2,1:T(8,128)S(1)} %bitcast_add_fusion.5) | copy-start | bytes 4718596 | tf_op jit(solution)/shard_map/while/body/eval_jaxpr/while
  245.4 6.9 copy-start.11
  256.1 3.7 copy-start.25
  263.5 7.4 %copy-start.19 = (bf16[1024,1536]{1,0:T(8,128)(2,1)S(1)}, bf16[1024,1536]{1,0:T(8,128)(2,1)}, u32[]{:S(2)}) copy-start(bf16[1024,1536]{1,0:T(8,128)(2,1)} %copy-done.18) | copy-start | bytes 9437188
  263.5 422.4 %all-reduce.5.cloned.1.call-start = ((), (), s32[]{:S(2)}) async-start(), calls=%async_computation.12 | async-start | bytes 28311552 | tf_op jit(solution)/shard_map/psum | solution.py:291
  263.6 7.4 %copy-start.27 = (bf16[1024,768]{1,0:T(8,128)(2,1)S(1)}, bf16[1024,768]{1,0:T(8,128)(2,1)}, u32[]{:S(2)}) copy-start(bf16[1024,768]{1,0:T(8,128)(2,1)} %all-gather.8.cloned.1.call-done) | copy-start | bytes 4718596
  270.9 4.4 copy-start.21
  271.0 4.4 copy-start.55
  282.5 45.3 %copy-start.13 = (bf16[2,512,6,64]{1,3,2,0:T(8,128)(2,1)S(1)}, bf16[2,512,6,64]{1,3,2,0:T(8,128)(2,1)}, u32[]{:S(2)}) copy-start(bf16[2,512,6,64]{1,3,2,0:T(8,128)(2,1)} %get-tuple-element.172) | copy-start | bytes 2359300
  282.5 45.7 %copy-start.48 = (f32[1536]{0:T(1024)S(1)}, f32[1536]{0:T(1024)}, u32[]{:S(2)}) copy-start(f32[1536]{0:T(1024)} %get-tuple-element.384) | copy-start | bytes 18436
  282.6 125.5 %copy-start.8 = (f32[512,768]{1,0:T(8,128)S(1)}, f32[512,768]{1,0:T(8,128)}, u32[]{:S(2)}) copy-start(f32[512,768]{1,0:T(8,128)} %copy-done.7) | copy-start | bytes 4718596
  685.9 5.5 copy-start.32
  685.9 6.8 copy-start.31
  692.8 6.5 slice-start
  693.8 5.5 slice-start.1
  693.8 7.7 %copy-start.1 = (bf16[768,1536]{1,0:T(8,128)(2,1)S(1)}, bf16[768,1536]{1,0:T(8,128)(2,1)}, u32[]{:S(2)}) copy-start(bf16[768,1536]{1,0:T(8,128)(2,1)} %param.33) | copy-start | bytes 7077892
  (32 other events, 50.1 us)
Sparse Core Ops, SparseCore 0:
  9.6 12.4 all-gather.5
  67.2 12.0 reduce-scatter.4
  83.7 10.9 all-gather.7
  119.0 12.0 reduce-scatter.6
  139.7 10.9 all-gather.9
  167.6 12.0 reduce-scatter.8
  186.4 10.9 all-gather.11
  263.6 10.2 reduce-scatter.10
  282.7 403.1 all-reduce.4
where the time goes:
time: 717 us; the launch traced here: 708 us
  waiting for transfers between devices  357 us (50%)
  blocking collectives  127 us (18%)
  matrix products  124 us (17%)
  local copies, waits for them, and re-layouts  42.5 us (6%)
  other arithmetic  41.5 us (6%)
  between operations  14.7 us (2%)
    psum x1, waiting for transfers between devices, shards(): lax.psum((grad_w_query, grad_w_key, grad_w_value, grad_b_query, grad_b_va...  275 us
    psum x1, blocking collectives, shards(): lax.psum((grad_w_query, grad_w_key, grad_w_value, grad_b_query, grad_b_va...  79.8 us
    psum x1, blocking collectives, shards(): lax.psum((grad_b_out, grad_gain_attn, grad_shift_attn, grad_b_down, grad_...  44.6 us
    unnamed x112, local copies, waits for them, and re-layouts  26.4 us
    dot_general x1, matrix products, shards(): upper = jnp.dot(after_all, w_up, preferred_element_type=jnp.float32) + b_up  18.3 us
  transfers between devices with their start and end apart: 9, of which 8 were waited for; matrix products, arithmetic and copies ran while one was open for 3% of the time, Pallas kernels for 0%

commit v1 on v0

v1 whole, which is shorter than its diff:
```python
from functools import partial

import jax
import jax.numpy as jnp
from jax import lax
from jax.experimental import pallas as pl
from jax.experimental.pallas import tpu as pltpu
from jax.sharding import PartitionSpec as P

HD = 64
LEN = 1024
EPSILON = 1e-05
MASKED = -1e30
SCALE = HD**-0.5
BLOCKS = 16
PAIR = 2 * HD
MIB = 1 << 20

RATE = 0.43
TERMS = (
    0.12126930983343633,
    0.12199507019903895,
    0.1037291362969846,
    0.11912425719127386,
    -0.03444926125853447,
    0.18241234969276796,
    -0.14954241308342106,
    0.035461460124125724,
)

F32 = jnp.float32
BF16 = jnp.bfloat16


def nn(left, right):
    return lax.dot_general(left, right, (((1,), (0,)), ((), ())), preferred_element_type=F32)


def nt(left, right):
    return lax.dot_general(left, right, (((1,), (1,)), ((), ())), preferred_element_type=F32)


def tn(left, right):
    return lax.dot_general(left, right, (((0,), (0,)), ((), ())), preferred_element_type=F32)


def normalize_parts(hidden):
    average = jnp.mean(hidden, axis=-1, keepdims=True)
    centred = hidden - average
    spread = jnp.mean(centred * centred, axis=-1, keepdims=True)
    inverse = lax.rsqrt(spread + EPSILON)
    return centred * inverse, inverse


def normalize_back(grad_out, normed, inverse, gain):
    scaled = grad_out * gain
    first_mean = jnp.mean(scaled, axis=-1, keepdims=True)
    second_mean = jnp.mean(scaled * normed, axis=-1, keepdims=True)
    return inverse * (scaled - first_mean - normed * second_mean)


def gelu_parts(upper):
    size = jnp.abs(upper) * (0.5**0.5)
    t = 1.0 / (1.0 + RATE * size)
    series = TERMS[-1] * t + TERMS[-2]
    for term in TERMS[-3::-1]:
        series = series * t + term
    bell = jnp.exp(upper * upper * -0.5)
    tail = series * t * bell
    phi = jnp.where(upper >= 0.0, 1.0 - tail, tail)
    return upper * phi, phi + upper * bell * 0.3989422804014327


def call(kernel, outs, ins, scratch=(), limit=48, smem=(), flops=0, moved=0):
    moved = moved or sum(a.size * a.dtype.itemsize for a in ins) + sum(
        o.size * o.dtype.itemsize for o in outs
    )
    return pl.pallas_call(
        kernel,
        out_shape=outs,
        in_specs=[
            pl.BlockSpec(memory_space=pltpu.SMEM if i in smem else pltpu.VMEM)
            for i in range(len(ins))
        ],
        out_specs=[pl.BlockSpec(memory_space=pltpu.VMEM) for _ in outs],
        scratch_shapes=list(scratch),
        compiler_params=pltpu.CompilerParams(vmem_limit_bytes=limit * MIB),
        cost_estimate=pl.CostEstimate(flops=flops, bytes_accessed=moved, transcendentals=0),
    )(*ins)


def shape(*dims, dtype=F32):
    return jax.ShapeDtypeStruct(dims, dtype)


def fill_bias(bias, segc_ref, segr_ref):
    bias[...] = jnp.where(segc_ref[...] == segr_ref[0], 0.0, MASKED)


def attend_kernel(
    x_ref, wq_ref, wk_ref, wv_ref, bq_ref, bv_ref, segr_ref, segc_ref,
    q_ref, k_ref, v_ref, ctx_ref, lse_ref,
    bias, vt, ctxt,
):
    heads = q_ref.shape[1] // HD
    block = 256
    x = x_ref[...]
    fill_bias(bias, segc_ref, segr_ref)
    q_ref[...] = ((nn(x, wq_ref[...]) + bq_ref[...]) * SCALE).astype(BF16)
    k_ref[...] = nn(x, wk_ref[...]).astype(BF16)
    value = (nn(x, wv_ref[...]) + bv_ref[...]).astype(BF16)
    v_ref[...] = value
    vt[...] = value.T

    @pl.loop(0, LEN // block)
    def _(j):
        here = pl.ds(pl.multiple_of(j * block, block), block)
        for pair in range(heads // 2):
            lanes = pl.ds(pair * PAIR, PAIR)
            keys = k_ref[:, lanes]
            queries = q_ref[here, lanes]
            owner = lax.broadcasted_iota(jnp.int32, queries.shape, 1) // HD
            for side in range(2):
                head = 2 * pair + side
                mine = jnp.where(owner == side, queries, jnp.zeros_like(queries))
                scores = nt(keys, mine) + bias[:, here]
                top = jnp.max(scores, axis=0, keepdims=True)
                weight = jnp.exp(scores - top)
                total = jnp.sum(weight, axis=0, keepdims=True)
                out = nn(vt[pl.ds(head * HD, HD), :], weight.astype(BF16))
                ctxt[pl.ds(head * HD, HD), here] = out * (1.0 / total)
                lse_ref[0, pl.ds(head, 1), here] = top + jnp.log(total)

    ctx_ref[...] = ctxt[...].T.astype(BF16)


def attention_forward(tokens, w_query, w_key, w_value, b_query, b_value, seg_rows, seg_cols):
    rows, width = seg_rows.shape[0], w_query.shape[1]
    model = tokens.shape[1]
    by_row = pl.BlockSpec((LEN, width), lambda r: (r, 0))
    whole = lambda *dims: pl.BlockSpec(dims, lambda r: (0,) * len(dims))
    flops = rows * (2 * LEN * model * 3 * width + 4 * 4 * LEN * LEN * width)
    return pl.pallas_call(
        attend_kernel,
        grid=(rows,),
        out_shape=[
            shape(rows * LEN, width, dtype=BF16),
            shape(rows * LEN, width, dtype=BF16),
            shape(rows * LEN, width, dtype=BF16),
            shape(rows * LEN, width, dtype=BF16),
            shape(rows, 8, LEN),
        ],
        in_specs=[
            pl.BlockSpec((LEN, model), lambda r: (r, 0)),
            whole(model, width),
            whole(model, width),
            whole(model, width),
            whole(1, width),
            whole(1, width),
            pl.BlockSpec((1, 1, LEN), lambda r: (r, 0, 0)),
            pl.BlockSpec((LEN, 1), lambda r: (r, 0)),
        ],
        out_specs=[by_row] * 4 + [pl.BlockSpec((1, 8, LEN), lambda r: (r, 0, 0))],
        scratch_shapes=[
            pltpu.VMEM((LEN, LEN), F32),
            pltpu.VMEM((width, LEN), BF16),
            pltpu.VMEM((width, LEN), F32),
        ],
        compiler_params=pltpu.CompilerParams(vmem_limit_bytes=40 * MIB),
        cost_estimate=pl.CostEstimate(flops=flops, bytes_accessed=8 * MIB, transcendentals=0),
    )(tokens, w_query, w_key, w_value, b_query, b_value, seg_rows, seg_cols)


def attend_back_kernel(
    q_ref, k_ref, v_ref, ctx_ref, dctx_ref, lse_ref, segr_ref, segc_ref,
    dq_ref, dk_ref, dv_ref,
    bias, kt, dqt, dk_sum, dv_sum, inner,
):
    width = q_ref.shape[1]
    heads = width // HD
    block = 256
    fill_bias(bias, segc_ref, segr_ref)
    kt[...] = k_ref[...].T
    picks = lax.broadcasted_iota(jnp.int32, (8, width), 0) == (
        lax.broadcasted_iota(jnp.int32, (8, width), 1) // HD
    )
    product = ctx_ref[...].astype(F32) * dctx_ref[...].astype(F32)
    inner[...] = lax.dot_general(
        picks.astype(F32), product, (((1,), (1,)), ((), ())),
        precision=lax.Precision.HIGHEST, preferred_element_type=F32,
    )
    dk_sum[...] = jnp.zeros_like(dk_sum)
    dv_sum[...] = jnp.zeros_like(dv_sum)

    @pl.loop(0, LEN // block)
    def _(j):
        here = pl.ds(pl.multiple_of(j * block, block), block)
        for pair in range(heads // 2):
            lanes = pl.ds(pair * PAIR, PAIR)
            keys, values = k_ref[:, lanes], v_ref[:, lanes]
            queries, grads = q_ref[here, lanes], dctx_ref[here, lanes]
            owner = lax.broadcasted_iota(jnp.int32, queries.shape, 1) // HD
            for side in range(2):
                head = 2 * pair + side
                query = jnp.where(owner == side, queries, jnp.zeros_like(queries))
                grad = jnp.where(owner == side, grads, jnp.zeros_like(grads))
                scores = nt(keys, query) + bias[:, here]
                weight = jnp.exp(scores - lse_ref[0, pl.ds(head, 1), here])
                slope = nt(values, grad) - inner[pl.ds(head, 1), here]
                change = (weight * slope).astype(BF16)
                dv_sum[:, lanes] += nn(weight.astype(BF16), grad)
                dk_sum[:, lanes] += nn(change, query)
                dqt[pl.ds(head * HD, HD), here] = nn(kt[pl.ds(head * HD, HD), :], change) * SCALE

    dq_ref[...] = dqt[...].T.astype(BF16)
    dk_ref[...] = dk_sum[...].astype(BF16)
    dv_ref[...] = dv_sum[...].astype(BF16)


def attention_backward(query, key, value, context, grad_context, lse, seg_rows, seg_cols):
    rows, width = seg_rows.shape[0], query.shape[1]
    by_row = pl.BlockSpec((LEN, width), lambda r: (r, 0))
    flops = rows * 4 * 10 * LEN * LEN * width
    return pl.pallas_call(
        attend_back_kernel,
        grid=(rows,),
        out_shape=[shape(rows * LEN, width, dtype=BF16)] * 3,
        in_specs=[by_row] * 5
        + [
            pl.BlockSpec((1, 8, LEN), lambda r: (r, 0, 0)),
            pl.BlockSpec((1, 1, LEN), lambda r: (r, 0, 0)),
            pl.BlockSpec((LEN, 1), lambda r: (r, 0)),
        ],
        out_specs=[by_row] * 3,
        scratch_shapes=[
            pltpu.VMEM((LEN, LEN), F32),
            pltpu.VMEM((width, LEN), BF16),
            pltpu.VMEM((width, LEN), F32),
            pltpu.VMEM((LEN, width), F32),
            pltpu.VMEM((LEN, width), F32),
            pltpu.VMEM((8, LEN), F32),
        ],
        compiler_params=pltpu.CompilerParams(vmem_limit_bytes=40 * MIB),
        cost_estimate=pl.CostEstimate(flops=flops, bytes_accessed=8 * MIB, transcendentals=0),
    )(query, key, value, context, grad_context, lse, seg_rows, seg_cols)


def pack_down(order, total, out_ref):
    part, _, wide = out_ref.shape
    size, cols = out_ref.shape[1] // BLOCKS, wide // 2
    for p in range(part):
        for place in range(BLOCKS):
            start = order[p, place] * (2 * size)
            for half in range(2):
                rows = pl.ds(pl.multiple_of(start + half * size, 8), size)
                out_ref[p, pl.ds(place * size, size), pl.ds(half * cols, cols)] = total[
                    rows, pl.ds(p * cols, cols)
                ].astype(BF16)


def pack_up(order, total, out_ref):
    part, _, cols = out_ref.shape
    size = out_ref.shape[1] // BLOCKS
    for p in range(part):
        for place in range(BLOCKS):
            rows = pl.ds(pl.multiple_of(order[p, place] * size, 8), size)
            out_ref[p, pl.ds(place * size, size), :] = total[
                rows, pl.ds(p * cols, cols)
            ].astype(BF16)


def forward_kernel(
    x_ref, ctx_a, ctx_b, wo_a, wo_b, b_out, gain_one, shift_one,
    wu_a, wu_b, bu_a, bu_b, wd_a, wd_b, b_down, gain_two, shift_two, cot_ref, order,
    mixed_ref, after_ref, normed_ref, inverse_ref, slope_a, slope_b, grad_ref, low_ref, sums_ref,
    down_a, down_b,
    act, total,
):
    half = wu_a.shape[1]
    chunk = 512
    hidden = (
        x_ref[...].astype(F32)
        + nn(ctx_a[...], wo_a[...])
        + nn(ctx_b[...], wo_b[...])
        + b_out[...]
    )
    normed, inverse = normalize_parts(hidden)
    normed_ref[...] = normed
    inverse_ref[...] = inverse
    after = normed * gain_one[...] + shift_one[...]
    after_low = after.astype(BF16)
    after_ref[...] = after_low
    second = after + b_down[...]
    for side, (wu, bu, wd, slope) in enumerate(
        ((wu_a, bu_a, wd_a, slope_a), (wu_b, bu_b, wd_b, slope_b))
    ):
        for start in range(0, half, chunk):
            here = pl.ds(start, chunk)
            upper = nn(after_low, wu[:, here]) + bu[:, here]
            active, steep = gelu_parts(upper)
            active = active.astype(BF16)
            slope[:, here] = steep.astype(BF16)
            act[:, pl.ds(side * half + start, chunk)] = active
            second = second + nn(active, wd[here, :])
    normed_two, inverse_two = normalize_parts(second)
    mixed_ref[...] = (normed_two * gain_two[...] + shift_two[...]).astype(BF16)
    outer = cot_ref[...].astype(F32)
    grad = normalize_back(outer, normed_two, inverse_two, gain_two[...])
    grad_ref[...] = grad
    low = grad.astype(BF16)
    low_ref[...] = low
    sums_ref[...] = jnp.zeros_like(sums_ref)
    sums_ref[0:1, :] = jnp.sum(outer * normed_two, axis=0, keepdims=True)
    sums_ref[1:2, :] = jnp.sum(outer, axis=0, keepdims=True)
    sums_ref[2:3, :] = jnp.sum(grad, axis=0, keepdims=True)
    for side, out_ref in ((1, down_b), (0, down_a)):
        for start in range(0, half, chunk):
            total[pl.ds(start, chunk), :] = tn(act[:, pl.ds(side * half + start, chunk)], low)
        pack_down(order, total, out_ref)


def upper_kernel(
    low_ref, wd_a, wd_b, slope_a, slope_b, after_ref, order,
    gu_a, gu_b, sum_a, sum_b, up_a, up_b,
    total,
):
    half = wd_a.shape[0]
    chunk = 512
    low, after = low_ref[...], after_ref[...]
    for wd, slope, gu, sums, out_ref in (
        (wd_b, slope_b, gu_b, sum_b, up_b),
        (wd_a, slope_a, gu_a, sum_a, up_a),
    ):
        for start in range(0, half, chunk):
            here = pl.ds(start, chunk)
            grad = (nt(low, wd[here, :]) * slope[:, here].astype(F32)).astype(BF16)
            gu[:, here] = grad
            sums[:, here] = jnp.sum(grad.astype(F32), axis=0, keepdims=True)
            total[:, here] = tn(after, grad)
        pack_up(order, total, out_ref)


def first_norm_kernel(
    gu_a, gu_b, wu_a, wu_b, grad_ref, normed_ref, inverse_ref, gain_one, wo_a, wo_b, ctx_a, ctx_b,
    grad_one_ref, sums_ref, gctx_a, gctx_b, out_a, out_b,
):
    width = ctx_a.shape[1]
    after = grad_ref[...] + nt(gu_a[...], wu_a[...]) + nt(gu_b[...], wu_b[...])
    normed = normed_ref[...]
    grad = normalize_back(after, normed, inverse_ref[...], gain_one[...])
    grad_one_ref[...] = grad
    low = grad.astype(BF16)
    gctx_b[...] = nt(low, wo_b[...]).astype(BF16)
    gctx_a[...] = nt(low, wo_a[...]).astype(BF16)
    sums_ref[...] = jnp.zeros_like(sums_ref)
    sums_ref[0:1, :] = jnp.sum(after * normed, axis=0, keepdims=True)
    sums_ref[1:2, :] = jnp.sum(after, axis=0, keepdims=True)
    sums_ref[2:3, :] = jnp.sum(grad, axis=0, keepdims=True)
    for ctx, out_ref in ((ctx_b, out_b), (ctx_a, out_a)):
        both = tn(ctx[...], low).astype(BF16)
        out_ref[pl.ds(0, width), :] = both[:, :width]
        out_ref[pl.ds(width, width), :] = both[:, width:]


def project_kernel(
    x_ref, dq_ref, dk_ref, dv_ref, out_a, out_b, order, packed, sum_q, sum_v, total, both
):
    width = dq_ref.shape[1]
    size = packed.shape[1] // BLOCKS
    cols = width // 3
    x = x_ref[...]
    sum_q[...] = jnp.sum(dq_ref[...].astype(F32), axis=0, keepdims=True)
    sum_v[...] = jnp.sum(dv_ref[...].astype(F32), axis=0, keepdims=True)
    both[...] = out_a[...].astype(F32) + out_b[...].astype(F32)
    for p, grad in enumerate((dq_ref, dk_ref, dv_ref)):
        total[...] = tn(x, grad[...])
        for place in range(BLOCKS):
            rows = pl.ds(pl.multiple_of(order[p, place] * size, 8), size)
            to = pl.ds(place * size, size)
            packed[p, to, pl.ds(0, width)] = total[rows, :].astype(BF16)
            packed[p, to, pl.ds(width, cols)] = both[rows, pl.ds(p * cols, cols)].astype(BF16)


def unpack_down_kernel(a_ref, b_ref, c_ref, order, out_ref):
    size, cols = a_ref.shape[0] // BLOCKS, a_ref.shape[1] // 2
    for p, ref in enumerate((a_ref, b_ref, c_ref)):
        for place in range(BLOCKS):
            start = order[p, place] * (2 * size)
            for half in range(2):
                rows = pl.ds(pl.multiple_of(start + half * size, 8), size)
                out_ref[rows, pl.ds(p * cols, cols)] = ref[
                    pl.ds(place * size, size), pl.ds(half * cols, cols)
                ].astype(F32)


def unpack_up_kernel(a_ref, b_ref, c_ref, order, out_ref):
    size, cols = a_ref.shape[0] // BLOCKS, a_ref.shape[1]
    for p, ref in enumerate((a_ref, b_ref, c_ref)):
        for place in range(BLOCKS):
            rows = pl.ds(pl.multiple_of(order[p, place] * size, 8), size)
            out_ref[rows, pl.ds(p * cols, cols)] = ref[pl.ds(place * size, size), :].astype(F32)


def unpack_project_kernel(a_ref, b_ref, c_ref, order, q_ref, k_ref, v_ref, out_ref):
    width = q_ref.shape[1]
    size, cols = a_ref.shape[0] // BLOCKS, width // 3
    for p, (ref, grad) in enumerate(((a_ref, q_ref), (b_ref, k_ref), (c_ref, v_ref))):
        for place in range(BLOCKS):
            which = order[p, place]
            rows = pl.ds(pl.multiple_of(which * size, 8), size)
            grad[rows, :] = ref[pl.ds(place * size, size), pl.ds(0, width)].astype(F32)
            left = ref[pl.ds(place * size, size), pl.ds(width, cols)].astype(F32)
            rows = pl.ds(pl.multiple_of(lax.rem(which, BLOCKS // 2) * size, 8), size)
            at = pl.multiple_of(lax.div(which, BLOCKS // 2) * width + p * cols, 128)
            out_ref[rows, pl.ds(at, cols)] = left


def swap(value, bit, count):
    return lax.ppermute(value, "dp", [(i, i ^ bit) for i in range(count)])


def across(value):
    return lax.ppermute(value, "tensor", [(0, 1), (1, 0)])


def add(left, right):
    return (left.astype(F32) + right.astype(F32)).astype(BF16)


STAGES = ((1, 2, 4, 8), (2, 4, 1, 8), (4, 1, 2, 8))


def block_order():
    mine = lax.rem(lax.axis_index("dp"), BLOCKS // 2)
    rows = []
    for bits in STAGES:
        rows.append(
            [
                sum(bit for i, bit in enumerate(bits) if place >> (len(bits) - 1 - i) & 1)
                for place in range(BLOCKS)
            ]
        )
    return jnp.bitwise_xor(jnp.array(rows, jnp.int32), mine.astype(jnp.int32))


def sum_over_dp(own, other, count):
    results = []
    for p, bits in enumerate(STAGES):
        half = own[p].shape[0] // 2
        keep = add(own[p][:half], other[p][:half]) if other is not None else own[p][:half]
        send = add(own[p][half:], other[p][half:]) if other is not None else own[p][half:]
        for step in range(3):
            got = swap(send, bits[step], count)
            both = add(keep, got)
            half //= 2
            if step < 2:
                keep, send = both[:half], both[half:]
        extra = BLOCKS // 2
        while extra < count:
            both = add(both, swap(both, extra, count))
            extra *= 2
        for step in (2, 1, 0):
            both = jnp.concatenate([both, swap(both, bits[step], count)], axis=0)
        results.append(both)
    return results


def shards(
    tokens, segment_ids, w_query, w_key, w_value, b_query, b_value, w_out, b_out, gain_attn,
    shift_attn, w_up, b_up, w_down, b_down, gain_ffn, shift_ffn, cotangent,
):
    count = lax.axis_size("dp")
    here, model = tokens.shape
    width, half = w_query.shape[1], w_up.shape[1]
    row = lambda vector: vector.reshape(1, -1)

    tokens_b = across(tokens)
    segments_b = across(segment_ids)
    wo_b, wu_b, bu_b, wd_b = across(w_out), across(w_up), across(b_up), across(w_down)
    order = block_order()

    inputs = jnp.concatenate([tokens, tokens_b], axis=0)
    segments = jnp.concatenate([segment_ids, segments_b], axis=0)
    rows = inputs.shape[0] // LEN
    seg_rows, seg_cols = segments.reshape(rows, 1, LEN), segments.reshape(rows * LEN, 1)
    query, key, value, context, lse = attention_forward(
        inputs, w_query, w_key, w_value, row(b_query), row(b_value), seg_rows, seg_cols
    )
    ctx_a, ctx_b = context[:here], across(context[here:])

    parts = shape(3, model, half // 3, dtype=BF16)
    (
        mixed, after_low, normed_one, inverse_one, slope_a, slope_b, grad_two, grad_two_low, sums_two,
        down_a, down_b,
    ) = call(
        forward_kernel,
        [
            shape(here, model, dtype=BF16),
            shape(here, model, dtype=BF16),
            shape(here, model),
            shape(here, 1),
            shape(here, half, dtype=BF16),
            shape(here, half, dtype=BF16),
            shape(here, model),
            shape(here, model, dtype=BF16),
            shape(8, model),
            parts,
            parts,
        ],
        [
            tokens, ctx_a, ctx_b, w_out, wo_b, row(b_out), row(gain_attn), row(shift_attn),
            w_up, wu_b, row(b_up), row(bu_b), w_down, wd_b, row(b_down), row(gain_ffn),
            row(shift_ffn), cotangent, order,
        ],
        [pltpu.VMEM((here, 2 * half), BF16), pltpu.VMEM((half, model), F32)],
        limit=56,
        smem=(18,),
        flops=2 * here * model * (2 * width + 6 * half),
    )
    down_got = across(down_b)

    gu_a, gu_b, sum_up_a, sum_up_b, up_a, up_b = call(
        upper_kernel,
        [
            shape(here, half, dtype=BF16),
            shape(here, half, dtype=BF16),
            shape(1, half),
            shape(1, half),
            parts,
            parts,
        ],
        [grad_two_low, w_down, wd_b, slope_a, slope_b, after_low, order],
        [pltpu.VMEM((model, half), F32)],
        smem=(6,),
        flops=2 * here * model * 4 * half,
    )
    up_got = across(up_b)

    grad_one, sums_one, gctx_a, gctx_b, out_a, out_b = call(
        first_norm_kernel,
        [
            shape(here, model),
            shape(8, model),
            shape(here, width, dtype=BF16),
            shape(here, width, dtype=BF16),
            shape(model, width, dtype=BF16),
            shape(model, width, dtype=BF16),
        ],
        [
            gu_a, gu_b, w_up, wu_b, grad_two, normed_one, inverse_one, row(gain_attn),
            w_out, wo_b, ctx_a, ctx_b,
        ],
        flops=2 * here * model * (2 * half + 4 * width),
    )
    grad_context = jnp.concatenate([gctx_a, across(gctx_b)], axis=0)
    out_got = across(out_b)

    dq, dk, dv = attention_backward(
        query, key, value, context, grad_context, lse, seg_rows, seg_cols
    )
    packed, sum_q, sum_v = call(
        project_kernel,
        [parts, shape(1, width), shape(1, width)],
        [inputs, dq, dk, dv, out_a, out_got, order],
        [pltpu.VMEM((model, width), F32), pltpu.VMEM((model, width), F32)],
        smem=(6,),
        flops=2 * 2 * here * model * 3 * width,
    )

    def to_tokens(part):
        return nt(dq[part], w_query) + nt(dk[part], w_key) + nt(dv[part], w_value)

    token_got = across(to_tokens(slice(here, None)).astype(BF16))
    grad_tokens = to_tokens(slice(0, here)) + token_got.astype(F32) + grad_one

    downs = sum_over_dp(down_a, down_got, count)
    ups = sum_over_dp(up_a, up_got, count)
    projects = sum_over_dp(packed, None, count)
    (grad_w_down,) = call(
        unpack_down_kernel, [shape(half, model)], [*downs, order], limit=32, smem=(3,)
    )
    (grad_w_up,) = call(
        unpack_up_kernel, [shape(model, half)], [*ups, order], limit=32, smem=(3,)
    )
    grad_w_query, grad_w_key, grad_w_value, grad_w_out = call(
        unpack_project_kernel,
        [shape(model, width)] * 3 + [shape(width, model)],
        [*projects, order],
        limit=32,
        smem=(3,),
    )

    sums_up = sum_up_a + across(sum_up_b)
    shared = jnp.concatenate([sums_one[:3], sums_two[:3]], axis=0)
    shared = (shared + across(shared)).reshape(-1)
    small = jnp.concatenate([shared, sum_q[0], sum_v[0], sums_up[0]]).reshape(-1, 128)
    bit = 1
    while bit < count:
        small = small + swap(small, bit, count)
        bit *= 2
    small = small.reshape(-1)
    cuts = [model * i for i in range(1, 7)] + [6 * model + width, 6 * model + 2 * width]
    (
        grad_gain_attn, grad_shift_attn, grad_b_out, grad_gain_ffn, grad_shift_ffn, grad_b_down,
        grad_b_query, grad_b_value, grad_b_up,
    ) = jnp.split(small, cuts)
    return (
        mixed, grad_tokens, grad_w_query, grad_w_key, grad_w_value, grad_b_query, grad_b_value,
        grad_w_out, grad_b_out, grad_gain_attn, grad_shift_attn, grad_w_up, grad_b_up, grad_w_down,
        grad_b_down, grad_gain_ffn, grad_shift_ffn,
    )


def solution(mesh):
    placed = (
        P(("dp", "tensor"), None),
        P(("dp", "tensor")),
        P(None, "tensor"),
        P(None, "tensor"),
        P(None, "tensor"),
        P("tensor"),
        P("tensor"),
        P("tensor", None),
        P(),
        P(),
        P(),
        P(None, "tensor"),
        P("tensor"),
        P("tensor", None),
        P(),
        P(),
        P(),
        P(("dp", "tensor"), None),
    )
    return jax.shard_map(
        shards,
        mesh=mesh,
        in_specs=placed,
        out_specs=(
            P(("dp", "tensor"), None),
            P(("dp", "tensor"), None),
            P(None, "tensor"),
            P(None, "tensor"),
            P(None, "tensor"),
            P("tensor"),
            P("tensor"),
            P("tensor", None),
            P(),
            P(),
            P(),
            P(None, "tensor"),
            P("tensor"),
            P("tensor", None),
            P(),
            P(),
            P(),
        ),
        check_vma=False,
    )
```

time: 717 us -> 307 us (0.43)
  waiting for transfers between devices: 357 us -> 67 us
  blocking collectives: 127 us -> 0 us
  matrix products: 124 us -> 5.43 us
  Pallas kernels: 0 us -> 103 us
  starting transfers between devices: 0.99 us -> 85.8 us
  other arithmetic: 41.5 us -> 12.7 us
  local copies, waits for them, and re-layouts: 42.5 us -> 25.7 us
  between operations: 14.7 us -> 1.99 us
    psum x1 -> x0, waiting for transfers between devices: 275 us -> none  [shards(): lax.psum((grad_w_query, grad_w_key, grad_w_value, grad_b_query, grad_b_va...]
    psum x2 -> x0, blocking collectives: 124 us -> none  [the longest x1 79.8 us: shards(): lax.psum((grad_w_query, grad_w_key, grad_w_value, grad_b_query, grad_b_va...]
    dot_general x32 -> x6, matrix products: 124 us -> 5.43 us  [nt(): lax.dot_general(left, right, (((1,), (1,)), ((), ())), preferred_element_...]
    pallas_call x0 -> x9, Pallas kernels: none -> 103 us  [the longest x7 62.9 us: call(): pl.pallas_call(kernel, out_shape=outs, in_specs=[pl.BlockSpec(memory_spac...]
    ppermute x0 -> x81, starting transfers between devices: none -> 85.8 us  [the longest x67 82.1 us: swap(): return lax.ppermute(value, 'dp', [(i, i ^ bit) for i in range(count)])]
    ppermute x0 -> x81, waiting for transfers between devices: none -> 67 us  [the longest x67 62.7 us: swap(): return lax.ppermute(value, 'dp', [(i, i ^ bit) for i in range(count)])]
    all_gather x4 -> x0, waiting for transfers between devices: 44.7 us -> none  [the longest x1 12.1 us: shards(): lax.all_gather(tokens, 'tensor', axis=0, tiled=True)]
    reduce_scatter x4 -> x0, waiting for transfers between devices: 36.5 us -> none  [the longest x1 12.2 us: shards(): lax.psum_scatter(jnp.einsum('tf,df->td', grad_upper, w_up, preferred_elem...]
  transfers between devices with their start and end apart: 9 -> 81, of which waited for: 8 -> 33; matrix products, arithmetic and copies ran while one was open for 3% -> 10% of each run, Pallas kernels for 0% -> 25%
where the time goes in v1:
time: 307 us; the launch traced here: 301 us
  Pallas kernels  103 us (34%)
  starting transfers between devices  85.8 us (28%)
  waiting for transfers between devices  67 us (22%)
  local copies, waits for them, and re-layouts  25.7 us (8%)
  other arithmetic  12.7 us (4%)
  matrix products  5.43 us (2%)
    ppermute x67, starting transfers between devices, swap(): return lax.ppermute(value, 'dp', [(i, i ^ bit) for i in range(count)])  82.1 us
    pallas_call x7, Pallas kernels, call(): pl.pallas_call(kernel, out_shape=outs, in_specs=[pl.BlockSpec(memory_spac...  62.9 us
    ppermute x67, waiting for transfers between devices, swap(): return lax.ppermute(value, 'dp', [(i, i ^ bit) for i in range(count)])  62.7 us
    pallas_call x1, Pallas kernels, attention_forward(): pl.pallas_call(attend_kernel, grid=(rows,), out_shape=[shape(rows * LEN,...  21.5 us
    pallas_call x1, Pallas kernels, attention_backward(): pl.pallas_call(attend_back_kernel, grid=(rows,), out_shape=[shape(rows *...  18.2 us
    unnamed x100, local copies, waits for them, and re-layouts  16 us
    convert_element_type x32, other arithmetic, add(): return (left.astype(F32) + right.astype(F32)).astype(BF16)  8.26 us
  transfers between devices with their start and end apart: 81, of which 33 were waited for; matrix products, arithmetic and copies ran while one was open for 10% of the time, Pallas kernels for 25%

profile of v1, /device:TPU:0, one launch (start us, length us, event | category | flops | bytes accessed | tf_op | source)
XLA Modules:
  0.0 301.2 jit_solution(220327782620522219)
XLA Ops:
  2.2 2.2 constant_dynamic-update-slice_fusion.1
  4.5 3.4 %collective-permute-done.1 = s32[512]{0:T(512)S(1)} collective-permute-done((s32[512]{0:T(512)}, s32[512]{0:T(512)S(1)}, u32[]{:S(2)}, u32[]{:S(2)}) %collective-permute-start.1) | collective-permute-done | bytes 2080 | tf_op jit(solution)/shard_map/ppermute | solution.py:423
  10.5 21.5 %shard_map.314 = (bf16[1024,384]{1,0:T(8,128)(2,1)S(1)}, bf16[1024,384]{1,0:T(8,128)(2,1)S(1)}, bf16[1024,384]{1,0:T(8,128)(2,1)S(1)}, bf16[1024,384]{1,0:T(8,128)(2,1)S(1)}, f32[1,8,1024]{2,1,0:T(8,128)S(1)}) custom-call(bf16[1024,768]{1,0:T(8,128)(2,1)S(1)} %copy-done.12, bf16[768,384]{1,0:T(8,128)(2,1)S(1)} %copy-done.1, bf16[768,384]{1,0:T(8,128)(2,1)S(1)} %copy-done.2, ...), custom_call_target="tpu_custom_call" | custom-call | flops 8254390272 | bytes 8388608 | tf_op jit(solution)/shard_map/pallas_call | solution.py:143
  41.5 25.5 %shard_map.315 = (bf16[512,768]{1,0:T(8,128)(2,1)}, bf16[512,768]{1,0:T(8,128)(2,1)}, f32[512,768]{1,0:T(8,128)}, f32[512,1]{1,0:T(8,128)}, bf16[512,1536]{1,0:T...) custom-call(bf16[512,768]{1,0:T(8,128)(2,1)} %x_ref.1, ...), custom_call_target="tpu_custom_call" | custom-call | flops 7851737088 | bytes 26403008 | tf_op jit(solution)/shard_map/pallas_call | solution.py:78
  70.4 11.6 %shard_map.316 = (bf16[512,1536]{1,0:T(8,128)(2,1)S(1)}, bf16[512,1536]{1,0:T(8,128)(2,1)S(1)}, f32[1,1536]{1,0:T(1,128)S(1)}, f32[1,1536]{1,0:T(1,128)S(1)}, bf...) custom-call(bf16[512,768]{1,0:T(8,128)(2,1)S(1)} %copy-done.27, bf16[1536,768]{1,0:T(8,128)(2,1)} %wd_a.3, ...), custom_call_target="tpu_custom_call" | custom-call | flops 4831838208 | bytes 17313984 | tf_op jit(solution)/shard_map/pallas_call | solution.py:78
  84.4 11.0 %shard_map.317 = (f32[512,768]{1,0:T(8,128)S(1)}, f32[8,768]{1,0:T(8,128)S(1)}, bf16[512,384]{1,0:T(8,128)(2,1)S(1)}, bf16[512,384]{1,0:T(8,128)(2,1)}, bf16[768...) custom-call(bf16[512,1536]{1,0:T(8,128)(2,1)} %copy-done.21, bf16[512,1536]{1,0:T(8,128)(2,1)} %copy-done.22, ...), custom_call_target="tpu_custom_call" | custom-call | flops 3623878656 | bytes 16544768 | tf_op jit(solution)/shard_map/pallas_call | solution.py:78
  103.9 18.2 %shard_map.318 = (bf16[1024,384]{1,0:T(8,128)(2,1)S(1)}, bf16[1024,384]{1,0:T(8,128)(2,1)S(1)}, bf16[1024,384]{1,0:T(8,128)(2,1)S(1)}) custom-call(bf16[1024,384]{1,0:T(8,128)(2,1)S(1)} %copy-done.29, bf16[1024,384]{1,0:T(8,128)(2,1)S(1)} %copy-done.31, bf16[1024,384]{1,0:T(8,128)(2,1)S(1)} %copy-done.33, bf16[1024,384]{1,0:T(8,128)(2,1)S(1)} %copy-done.9, ...), custom_call_target="tpu_custom_call" | custom-call | flops 16106127360 | bytes 8388608 | tf_op jit(solution)/shard_map/pallas_call | solution.py:224
  124.9 5.5 %shard_map.319 = (bf16[3,768,512]{2,1,0:T(8,128)(2,1)}, f32[1,384]{1,0:T(1,128)S(1)}, f32[1,384]{1,0:T(1,128)S(1)}) custom-call(bf16[1024,768]{1,0:T(8,128)(2,1)S(1)} %copy-done.13, bf16[1024,384]{1,0:T(8,128)(2,1)S(1)} %get-tuple-element.72.dq_ref, bf16[1024,384]{1,0:T(8,128)(2,1)S(1)} %get-tuple-element.73.dk_ref, ...), custom_call_target="tpu_custom_call" | custom-call | flops 1811939328 | bytes 7474368 | tf_op jit(solution)/shard_map/pallas_call | solution.py:78
  130.5 2.9 collective-permute-start.33
  133.5 1.6 fusion.30
  135.3 2.1 collective-permute-start.34
  139.3 2.1 collective-permute-start.35
  143.3 3.3 %collective-permute-start.36 = (f32[54,128]{1,0:T(8,128)S(1)}, f32[54,128]{1,0:T(8,128)S(1)}, u32[]{:S(2)}, u32[]{:S(2)}) collective-permute-start(f32[54,128]{1,0:T(8,128)S(1)} %add.214), channel_id=1, source_target_pairs={{0,16},{2,18},{4,20},{6,22},{8,24},{10,26},{12,28},{14,30},{16,0},... | collective-permute-start | bytes 82952 | tf_op jit(solution)/shard_map/ppermute | solution.py:419
  146.7 1.6 collective-permute-start.24
  148.4 1.5 collective-permute-start.17
  152.6 2.0 collective-permute-done.24
  154.6 1.6 collective-permute-done.17
  156.1 1.5 collective-permute-done.10
  159.2 1.6 collective-permute-start.18
  160.9 2.9 collective-permute-done.11
  166.7 3.8 %collective-permute-done.25 = bf16[192,512]{1,0:T(8,128)(2,1)S(1)} collective-permute-done((bf16[192,512]{1,0:T(8,128)(2,1)S(1)}, bf16[192,512]{1,0:T(8,128)(2,1)S(1)}, u32[]{:S(2)}, u32[]{:S(2)}) %collective-permute-start.25) | collective-permute-done | bytes 196640 | tf_op jit(solution)/shard_map/ppermute | solution.py:419
  172.6 2.5 collective-permute-done.19
  178.2 5.7 %collective-permute-done.13 = bf16[96,512]{1,0:T(8,128)(2,1)S(1)} collective-permute-done((bf16[96,512]{1,0:T(8,128)(2,1)S(1)}, bf16[96,512]{1,0:T(8,128)(2,1)S(1)}, u32[]{:S(2)}, u32[]{:S(2)}) %collective-permute-start.13) | collective-permute-done | bytes 98336 | tf_op jit(solution)/shard_map/ppermute | solution.py:419
  185.1 4.4 %collective-permute-done.27 = bf16[96,512]{1,0:T(8,128)(2,1)S(1)} collective-permute-done((bf16[96,512]{1,0:T(8,128)(2,1)S(1)}, bf16[96,512]{1,0:T(8,128)(2,1)S(1)}, u32[]{:S(2)}, u32[]{:S(2)}) %collective-permute-start.27) | collective-permute-done | bytes 98336 | tf_op jit(solution)/shard_map/ppermute | solution.py:419
  192.2 1.8 collective-permute-done.21
  195.7 6.0 %collective-permute-done.15 = bf16[192,512]{1,0:T(8,128)(2,1)S(1)} collective-permute-done((bf16[192,512]{1,0:T(8,128)(2,1)S(1)}, bf16[192,512]{1,0:T(8,128)(2,1)S(1)}, u32[]{:S(2)}, u32[]{:S(2)}) %collective-permute-start.15) | collective-permute-done | bytes 196640 | tf_op jit(solution)/shard_map/ppermute | solution.py:419
  203.8 1.6 add_add_fusion
  207.4 8.2 %collective-permute-done.16 = bf16[384,512]{1,0:T(8,128)(2,1)S(1)} collective-permute-done((bf16[384,512]{1,0:T(8,128)(2,1)S(1)}, bf16[384,512]{1,0:T(8,128)(2,1)S(1)}, u32[]{:S(2)}, u32[]{:S(2)}) %collective-permute-start.16) | collective-permute-done | bytes 393248 | tf_op jit(solution)/shard_map/ppermute | solution.py:419
  215.8 1.7 fusion.20
  220.4 1.6 fusion.14
  222.0 2.1 collective-permute-start.52
  224.9 4.5 %collective-permute-done.74 = bf16[384,512]{1,0:T(8,128)(2,1)S(1)} collective-permute-done((bf16[384,512]{1,0:T(8,128)(2,1)S(1)}, bf16[384,512]{1,0:T(8,128)(2,1)S(1)}, u32[]{:S(2)}, u32[]{:S(2)}) %collective-permute-start.74) | collective-permute-done | bytes 393248 | tf_op jit(solution)/shard_map/ppermute | solution.py:419
  230.9 3.2 %shard_map.320 = (f32[768,384]{1,0:T(8,128)}, f32[768,384]{1,0:T(8,128)}, f32[768,384]{1,0:T(8,128)}, f32[384,768]{1,0:T(8,128)}) custom-call(bf16[768,512]{1,0:T(8,128)(2,1)S(1)} %pad_maximum_fusion.1.a_ref, bf16[768,512]{1,0:T(8,128)(2,1)S(1)} %pad_maximum_fusion.2.b_ref, bf16[768,512]{1,0:T(8,128)(2,1)S(1)} %pad_maximum_fusion.3.c_ref, s32[3,16]{1,0:T(4,128)S(1)} %copy-done.16), custom_call_target="tpu_custom_call" | custom-call | bytes 7078080 | tf_op jit(solution)/shard_map/pallas_call | solution.py:78
  234.1 1.7 fusion
  238.2 1.9 fusion.3
  247.1 4.7 %collective-permute-done.46 = bf16[192,512]{1,0:T(8,128)(2,1)S(1)} collective-permute-done((bf16[192,512]{1,0:T(8,128)(2,1)S(1)}, bf16[192,512]{1,0:T(8,128)(2,1)S(1)}, u32[]{:S(2)}, u32[]{:S(2)}) %collective-permute-start.46) | collective-permute-done | bytes 196640 | tf_op jit(solution)/shard_map/ppermute | solution.py:419
  252.0 1.7 collective-permute-start.47
  254.7 1.8 collective-permute-start.63
  257.9 1.8 collective-permute-start.77
  261.0 1.8 collective-permute-start.48
  264.2 3.0 collective-permute-start.64
  267.4 1.8 collective-permute-start.78
  269.5 2.0 collective-permute-start.42
  276.0 2.0 collective-permute-start.79
  287.2 2.8 collective-permute-done.66
  291.6 3.1 %shard_map.322 = f32[1536,768]{1,0:T(8,128)} custom-call(bf16[768,512]{1,0:T(8,128)(2,1)S(1)} %pad_maximum_fusion.7.a_ref, bf16[768,512]{1,0:T(8,128)(2,1)S(1)} %pad_maximum_fusion.8.b_ref, bf16[768,512]{1,0:T(8,128)(2,1)S(1)} %pad_maximum_fusion.9.c_ref, s32[3,16]{1,0:T(4,128)S(1)} %copy-done.16), custom_call_target="tpu_custom_call" | custom-call | bytes 7078080 | tf_op jit(solution)/shard_map/pallas_call | solution.py:78
  294.8 3.0 collective-permute-done.58
  297.9 3.1 %shard_map.321 = f32[768,1536]{1,0:T(8,128)} custom-call(bf16[768,512]{1,0:T(8,128)(2,1)S(1)} %pad_maximum_fusion.4.a_ref, bf16[768,512]{1,0:T(8,128)(2,1)S(1)} %pad_maximum_fusion.5.b_ref, bf16[768,512]{1,0:T(8,128)(2,1)S(1)} %pad_maximum_fusion.6.c_ref, s32[3,16]{1,0:T(4,128)S(1)} %copy-done.16), custom_call_target="tpu_custom_call" | custom-call | bytes 7078080 | tf_op jit(solution)/shard_map/pallas_call | solution.py:78
  (341 shorter events, 92.2 us)
Async XLA Ops:
  0.7 40.1 %collective-permute-start.4 = (bf16[768,1536]{1,0:T(8,128)(2,1)}, bf16[768,1536]{1,0:T(8,128)(2,1)}, u32[]{:S(2)}, u32[]{:S(2)}) collective-permute-start(bf16[768,1536]{1,0:T(8,128)(2,1)} %wu_a.3), channel_id=1, source_target_pairs={{0,1},{1,0},{2,3},{3,2},{4,5},{5,4},{6,7},{7,6},{8,9},{9,8},{10,11... | collective-permute-start | bytes 7077896 | tf_op jit(solution)/shard_map/ppermute | solution.py:423
  1.2 39.6 %collective-permute-start.6 = (bf16[1536,768]{1,0:T(8,128)(2,1)}, bf16[1536,768]{1,0:T(8,128)(2,1)}, u32[]{:S(2)}, u32[]{:S(2)}) collective-permute-start(bf16[1536,768]{1,0:T(8,128)(2,1)} %wd_a.3), channel_id=1, source_target_pairs={{0,1},{1,0},{2,3},{3,2},{4,5},{5,4},{6,7},{7,6},{8,9},{9,8},{10,11... | collective-permute-start | bytes 7077896 | tf_op jit(solution)/shard_map/ppermute | solution.py:423
  1.3 6.8 %collective-permute-start = (bf16[512,768]{1,0:T(8,128)(2,1)}, bf16[512,768]{1,0:T(8,128)(2,1)S(1)}, u32[]{:S(2)}, u32[]{:S(2)}) collective-permute-start(bf16[512,768]{1,0:T(8,128)(2,1)} %x_ref.1), channel_id=1, source_target_pairs={{0,1},{1,0},{2,3},{3,2},{4,5},{5,4},{6,7},{7,6},{8,9},{9,8},{10,11... | collective-permute-start | bytes 2359304 | tf_op jit(solution)/shard_map/ppermute | solution.py:423
  1.8 39.0 %collective-permute-start.3 = (bf16[384,768]{1,0:T(8,128)(2,1)}, bf16[384,768]{1,0:T(8,128)(2,1)}, u32[]{:S(2)}, u32[]{:S(2)}) collective-permute-start(bf16[384,768]{1,0:T(8,128)(2,1)} %wo_a.3), channel_id=1, source_target_pairs={{0,1},{1,0},{2,3},{3,2},{4,5},{5,4},{6,7},{7,6},{8,9},{9,8},{10,11... | collective-permute-start | bytes 1769480 | tf_op jit(solution)/shard_map/ppermute | solution.py:423
  67.7 148.0 %collective-permute-start.59 = (bf16[3,768,512]{2,1,0:T(8,128)(2,1)}, bf16[3,768,512]{2,1,0:T(8,128)(2,1)}, u32[]{:S(2)}, u32[]{:S(2)}) collective-permute-start(bf16[3,768,512]{2,1,0:T(8,128)(2,1)} %get-tuple-element.92), channel_id=1, source_target_pairs={{0,1},{1,0},{2,3},{3,2},{4,5},{5,4},{6,7},{7,6},{8,9},{9,8},{10,11... | collective-permute-start | bytes 7077896 | tf_op jit(solution)/shard_map/ppermute | solution.py:423
  97.7 27.1 %collective-permute-start.9 = (bf16[768,384]{1,0:T(8,128)(2,1)}, bf16[768,384]{1,0:T(8,128)(2,1)}, u32[]{:S(2)}, u32[]{:S(2)}) collective-permute-start(bf16[768,384]{1,0:T(8,128)(2,1)} %get-tuple-element.77), channel_id=1, source_target_pairs={{0,1},{1,0},{2,3},{3,2},{4,5},{5,4},{6,7},{7,6},{8,9},{9,8},{10,11... | collective-permute-start | bytes 1769480 | tf_op jit(solution)/shard_map/ppermute | solution.py:423
  98.2 122.2 %collective-permute-start.37 = (bf16[3,768,512]{2,1,0:T(8,128)(2,1)}, bf16[3,768,512]{2,1,0:T(8,128)(2,1)}, u32[]{:S(2)}, u32[]{:S(2)}) collective-permute-start(bf16[3,768,512]{2,1,0:T(8,128)(2,1)} %get-tuple-element.90), channel_id=1, source_target_pairs={{0,1},{1,0},{2,3},{3,2},{4,5},{5,4},{6,7},{7,6},{8,9},{9,8},{10,11... | collective-permute-start | bytes 7077896 | tf_op jit(solution)/shard_map/ppermute | solution.py:423
  146.7 7.8 %collective-permute-start.24 = (bf16[384,512]{1,0:T(8,128)(2,1)S(1)}, bf16[384,512]{1,0:T(8,128)(2,1)S(1)}, u32[]{:S(2)}, u32[]{:S(2)}) collective-permute-start(bf16[384,512]{1,0:T(8,128)(2,1)S(1)} %get-tuple-element.108), channel_id=1, source_target_pairs={{0,8},{2,10},{4,12},{6,14},{8,0},{10,2},{12,4},{14,6},{16,24},{18,... | collective-permute-start | bytes 1179656 | tf_op jit(solution)/shard_map/ppermute | solution.py:419
  148.4 7.8 %collective-permute-start.17 = (bf16[384,512]{1,0:T(8,128)(2,1)S(1)}, bf16[384,512]{1,0:T(8,128)(2,1)S(1)}, u32[]{:S(2)}, u32[]{:S(2)}) collective-permute-start(bf16[384,512]{1,0:T(8,128)(2,1)S(1)} %get-tuple-element.109), channel_id=1, source_target_pairs={{0,4},{2,6},{4,0},{6,2},{8,12},{10,14},{12,8},{14,10},{16,20},{18,... | collective-permute-start | bytes 1179656 | tf_op jit(solution)/shard_map/ppermute | solution.py:419
  149.9 7.8 %collective-permute-start.10 = (bf16[384,512]{1,0:T(8,128)(2,1)S(1)}, bf16[384,512]{1,0:T(8,128)(2,1)S(1)}, u32[]{:S(2)}, u32[]{:S(2)}) collective-permute-start(bf16[384,512]{1,0:T(8,128)(2,1)S(1)} %get-tuple-element.110), channel_id=1, source_target_pairs={{0,2},{2,0},{4,6},{6,4},{8,10},{10,8},{12,14},{14,12},{16,18},{18,... | collective-permute-start | bytes 1179656 | tf_op jit(solution)/shard_map/ppermute | solution.py:419
  154.6 48.6 %collective-permute-start.8 = (bf16[512,768]{1,0:T(8,128)(2,1)S(1)}, bf16[512,768]{1,0:T(8,128)(2,1)S(1)}, u32[]{:S(2)}, u32[]{:S(2)}) collective-permute-start(bf16[512,768]{1,0:T(8,128)(2,1)S(1)} %copy-done.37), channel_id=1, source_target_pairs={{0,1},{1,0},{2,3},{3,2},{4,5},{5,4},{6,7},{7,6},{8,9},{9,8},{10,11... | collective-permute-start | bytes 2359304 | tf_op jit(solution)/shard_map/ppermute | solution.py:423
  175.1 8.7 %collective-permute-start.13 = (bf16[96,512]{1,0:T(8,128)(2,1)S(1)}, bf16[96,512]{1,0:T(8,128)(2,1)S(1)}, u32[]{:S(2)}, u32[]{:S(2)}) collective-permute-start(bf16[96,512]{1,0:T(8,128)(2,1)S(1)} %add_convert_fusion.39), channel_id=1, source_target_pairs={{0,16},{2,18},{4,20},{6,22},{8,24},{10,26},{12,28},{14,30},{16,0},... | collective-permute-start | bytes 294920 | tf_op jit(solution)/shard_map/ppermute | solution.py:419
  176.8 8.1 %collective-permute-start.20 = (bf16[96,512]{1,0:T(8,128)(2,1)S(1)}, bf16[96,512]{1,0:T(8,128)(2,1)S(1)}, u32[]{:S(2)}, u32[]{:S(2)}) collective-permute-start(bf16[96,512]{1,0:T(8,128)(2,1)S(1)} %add_convert_fusion.37), channel_id=1, source_target_pairs={{0,16},{2,18},{4,20},{6,22},{8,24},{10,26},{12,28},{14,30},{16,0},... | collective-permute-start | bytes 294920 | tf_op jit(solution)/shard_map/ppermute | solution.py:419
  194.1 7.6 %collective-permute-start.15 = (bf16[192,512]{1,0:T(8,128)(2,1)S(1)}, bf16[192,512]{1,0:T(8,128)(2,1)S(1)}, u32[]{:S(2)}, u32[]{:S(2)}) collective-permute-start(bf16[192,512]{1,0:T(8,128)(2,1)S(1)} %pad_maximum_fusion.19), channel_id=1, source_target_pairs={{0,4},{2,6},{4,0},{6,2},{8,12},{10,14},{12,8},{14,10},{16,20},{18,... | collective-permute-start | bytes 589832 | tf_op jit(solution)/shard_map/ppermute | solution.py:419
  195.7 9.7 %collective-permute-start.22 = (bf16[192,512]{1,0:T(8,128)(2,1)S(1)}, bf16[192,512]{1,0:T(8,128)(2,1)S(1)}, u32[]{:S(2)}, u32[]{:S(2)}) collective-permute-start(bf16[192,512]{1,0:T(8,128)(2,1)S(1)} %pad_maximum_fusion.20), channel_id=1, source_target_pairs={{0,8},{2,10},{4,12},{6,14},{8,0},{10,2},{12,4},{14,6},{16,24},{18,... | collective-permute-start | bytes 589832 | tf_op jit(solution)/shard_map/ppermute | solution.py:419
  203.2 12.5 %collective-permute-start.16 = (bf16[384,512]{1,0:T(8,128)(2,1)S(1)}, bf16[384,512]{1,0:T(8,128)(2,1)S(1)}, u32[]{:S(2)}, u32[]{:S(2)}) collective-permute-start(bf16[384,512]{1,0:T(8,128)(2,1)S(1)} %pad_maximum_fusion.10), channel_id=1, source_target_pairs={{0,2},{2,0},{4,6},{6,4},{8,10},{10,8},{12,14},{14,12},{16,18},{18,... | collective-permute-start | bytes 1179656 | tf_op jit(solution)/shard_map/ppermute | solution.py:419
  205.4 12.1 %collective-permute-start.23 = (bf16[384,512]{1,0:T(8,128)(2,1)S(1)}, bf16[384,512]{1,0:T(8,128)(2,1)S(1)}, u32[]{:S(2)}, u32[]{:S(2)}) collective-permute-start(bf16[384,512]{1,0:T(8,128)(2,1)S(1)} %pad_maximum_fusion.11), channel_id=1, source_target_pairs={{0,4},{2,6},{4,0},{6,2},{8,12},{10,14},{12,8},{14,10},{16,20},{18,... | collective-permute-start | bytes 1179656 | tf_op jit(solution)/shard_map/ppermute | solution.py:419
  207.4 16.7 %collective-permute-start.30 = (bf16[384,512]{1,0:T(8,128)(2,1)S(1)}, bf16[384,512]{1,0:T(8,128)(2,1)S(1)}, u32[]{:S(2)}, u32[]{:S(2)}) collective-permute-start(bf16[384,512]{1,0:T(8,128)(2,1)S(1)} %pad_maximum_fusion.12), channel_id=1, source_target_pairs={{0,8},{2,10},{4,12},{6,14},{8,0},{10,2},{12,4},{14,6},{16,24},{18,... | collective-permute-start | bytes 1179656 | tf_op jit(solution)/shard_map/ppermute | solution.py:419
  217.5 11.9 %collective-permute-start.74 = (bf16[384,512]{1,0:T(8,128)(2,1)S(1)}, bf16[384,512]{1,0:T(8,128)(2,1)S(1)}, u32[]{:S(2)}, u32[]{:S(2)}) collective-permute-start(bf16[384,512]{1,0:T(8,128)(2,1)S(1)} %get-tuple-element.96), channel_id=1, source_target_pairs={{0,8},{2,10},{4,12},{6,14},{8,0},{10,2},{12,4},{14,6},{16,24},{18,... | collective-permute-start | bytes 1179656 | tf_op jit(solution)/shard_map/ppermute | solution.py:419
  217.6 16.5 %collective-permute-start.67 = (bf16[384,512]{1,0:T(8,128)(2,1)S(1)}, bf16[384,512]{1,0:T(8,128)(2,1)S(1)}, u32[]{:S(2)}, u32[]{:S(2)}) collective-permute-start(bf16[384,512]{1,0:T(8,128)(2,1)S(1)} %get-tuple-element.97), channel_id=1, source_target_pairs={{0,4},{2,6},{4,0},{6,2},{8,12},{10,14},{12,8},{14,10},{16,20},{18,... | collective-permute-start | bytes 1179656 | tf_op jit(solution)/shard_map/ppermute | solution.py:419
  218.9 15.2 %collective-permute-start.60 = (bf16[384,512]{1,0:T(8,128)(2,1)S(1)}, bf16[384,512]{1,0:T(8,128)(2,1)S(1)}, u32[]{:S(2)}, u32[]{:S(2)}) collective-permute-start(bf16[384,512]{1,0:T(8,128)(2,1)S(1)} %get-tuple-element.98), channel_id=1, source_target_pairs={{0,2},{2,0},{4,6},{6,4},{8,10},{10,8},{12,14},{14,12},{16,18},{18,... | collective-permute-start | bytes 1179656 | tf_op jit(solution)/shard_map/ppermute | solution.py:419
  222.0 15.1 %collective-permute-start.52 = (bf16[384,512]{1,0:T(8,128)(2,1)S(1)}, bf16[384,512]{1,0:T(8,128)(2,1)S(1)}, u32[]{:S(2)}, u32[]{:S(2)}) collective-permute-start(bf16[384,512]{1,0:T(8,128)(2,1)S(1)} %get-tuple-element.102), channel_id=1, source_target_pairs={{0,8},{2,10},{4,12},{6,14},{8,0},{10,2},{12,4},{14,6},{16,24},{18,... | collective-permute-start | bytes 1179656 | tf_op jit(solution)/shard_map/ppermute | solution.py:419
  224.0 13.6 %collective-permute-start.45 = (bf16[384,512]{1,0:T(8,128)(2,1)S(1)}, bf16[384,512]{1,0:T(8,128)(2,1)S(1)}, u32[]{:S(2)}, u32[]{:S(2)}) collective-permute-start(bf16[384,512]{1,0:T(8,128)(2,1)S(1)} %get-tuple-element.103), channel_id=1, source_target_pairs={{0,4},{2,6},{4,0},{6,2},{8,12},{10,14},{12,8},{14,10},{16,20},{18,... | collective-permute-start | bytes 1179656 | tf_op jit(solution)/shard_map/ppermute | solution.py:419
  229.3 8.8 %collective-permute-start.38 = (bf16[384,512]{1,0:T(8,128)(2,1)S(1)}, bf16[384,512]{1,0:T(8,128)(2,1)S(1)}, u32[]{:S(2)}, u32[]{:S(2)}) collective-permute-start(bf16[384,512]{1,0:T(8,128)(2,1)S(1)} %get-tuple-element.104), channel_id=1, source_target_pairs={{0,2},{2,0},{4,6},{6,4},{8,10},{10,8},{12,14},{14,12},{16,18},{18,... | collective-permute-start | bytes 1179656 | tf_op jit(solution)/shard_map/ppermute | solution.py:419
  237.1 7.2 %collective-permute-start.68 = (bf16[192,512]{1,0:T(8,128)(2,1)S(1)}, bf16[192,512]{1,0:T(8,128)(2,1)S(1)}, u32[]{:S(2)}, u32[]{:S(2)}) collective-permute-start(bf16[192,512]{1,0:T(8,128)(2,1)S(1)} %slice.451), channel_id=1, source_target_pairs={{0,8},{2,10},{4,12},{6,14},{8,0},{10,2},{12,4},{14,6},{16,24},{18,... | collective-permute-start | bytes 589832 | tf_op jit(solution)/shard_map/ppermute | solution.py:419
  237.1 7.9 %collective-permute-start.75 = (bf16[192,512]{1,0:T(8,128)(2,1)S(1)}, bf16[192,512]{1,0:T(8,128)(2,1)S(1)}, u32[]{:S(2)}, u32[]{:S(2)}) collective-permute-start(bf16[192,512]{1,0:T(8,128)(2,1)S(1)} %slice.457), channel_id=1, source_target_pairs={{0,2},{2,0},{4,6},{6,4},{8,10},{10,8},{12,14},{14,12},{16,18},{18,... | collective-permute-start | bytes 589832 | tf_op jit(solution)/shard_map/ppermute | solution.py:419
  241.4 10.5 %collective-permute-start.46 = (bf16[192,512]{1,0:T(8,128)(2,1)S(1)}, bf16[192,512]{1,0:T(8,128)(2,1)S(1)}, u32[]{:S(2)}, u32[]{:S(2)}) collective-permute-start(bf16[192,512]{1,0:T(8,128)(2,1)S(1)} %slice.433), channel_id=1, source_target_pairs={{0,8},{2,10},{4,12},{6,14},{8,0},{10,2},{12,4},{14,6},{16,24},{18,... | collective-permute-start | bytes 589832 | tf_op jit(solution)/shard_map/ppermute | solution.py:419
  242.6 9.4 %collective-permute-start.53 = (bf16[192,512]{1,0:T(8,128)(2,1)S(1)}, bf16[192,512]{1,0:T(8,128)(2,1)S(1)}, u32[]{:S(2)}, u32[]{:S(2)}) collective-permute-start(bf16[192,512]{1,0:T(8,128)(2,1)S(1)} %slice.439), channel_id=1, source_target_pairs={{0,2},{2,0},{4,6},{6,4},{8,10},{10,8},{12,14},{14,12},{16,18},{18,... | collective-permute-start | bytes 589832 | tf_op jit(solution)/shard_map/ppermute | solution.py:419
  244.3 9.5 %collective-permute-start.62 = (bf16[96,512]{1,0:T(8,128)(2,1)S(1)}, bf16[96,512]{1,0:T(8,128)(2,1)S(1)}, u32[]{:S(2)}, u32[]{:S(2)}) collective-permute-start(bf16[96,512]{1,0:T(8,128)(2,1)S(1)} %slice.447), channel_id=1, source_target_pairs={{0,8},{2,10},{4,12},{6,14},{8,0},{10,2},{12,4},{14,6},{16,24},{18,... | collective-permute-start | bytes 294920 | tf_op jit(solution)/shard_map/ppermute | solution.py:419
  245.0 9.8 %collective-permute-start.69 = (bf16[96,512]{1,0:T(8,128)(2,1)S(1)}, bf16[96,512]{1,0:T(8,128)(2,1)S(1)}, u32[]{:S(2)}, u32[]{:S(2)}) collective-permute-start(bf16[96,512]{1,0:T(8,128)(2,1)S(1)} %slice.453), channel_id=1, source_target_pairs={{0,2},{2,0},{4,6},{6,4},{8,10},{10,8},{12,14},{14,12},{16,18},{18,... | collective-permute-start | bytes 294920 | tf_op jit(solution)/shard_map/ppermute | solution.py:419
  245.9 10.7 %collective-permute-start.76 = (bf16[96,512]{1,0:T(8,128)(2,1)S(1)}, bf16[96,512]{1,0:T(8,128)(2,1)S(1)}, u32[]{:S(2)}, u32[]{:S(2)}) collective-permute-start(bf16[96,512]{1,0:T(8,128)(2,1)S(1)} %slice.459), channel_id=1, source_target_pairs={{0,4},{2,6},{4,0},{6,2},{8,12},{10,14},{12,8},{14,10},{16,20},{18,... | collective-permute-start | bytes 294920 | tf_op jit(solution)/shard_map/ppermute | solution.py:419
  252.0 7.7 %collective-permute-start.47 = (bf16[96,512]{1,0:T(8,128)(2,1)S(1)}, bf16[96,512]{1,0:T(8,128)(2,1)S(1)}, u32[]{:S(2)}, u32[]{:S(2)}) collective-permute-start(bf16[96,512]{1,0:T(8,128)(2,1)S(1)} %slice.435), channel_id=1, source_target_pairs={{0,2},{2,0},{4,6},{6,4},{8,10},{10,8},{12,14},{14,12},{16,18},{18,... | collective-permute-start | bytes 294920 | tf_op jit(solution)/shard_map/ppermute | solution.py:419
  253.8 7.2 %collective-permute-start.54 = (bf16[96,512]{1,0:T(8,128)(2,1)S(1)}, bf16[96,512]{1,0:T(8,128)(2,1)S(1)}, u32[]{:S(2)}, u32[]{:S(2)}) collective-permute-start(bf16[96,512]{1,0:T(8,128)(2,1)S(1)} %slice.441), channel_id=1, source_target_pairs={{0,4},{2,6},{4,0},{6,2},{8,12},{10,14},{12,8},{14,10},{16,20},{18,... | collective-permute-start | bytes 294920 | tf_op jit(solution)/shard_map/ppermute | solution.py:419
  254.7 8.1 %collective-permute-start.63 = (bf16[96,512]{1,0:T(8,128)(2,1)S(1)}, bf16[96,512]{1,0:T(8,128)(2,1)S(1)}, u32[]{:S(2)}, u32[]{:S(2)}) collective-permute-start(bf16[96,512]{1,0:T(8,128)(2,1)S(1)} %add_convert_fusion.27), channel_id=1, source_target_pairs={{0,16},{2,18},{4,20},{6,22},{8,24},{10,26},{12,28},{14,30},{16,0},... | collective-permute-start | bytes 294920 | tf_op jit(solution)/shard_map/ppermute | solution.py:419
  256.6 7.6 %collective-permute-start.70 = (bf16[96,512]{1,0:T(8,128)(2,1)S(1)}, bf16[96,512]{1,0:T(8,128)(2,1)S(1)}, u32[]{:S(2)}, u32[]{:S(2)}) collective-permute-start(bf16[96,512]{1,0:T(8,128)(2,1)S(1)} %add_convert_fusion.25), channel_id=1, source_target_pairs={{0,16},{2,18},{4,20},{6,22},{8,24},{10,26},{12,28},{14,30},{16,0},... | collective-permute-start | bytes 294920 | tf_op jit(solution)/shard_map/ppermute | solution.py:419
  257.9 9.3 %collective-permute-start.77 = (bf16[96,512]{1,0:T(8,128)(2,1)S(1)}, bf16[96,512]{1,0:T(8,128)(2,1)S(1)}, u32[]{:S(2)}, u32[]{:S(2)}) collective-permute-start(bf16[96,512]{1,0:T(8,128)(2,1)S(1)} %add_convert_fusion.23), channel_id=1, source_target_pairs={{0,16},{2,18},{4,20},{6,22},{8,24},{10,26},{12,28},{14,30},{16,0},... | collective-permute-start | bytes 294920 | tf_op jit(solution)/shard_map/ppermute | solution.py:419
  259.7 7.7 %collective-permute-start.41 = (bf16[96,512]{1,0:T(8,128)(2,1)S(1)}, bf16[96,512]{1,0:T(8,128)(2,1)S(1)}, u32[]{:S(2)}, u32[]{:S(2)}) collective-permute-start(bf16[96,512]{1,0:T(8,128)(2,1)S(1)} %add_convert_fusion.33), channel_id=1, source_target_pairs={{0,16},{2,18},{4,20},{6,22},{8,24},{10,26},{12,28},{14,30},{16,0},... | collective-permute-start | bytes 294920 | tf_op jit(solution)/shard_map/ppermute | solution.py:419
  261.0 8.5 %collective-permute-start.48 = (bf16[96,512]{1,0:T(8,128)(2,1)S(1)}, bf16[96,512]{1,0:T(8,128)(2,1)S(1)}, u32[]{:S(2)}, u32[]{:S(2)}) collective-permute-start(bf16[96,512]{1,0:T(8,128)(2,1)S(1)} %add_convert_fusion.31), channel_id=1, source_target_pairs={{0,16},{2,18},{4,20},{6,22},{8,24},{10,26},{12,28},{14,30},{16,0},... | collective-permute-start | bytes 294920 | tf_op jit(solution)/shard_map/ppermute | solution.py:419
  262.8 8.7 %collective-permute-start.55 = (bf16[96,512]{1,0:T(8,128)(2,1)S(1)}, bf16[96,512]{1,0:T(8,128)(2,1)S(1)}, u32[]{:S(2)}, u32[]{:S(2)}) collective-permute-start(bf16[96,512]{1,0:T(8,128)(2,1)S(1)} %add_convert_fusion.29), channel_id=1, source_target_pairs={{0,16},{2,18},{4,20},{6,22},{8,24},{10,26},{12,28},{14,30},{16,0},... | collective-permute-start | bytes 294920 | tf_op jit(solution)/shard_map/ppermute | solution.py:419
  264.2 9.0 %collective-permute-start.64 = (bf16[96,512]{1,0:T(8,128)(2,1)S(1)}, bf16[96,512]{1,0:T(8,128)(2,1)S(1)}, u32[]{:S(2)}, u32[]{:S(2)}) collective-permute-start(bf16[96,512]{1,0:T(8,128)(2,1)S(1)} %add_convert_fusion.26), channel_id=1, source_target_pairs={{0,8},{2,10},{4,12},{6,14},{8,0},{10,2},{12,4},{14,6},{16,24},{18,... | collective-permute-start | bytes 294920 | tf_op jit(solution)/shard_map/ppermute | solution.py:419
  267.2 7.3 %collective-permute-start.71 = (bf16[96,512]{1,0:T(8,128)(2,1)S(1)}, bf16[96,512]{1,0:T(8,128)(2,1)S(1)}, u32[]{:S(2)}, u32[]{:S(2)}) collective-permute-start(bf16[96,512]{1,0:T(8,128)(2,1)S(1)} %add_convert_fusion.24), channel_id=1, source_target_pairs={{0,2},{2,0},{4,6},{6,4},{8,10},{10,8},{12,14},{14,12},{16,18},{18,... | collective-permute-start | bytes 294920 | tf_op jit(solution)/shard_map/ppermute | solution.py:419
  267.4 8.0 %collective-permute-start.78 = (bf16[96,512]{1,0:T(8,128)(2,1)S(1)}, bf16[96,512]{1,0:T(8,128)(2,1)S(1)}, u32[]{:S(2)}, u32[]{:S(2)}) collective-permute-start(bf16[96,512]{1,0:T(8,128)(2,1)S(1)} %add_convert_fusion.22), channel_id=1, source_target_pairs={{0,4},{2,6},{4,0},{6,2},{8,12},{10,14},{12,8},{14,10},{16,20},{18,... | collective-permute-start | bytes 294920 | tf_op jit(solution)/shard_map/ppermute | solution.py:419
  281.4 8.7 %collective-permute-start.66 = (bf16[384,512]{1,0:T(8,128)(2,1)S(1)}, bf16[384,512]{1,0:T(8,128)(2,1)S(1)}, u32[]{:S(2)}, u32[]{:S(2)}) collective-permute-start(bf16[384,512]{1,0:T(8,128)(2,1)S(1)} %pad_maximum_fusion.16), channel_id=1, source_target_pairs={{0,2},{2,0},{4,6},{6,4},{8,10},{10,8},{12,14},{14,12},{16,18},{18,... | collective-permute-start | bytes 1179656 | tf_op jit(solution)/shard_map/ppermute | solution.py:419
  282.3 9.0 %collective-permute-start.73 = (bf16[384,512]{1,0:T(8,128)(2,1)S(1)}, bf16[384,512]{1,0:T(8,128)(2,1)S(1)}, u32[]{:S(2)}, u32[]{:S(2)}) collective-permute-start(bf16[384,512]{1,0:T(8,128)(2,1)S(1)} %pad_maximum_fusion.17), channel_id=1, source_target_pairs={{0,4},{2,6},{4,0},{6,2},{8,12},{10,14},{12,8},{14,10},{16,20},{18,... | collective-permute-start | bytes 1179656 | tf_op jit(solution)/shard_map/ppermute | solution.py:419
  283.8 7.8 %collective-permute-start.80 = (bf16[384,512]{1,0:T(8,128)(2,1)S(1)}, bf16[384,512]{1,0:T(8,128)(2,1)S(1)}, u32[]{:S(2)}, u32[]{:S(2)}) collective-permute-start(bf16[384,512]{1,0:T(8,128)(2,1)S(1)} %pad_maximum_fusion.18), channel_id=1, source_target_pairs={{0,8},{2,10},{4,12},{6,14},{8,0},{10,2},{12,4},{14,6},{16,24},{18,... | collective-permute-start | bytes 1179656 | tf_op jit(solution)/shard_map/ppermute | solution.py:419
  285.0 9.7 %collective-permute-start.44 = (bf16[384,512]{1,0:T(8,128)(2,1)S(1)}, bf16[384,512]{1,0:T(8,128)(2,1)S(1)}, u32[]{:S(2)}, u32[]{:S(2)}) collective-permute-start(bf16[384,512]{1,0:T(8,128)(2,1)S(1)} %pad_maximum_fusion.13), channel_id=1, source_target_pairs={{0,2},{2,0},{4,6},{6,4},{8,10},{10,8},{12,14},{14,12},{16,18},{18,... | collective-permute-start | bytes 1179656 | tf_op jit(solution)/shard_map/ppermute | solution.py:419
  286.1 8.7 %collective-permute-start.51 = (bf16[384,512]{1,0:T(8,128)(2,1)S(1)}, bf16[384,512]{1,0:T(8,128)(2,1)S(1)}, u32[]{:S(2)}, u32[]{:S(2)}) collective-permute-start(bf16[384,512]{1,0:T(8,128)(2,1)S(1)} %pad_maximum_fusion.14), channel_id=1, source_target_pairs={{0,4},{2,6},{4,0},{6,2},{8,12},{10,14},{12,8},{14,10},{16,20},{18,... | collective-permute-start | bytes 1179656 | tf_op jit(solution)/shard_map/ppermute | solution.py:419
  290.1 7.8 %collective-permute-start.58 = (bf16[384,512]{1,0:T(8,128)(2,1)S(1)}, bf16[384,512]{1,0:T(8,128)(2,1)S(1)}, u32[]{:S(2)}, u32[]{:S(2)}) collective-permute-start(bf16[384,512]{1,0:T(8,128)(2,1)S(1)} %pad_maximum_fusion.15), channel_id=1, source_target_pairs={{0,8},{2,10},{4,12},{6,14},{8,0},{10,2},{12,4},{14,6},{16,24},{18,... | collective-permute-start | bytes 1179656 | tf_op jit(solution)/shard_map/ppermute | solution.py:419
  (82 other events, 443.9 us)

commit v2 on v1

v2 whole, which is shorter than its diff:
```python
from functools import partial

import jax
import jax.numpy as jnp
from jax import lax
from jax.experimental import pallas as pl
from jax.experimental.pallas import tpu as pltpu
from jax.sharding import PartitionSpec as P

HD = 64
LEN = 1024
EPSILON = 1e-05
MASKED = -1e30
SCALE = HD**-0.5
BLOCKS = 16
PAIR = 2 * HD
MIB = 1 << 20

F32 = jnp.float32
BF16 = jnp.bfloat16


def nn(left, right):
    return lax.dot_general(left, right, (((1,), (0,)), ((), ())), preferred_element_type=F32)


def nt(left, right):
    return lax.dot_general(left, right, (((1,), (1,)), ((), ())), preferred_element_type=F32)


def tn(left, right):
    return lax.dot_general(left, right, (((0,), (0,)), ((), ())), preferred_element_type=F32)


def normalize_parts(hidden):
    average = jnp.mean(hidden, axis=-1, keepdims=True)
    centred = hidden - average
    spread = jnp.mean(centred * centred, axis=-1, keepdims=True)
    inverse = lax.rsqrt(spread + EPSILON)
    return centred * inverse, inverse


def normalize_back(grad_out, normed, inverse, gain):
    scaled = grad_out * gain
    first_mean = jnp.mean(scaled, axis=-1, keepdims=True)
    second_mean = jnp.mean(scaled * normed, axis=-1, keepdims=True)
    return inverse * (scaled - first_mean - normed * second_mean)


def gelu_parts(upper):
    phi = 0.5 + 0.5 * lax.erf(upper * 0.5**0.5)
    bell = jnp.exp(upper * upper * -0.5)
    return upper * phi, phi + upper * bell * 0.3989422804014327


def lasting(us):
    return pl.CostEstimate(flops=int(us * 1.15e9), bytes_accessed=0, transcendentals=0)


def call(kernel, outs, ins, scratch=(), limit=48, smem=(), hbm=(), hbm_outs=(), us=5):
    place = lambda i, far: pl.BlockSpec(memory_space=pl.ANY if i in far else pltpu.VMEM)
    return pl.pallas_call(
        kernel,
        out_shape=outs,
        in_specs=[
            pl.BlockSpec(memory_space=pltpu.SMEM) if i in smem else place(i, hbm)
            for i in range(len(ins))
        ],
        out_specs=[place(i, hbm_outs) for i in range(len(outs))],
        scratch_shapes=list(scratch),
        compiler_params=pltpu.CompilerParams(vmem_limit_bytes=limit * MIB),
        cost_estimate=lasting(us),
    )(*ins)


def shape(*dims, dtype=F32):
    return jax.ShapeDtypeStruct(dims, dtype)


def as_row(ref):
    return ref[...].reshape(1, -1)


def join_segments(refs):
    return jnp.concatenate([as_row(ref).astype(F32) for ref in refs], axis=1)


def as_column(row):
    return jnp.broadcast_to(row, (8, row.shape[1])).T[:, :1]


def pairs(heads):
    return [pl.ds(pair * PAIR, PAIR) for pair in range(heads // 2)]


def split_pair(block):
    owner = lax.broadcasted_iota(jnp.int32, block.shape, 1) // HD
    empty = jnp.zeros_like(block)
    return jnp.concatenate(
        [jnp.where(owner == 0, block, empty), jnp.where(owner == 1, block, empty)], axis=0
    )


def attend_kernel(*refs, split):
    xs, refs = refs[:split], refs[split:]
    segs, refs = refs[:split], refs[split:]
    wq_ref, wk_ref, wv_ref, bq_ref, bv_ref = refs[:5]
    q_ref, k_ref, v_ref, *ctx_refs, lse_ref, bias, vt, ctxt = refs[5:]
    heads = q_ref.shape[1] // HD
    block = 256
    segments = join_segments(segs)
    bias[...] = jnp.where(as_column(segments) == segments, 0.0, MASKED)
    size = LEN // split
    for i, x_ref in enumerate(xs):
        x, rows = x_ref[...], pl.ds(i * size, size)
        q_ref[rows, :] = ((nn(x, wq_ref[...]) + as_row(bq_ref)) * SCALE).astype(BF16)
        k_ref[rows, :] = nn(x, wk_ref[...]).astype(BF16)
        value = (nn(x, wv_ref[...]) + as_row(bv_ref)).astype(BF16)
        v_ref[rows, :] = value
        vt[:, rows] = value.T

    @pl.loop(0, LEN // block)
    def _(j):
        here = pl.ds(pl.multiple_of(j * block, block), block)
        products = [
            nt(k_ref[:, lanes], split_pair(q_ref[here, lanes])) for lanes in pairs(heads)
        ]
        mask = bias[:, here]
        weights, tops, totals = [], [], []
        for head in range(heads):
            start = head % 2 * block
            scores = products[head // 2][:, start : start + block] + mask
            tops.append(jnp.max(scores, axis=0, keepdims=True))
            weight = jnp.exp(scores - tops[-1])
            totals.append(jnp.sum(weight, axis=0, keepdims=True))
            weights.append(weight.astype(BF16))
        for head in range(heads):
            at = pl.ds(head * HD, HD)
            ctxt[at, here] = nn(vt[at, :], weights[head]) * (1.0 / totals[head])
            lse_ref[0, pl.ds(head, 1), here] = tops[head] + jnp.log(totals[head])

    for i, ctx_ref in enumerate(ctx_refs):
        ctx_ref[...] = ctxt[:, pl.ds(i * size, size)].T.astype(BF16)


def attention_forward(xs, segs, w_query, w_key, w_value, b_query, b_value):
    split = len(xs)
    size = LEN // split
    rows, model = xs[0].shape[0] // size, xs[0].shape[1]
    width = w_query.shape[1]
    by_row = pl.BlockSpec((LEN, width), lambda r: (r, 0))
    by_part = pl.BlockSpec((size, width), lambda r: (r, 0))
    whole = lambda *dims: pl.BlockSpec(dims, lambda r: (0,) * len(dims))
    us = 13 * rows
    query, key, value, *contexts, lse = pl.pallas_call(
        partial(attend_kernel, split=split),
        grid=(rows,),
        out_shape=[shape(rows * LEN, width, dtype=BF16)] * 3
        + [shape(rows * size, width, dtype=BF16)] * split
        + [shape(rows, 8, LEN)],
        in_specs=[pl.BlockSpec((size, model), lambda r: (r, 0))] * split
        + [pl.BlockSpec((size,), lambda r: (r,))] * split
        + [
            whole(model, width),
            whole(model, width),
            whole(model, width),
            whole(width),
            whole(width),
        ],
        out_specs=[by_row] * 3
        + [by_part] * split
        + [pl.BlockSpec((1, 8, LEN), lambda r: (r, 0, 0))],
        scratch_shapes=[
            pltpu.VMEM((LEN, LEN), F32),
            pltpu.VMEM((width, LEN), BF16),
            pltpu.VMEM((width, LEN), F32),
        ],
        compiler_params=pltpu.CompilerParams(vmem_limit_bytes=60 * MIB),
        cost_estimate=lasting(us),
    )(*xs, *segs, w_query, w_key, w_value, b_query, b_value)
    return query, key, value, contexts, lse


def attend_back_kernel(
    q_ref, k_ref, v_ref, lse_ref, *refs, pair, split
):
    segs, ctx_refs, dctx_refs = (refs[i * split : (i + 1) * split] for i in range(3))
    dq_ref, dk_ref, dv_ref, kt, dqt, dk_sum, dv_sum, inner, dctx_ref, ctx_ref, seg = refs[
        3 * split :
    ]
    size = LEN // split
    for i in range(split):
        dctx_ref[pl.ds(i * size, size), :] = dctx_refs[i][...]
        ctx_ref[pl.ds(i * size, size), :] = ctx_refs[i][...]
    width = q_ref.shape[1]
    block = 256
    kt[...] = k_ref[...].T
    seg[...] = join_segments(segs)
    column = as_column(seg[...])
    picks = lax.broadcasted_iota(jnp.int32, (8, width), 0) == (
        lax.broadcasted_iota(jnp.int32, (8, width), 1) // HD
    )
    product = ctx_ref[...].astype(F32) * dctx_ref[...].astype(F32)
    inner[...] = lax.dot_general(
        picks.astype(F32), product, (((1,), (1,)), ((), ())),
        precision=lax.Precision.HIGHEST, preferred_element_type=F32,
    )
    dk_sum[...] = jnp.zeros_like(dk_sum)
    dv_sum[...] = jnp.zeros_like(dv_sum)

    @pl.loop(0, LEN // block)
    def _(j):
        here = pl.ds(pl.multiple_of(j * block, block), block)
        allowed = column == seg[:, here]
        queries, grads = split_pair(q_ref[here, :]), split_pair(dctx_ref[here, :])
        products, slopes = nt(k_ref[...], queries), nt(v_ref[...], grads)
        weights, changes = [], []
        for side in range(2):
            at = slice(side * block, (side + 1) * block)
            scores = jnp.where(allowed, products[:, at], MASKED)
            weight = jnp.exp(scores - lse_ref[0, 2 * pair + side : 2 * pair + side + 1, here])
            change = weight * (slopes[:, at] - inner[side : side + 1, here])
            weights.append(weight.astype(BF16))
            changes.append(change.astype(BF16))
        dv_sum[...] += nn(jnp.concatenate(weights, axis=1), grads)
        dk_sum[...] += nn(jnp.concatenate(changes, axis=1), queries)
        for side in range(2):
            at = slice(side * HD, (side + 1) * HD)
            dqt[at, here] = nn(kt[at, :], changes[side]) * SCALE

    dq_ref[...] = dqt[...].T.astype(BF16)
    dk_ref[...] = dk_sum[...].astype(BF16)
    dv_ref[...] = dv_sum[...].astype(BF16)


def attention_backward(pair, query, key, value, contexts, grads, lse, segs):
    rows, split = query.shape[0] // LEN, len(contexts)
    columns = pl.BlockSpec((LEN, PAIR), lambda r: (r, pair))
    part = pl.BlockSpec((LEN // split, PAIR), lambda r: (r, pair))
    own = pl.BlockSpec((LEN, PAIR), lambda r: (r, 0))
    us = 7 * rows
    return pl.pallas_call(
        partial(attend_back_kernel, pair=pair, split=split),
        grid=(rows,),
        out_shape=[shape(rows * LEN, PAIR, dtype=BF16)] * 3,
        in_specs=[columns] * 3
        + [
            pl.BlockSpec((1, 8, LEN), lambda r: (r, 0, 0)),
        ]
        + [pl.BlockSpec((LEN // split,), lambda r: (r,))] * split
        + [part] * (2 * split),
        out_specs=[own] * 3,
        scratch_shapes=[
            pltpu.VMEM((PAIR, LEN), BF16),
            pltpu.VMEM((PAIR, LEN), F32),
            pltpu.VMEM((LEN, PAIR), F32),
            pltpu.VMEM((LEN, PAIR), F32),
            pltpu.VMEM((8, LEN), F32),
            pltpu.VMEM((LEN, PAIR), BF16),
            pltpu.VMEM((LEN, PAIR), BF16),
            pltpu.VMEM((1, LEN), F32),
        ],
        compiler_params=pltpu.CompilerParams(vmem_limit_bytes=24 * MIB),
        cost_estimate=lasting(us),
    )(query, key, value, lse, *segs, *contexts, *grads)


def rearrange(order, part, source, target):
    size = source.shape[0] // BLOCKS
    for place in range(BLOCKS):
        rows = pl.ds(pl.multiple_of(order[part, place] * size, 16), size)
        target[pl.ds(place * size, size), :] = source[rows, :]


class Copies:
    def __init__(self, sems):
        self.sems, self.used, self.open = sems, 0, []

    def start(self, source, target):
        copy = pltpu.make_async_copy(source, target, self.sems.at[self.used])
        self.used += 1
        copy.start()
        return copy

    def store(self, source, target):
        self.open.append(self.start(source, target))

    def drain(self):
        for copy in self.open:
            copy.wait()


STRIP = 512


def fold(rows):
    return sum(rows[i : i + 8, :] for i in range(0, rows.shape[0], 8))


def put_sums(sums_ref, sums):
    sums_ref[...] = jnp.zeros_like(sums_ref)
    for i, part in enumerate(sums):
        sums_ref[i : i + 1, :] = jnp.sum(part, axis=0, keepdims=True)


def forward_kernel(
    x_ref, ctx_a, ctx_b, wo_a, wo_b, b_out, gain_one, shift_one, b_down, gain_two, shift_two,
    bu_a, bu_b, order, wu_a, wu_b, wd_a, wd_b, cot_hbm,
    inverse_ref, sums_ref, mixed_hbm, after_hbm, normed_hbm, slope_hbm, grad_hbm, low_hbm,
    down_b, moved_hbm, act_hbm,
    wu, wd, cot, mixed, after_buf, normed_buf, slope, grad_buf, low_buf, act, flipped, moved, parts,
    total, sems,
):
    half = wu_a.shape[1]
    chunk = 512
    copies = Copies(sems)
    ups, downs = [], []
    for side, (up, down) in enumerate(((wu_a, wd_a), (wu_b, wd_b))):
        for start in range(0, half, chunk):
            to = pl.ds(side * half + start, chunk)
            ups.append(copies.start(up.at[:, pl.ds(start, chunk)], wu.at[:, to]))
            downs.append(copies.start(down.at[pl.ds(start, chunk), :], wd.at[to, :]))
    cot_copy = copies.start(cot_hbm, cot)
    b_out, gain_one, shift_one, b_down, gain_two, shift_two = map(
        as_row, (b_out, gain_one, shift_one, b_down, gain_two, shift_two)
    )
    biases = [as_row(bu_a), as_row(bu_b)]
    total[...] = nn(ctx_a[...], wo_a[...]) + nn(ctx_b[...], wo_b[...])

    @pl.loop(0, x_ref.shape[0] // STRIP)
    def _(i):
        rows = pl.ds(pl.multiple_of(i * STRIP, STRIP), STRIP)
        normed, inverse = normalize_parts(x_ref[rows, :].astype(F32) + total[rows, :] + b_out)
        normed_buf[rows, :] = normed
        inverse_ref[rows, :] = inverse
        after_buf[rows, :] = (normed * gain_one + shift_one).astype(BF16)

    copies.store(normed_buf, normed_hbm)
    copies.store(after_buf, after_hbm)
    after_low = after_buf[...]

    def raise_up(i):
        ups[i].wait()
        here = pl.ds(i * chunk, chunk)
        start = i * chunk % half
        return nn(after_low, wu[:, here]) + biases[i * chunk // half][:, start : start + chunk]

    count = 2 * half // chunk
    upper = raise_up(0)
    for i in range(count):
        following = raise_up(i + 1) if i + 1 < count else None
        here = pl.ds(i * chunk, chunk)
        active, steep = gelu_parts(upper)
        act[:, here] = active.astype(BF16)
        slope[:, here] = steep.astype(BF16)
        copies.store(slope.at[:, here], slope_hbm.at[:, here])
        upper = following
    for copy in downs:
        copy.wait()
    total[...] = nn(act[...], wd[...])
    cot_copy.wait()

    def finish(i, sums):
        rows = pl.ds(pl.multiple_of(i * STRIP, STRIP), STRIP)
        after = normed_buf[rows, :] * gain_one + shift_one
        normed, inverse = normalize_parts(after + total[rows, :] + b_down)
        mixed[rows, :] = (normed * gain_two + shift_two).astype(BF16)
        outer = cot[rows, :].astype(F32)
        grad = normalize_back(outer, normed, inverse, gain_two)
        grad_buf[rows, :] = grad
        low_buf[rows, :] = grad.astype(BF16)
        return tuple(
            held + fold(extra) for held, extra in zip(sums, (outer * normed, outer, grad))
        )

    empty = jnp.zeros((8, x_ref.shape[1]), F32)
    sums = lax.fori_loop(0, x_ref.shape[0] // STRIP, finish, (empty, empty, empty))
    copies.store(mixed, mixed_hbm)
    copies.store(grad_buf, grad_hbm)
    copies.store(low_buf, low_hbm)
    flipped[...] = grad_buf[...].T.astype(BF16)
    put_sums(sums_ref, sums)
    cols = half // 3
    for p in range(3):
        rearrange(order, p, flipped, moved.at[p])
    for p in range(3):
        here = pl.ds(half + p * cols, cols)
        parts[p] = nn(moved[p], act[:, here]).astype(BF16)
        copies.store(parts.at[p], down_b.at[p])
    copies.store(moved, moved_hbm)
    copies.store(act.at[:, pl.ds(0, half)], act_hbm)
    copies.drain()


def upper_kernel(
    order, low_hbm, after_hbm, moved_hbm, act_hbm, slope_hbm, wd_a, wd_b,
    sums, gu_hbm, down_a, up_a, up_b,
    wd, slope, gu, low_ref, after_ref, grad_moved, act_ref, flipped, moved, parts, sems,
):
    half = wd_a.shape[0]
    cols = half // 3
    copies = Copies(sems)
    slopes, downs = {}, {}
    low_copy = copies.start(low_hbm, low_ref)
    after_copy = copies.start(after_hbm, after_ref)
    for side, down in ((1, wd_b), (0, wd_a)):
        for p in range(3):
            to = pl.ds(side * half + p * cols, cols)
            downs[side, p] = copies.start(down.at[pl.ds(p * cols, cols), :], wd.at[to, :])
            slopes[side, p] = copies.start(slope_hbm.at[:, to], slope.at[:, to])
    rest = [copies.start(moved_hbm, grad_moved), copies.start(act_hbm, act_ref)]
    low_copy.wait()
    after_copy.wait()
    low = low_ref[...]
    flipped[...] = after_ref[...].T
    for p in range(3):
        rearrange(order, p, flipped, moved.at[p])

    def pull(side, p):
        downs[side, p].wait()
        return nt(low, wd[pl.ds(side * half + p * cols, cols), :])

    todo = [(side, p) for side in (1, 0) for p in range(3)]
    pulled = pull(*todo[0])
    for i, (side, p) in enumerate(todo):
        following = pull(*todo[i + 1]) if i + 1 < len(todo) else None
        here = pl.ds(side * half + p * cols, cols)
        slopes[side, p].wait()
        gu[:, here] = (pulled * slope[:, here].astype(F32)).astype(BF16)
        copies.store(gu.at[:, here], gu_hbm.at[:, here])
        grad = gu[:, here]
        sums[:, here] = jnp.sum(grad.astype(F32), axis=0, keepdims=True)
        parts[side, p] = nn(moved[p], grad).astype(BF16)
        copies.store(parts.at[side, p], (up_b if side else up_a).at[p])
        pulled = following
    for copy in rest:
        copy.wait()
    for p in range(3):
        parts[2, p] = nn(grad_moved[p], act_ref[:, pl.ds(p * cols, cols)]).astype(BF16)
        copies.store(parts.at[2, p], down_a.at[p])
    copies.drain()


def first_norm_kernel(
    inverse_ref, gain_ref, order, wo_a, wo_b, ctx_a, ctx_b, grad_hbm, normed_hbm, gu_hbm, wu_a, wu_b,
    sums_ref, gctx_a, gctx_b, out_a, out_b, grad_one_hbm,
    gu, wu, grad_buf, normed_buf, one, acc, low_buf, flipped, moved, sems,
):
    half = wu_a.shape[1]
    chunk = 512
    copies = Copies(sems)
    pending = []
    for side, up in enumerate((wu_a, wu_b)):
        for start in range(0, half, chunk):
            to = pl.ds(side * half + start, chunk)
            pending.append(
                (
                    copies.start(gu_hbm.at[:, to], gu.at[:, to]),
                    copies.start(up.at[:, pl.ds(start, chunk)], wu.at[:, to]),
                )
            )
    grad_copy = copies.start(grad_hbm, grad_buf)
    normed_copy = copies.start(normed_hbm, normed_buf)
    step = half // chunk
    for side in range(2):
        for first, second in pending[side * step : (side + 1) * step]:
            first.wait()
            second.wait()
        at = pl.ds(side * half, half)
        term = nt(gu[:, at], wu[:, at])
        acc[...] = term if side == 0 else acc[...] + term
    grad_copy.wait()
    normed_copy.wait()
    gain = as_row(gain_ref)

    def finish(i, sums):
        rows = pl.ds(pl.multiple_of(i * STRIP, STRIP), STRIP)
        after = grad_buf[rows, :] + acc[rows, :]
        normed = normed_buf[rows, :]
        grad = normalize_back(after, normed, inverse_ref[rows, :], gain)
        one[rows, :] = grad
        low_buf[rows, :] = grad.astype(BF16)
        return tuple(
            held + fold(extra) for held, extra in zip(sums, (after * normed, after, grad))
        )

    empty = jnp.zeros((8, one.shape[1]), F32)
    sums = lax.fori_loop(0, one.shape[0] // STRIP, finish, (empty, empty, empty))
    copies.store(one, grad_one_hbm)
    low = low_buf[...]
    gctx_b[...] = nt(low, wo_b[...]).astype(BF16)
    gctx_a[...] = nt(low, wo_a[...]).astype(BF16)
    flipped[...] = one[...].T.astype(BF16)
    put_sums(sums_ref, sums)
    cols = ctx_a.shape[1] // 3
    for p in range(3):
        rearrange(order, p, flipped, moved)
        here = pl.ds(p * cols, cols)
        out_b[p] = nn(moved[...], ctx_b[:, here]).astype(BF16)
        out_a[p] = nn(moved[...], ctx_a[:, here]).astype(BF16)
    copies.drain()


def project_kernel(*refs):
    x_a, x_b, out_a, out_b, order = refs[:5]
    grads, (packed, sums, joint, flipped, moved) = refs[5:-5], refs[-5:]
    width = joint.shape[1] // 3
    cols = width // 3
    here = x_a.shape[0]
    flipped[:, pl.ds(0, here)] = x_a[...].T
    flipped[:, pl.ds(here, here)] = x_b[...].T
    for i, grad in enumerate(grads):
        at = pl.ds(i % 3 * width + i // 3 * PAIR, PAIR)
        joint[:, at] = grad[...]
    sums[...] = jnp.sum(joint[...].astype(F32), axis=0, keepdims=True)
    for p in range(3):
        rearrange(order, p, flipped, moved)
        packed[p, :, pl.ds(0, width)] = nn(
            moved[...], joint[:, pl.ds(p * width, width)]
        ).astype(BF16)
        packed[p, :, pl.ds(width, cols)] = (
            out_a[p].astype(F32) + out_b[p].astype(F32)
        ).astype(BF16)


def tokens_kernel(joint, w_query, w_key, w_value, grad_one, part_ref, own_ref):
    rows, width = own_ref.shape[0], w_query.shape[1]
    for first, out_ref in ((rows, part_ref), (0, own_ref)):
        total = grad_one[...] if first == 0 else 0.0
        for i, weight in enumerate((w_query, w_key, w_value)):
            part = joint[pl.ds(first, rows), pl.ds(i * width, width)]
            total = total + nt(part, weight[...])
        out_ref[...] = total.astype(out_ref.dtype)


def unpack_both_kernel(a_ref, b_ref, c_ref, order, down_ref, up_ref, natural):
    size, cols = a_ref.shape[0] // BLOCKS, a_ref.shape[1] // 2
    for p, ref in enumerate((a_ref, b_ref, c_ref)):
        here = pl.ds(p * cols, cols)
        for place in range(BLOCKS):
            rows = pl.ds(pl.multiple_of(order[p, place] * size, 16), size)
            at = pl.ds(place * size, size)
            natural[rows, here] = ref[at, pl.ds(0, cols)].astype(F32)
            up_ref[rows, here] = ref[at, pl.ds(cols, cols)].astype(F32)
        down_ref[here, :] = natural[:, here].T


def unpack_project_kernel(a_ref, b_ref, c_ref, order, q_ref, k_ref, v_ref, out_ref, natural):
    width = q_ref.shape[1]
    size, cols = a_ref.shape[0] // BLOCKS, width // 3
    for p, (ref, grad) in enumerate(((a_ref, q_ref), (b_ref, k_ref), (c_ref, v_ref))):
        for place in range(BLOCKS):
            rows = pl.ds(pl.multiple_of(order[p, place] * size, 16), size)
            grad[rows, :] = ref[pl.ds(place * size, size), pl.ds(0, width)].astype(F32)
            natural[rows, pl.ds(p * cols, cols)] = ref[
                pl.ds(place * size, size), pl.ds(width, cols)
            ].astype(F32)
    out_ref[...] = natural[...].T


def swap(value, bit, count, name="swap"):
    with jax.named_scope(name):
        return lax.ppermute(value, "dp", [(i, i ^ bit) for i in range(count)])


def across(value):
    return lax.ppermute(value, "tensor", [(0, 1), (1, 0)])


def add(left, right):
    return (left.astype(F32) + right.astype(F32)).astype(BF16)


STAGES = ((1, 2, 4, 8), (2, 4, 1, 8), (4, 1, 2, 8))


def block_order():
    mine = lax.rem(lax.axis_index("dp"), BLOCKS // 2)
    rows = []
    for bits in STAGES:
        rows.append(
            [
                sum(bit for i, bit in enumerate(bits) if place >> (len(bits) - 1 - i) & 1)
                for place in range(BLOCKS)
            ]
        )
    return jnp.bitwise_xor(jnp.array(rows, jnp.int32), mine.astype(jnp.int32))


def halves(own, other):
    half = own.shape[1] // 2
    both = [
        [own[p, side * half : (side + 1) * half] for p in range(3)] for side in range(2)
    ]
    if other is not None:
        both = [
            [add(both[side][p], other[p, side * half : (side + 1) * half]) for p in range(3)]
            for side in range(2)
        ]
    return both


def send_stage(sends, step, count, name):
    return [
        swap(sends[p], STAGES[p][step], count, f"{name}_send{step}_{p}") for p in range(3)
    ]


def next_halves(keeps, gots):
    half = keeps[0].shape[0] // 2
    cut = lambda side: [
        add(keeps[p][side * half : (side + 1) * half], gots[p][side * half : (side + 1) * half])
        for p in range(3)
    ]
    return cut(0), cut(1)


def last_stages(keep, got, count, name):
    both = add(keep, got)
    extra = BLOCKS // 2
    while extra < count:
        both = add(both, swap(both, extra, count, name))
        extra *= 2
    return both


def gather_stage(values, step, count, name):
    return [
        jnp.concatenate(
            [values[p], swap(values[p], STAGES[p][step], count, f"{name}_gather{step}_{p}")],
            axis=0,
        )
        for p in range(3)
    ]


def after(values, *earlier):
    return lax.optimization_barrier((values, *earlier))[0]


def shards(
    tokens, segment_ids, w_query, w_key, w_value, b_query, b_value, w_out, b_out, gain_attn,
    shift_attn, w_up, b_up, w_down, b_down, gain_ffn, shift_ffn, cotangent,
):
    count = lax.axis_size("dp")
    here, model = tokens.shape
    width, half = w_query.shape[1], w_up.shape[1]
    row = lambda vector: vector.reshape(1, -1)

    tokens_b = across(tokens)
    segments_b, bu_b = across(segment_ids), across(b_up)
    wo_b, wu_b, wd_b = across(w_out), across(w_up), across(w_down)
    order = block_order()
    one_row = here < LEN
    lay = lambda own, other: (
        [own, other] if one_row else [jnp.concatenate([own, other], axis=0)]
    )
    segs = lay(segment_ids, segments_b)
    query, key, value, contexts, lse = attention_forward(
        lay(tokens, tokens_b), after(segs, order), w_query, w_key, w_value, b_query, b_value
    )
    if one_row:
        ctx_a, ctx_b = contexts
    else:
        ctx_a, ctx_b = contexts[0][:here], contexts[0][here:]
    ctx_b = across(ctx_b)

    low = lambda *dims: shape(*dims, dtype=BF16)
    held = lambda *dims: pltpu.VMEM(dims, BF16)
    wide = lambda *dims: pltpu.VMEM(dims, F32)
    parts = low(3, model, half // 3)
    (
        inverse_one, sums_two, mixed, after_low, normed_one, slope, grad_two, grad_two_low,
        down_b, grad_moved, act_a,
    ) = call(
        forward_kernel,
        [
            shape(here, 1), shape(8, model), low(here, model), low(here, model),
            shape(here, model), low(here, 2 * half), shape(here, model), low(here, model),
            parts, low(3, model, here), low(here, half),
        ],
        [
            tokens, ctx_a, ctx_b, w_out, wo_b, b_out, gain_attn, shift_attn, b_down, gain_ffn,
            shift_ffn, b_up, bu_b, order, w_up, wu_b, w_down, wd_b, cotangent,
        ],
        [
            held(model, 2 * half), held(2 * half, model), held(here, model), held(here, model),
            held(here, model), wide(here, model), held(here, 2 * half), wide(here, model),
            held(here, model), held(here, 2 * half), held(model, here), held(3, model, here),
            held(3, model, half // 3), wide(here, model), pltpu.SemaphoreType.DMA((40,)),
        ],
        limit=56,
        smem=(13,),
        hbm=(14, 15, 16, 17, 18),
        hbm_outs=range(2, 11),
        us=23,
    )
    down_got = across(down_b)

    sums_up, gu, down_a, up_a, up_b = call(
        upper_kernel,
        [shape(1, 2 * half), low(here, 2 * half), parts, parts, parts],
        [order, grad_two_low, after_low, grad_moved, act_a, slope, w_down, wd_b],
        [
            held(2 * half, model), held(here, 2 * half), held(here, 2 * half),
            held(here, model), held(here, model), held(3, model, here), held(here, half),
            held(model, here), held(3, model, here), held(3, 3, model, half // 3),
            pltpu.SemaphoreType.DMA((40,)),
        ],
        smem=(0,),
        hbm=(1, 2, 3, 4, 5, 6, 7),
        hbm_outs=(1, 2, 3, 4),
        limit=60,
        us=12,
    )
    up_got = across(up_b)
    down_keep, down_send = halves(down_a, down_got)
    down_new = send_stage(down_send, 0, count, "down")
    up_keep, up_send = halves(after(up_a, down_send), up_got)
    up_new = send_stage(up_send, 0, count, "up")

    sums_one, gctx_a, gctx_b, out_a, out_b, grad_one = call(
        first_norm_kernel,
        [
            shape(8, model), low(here, width), low(here, width),
            low(3, model, width // 3), low(3, model, width // 3), shape(here, model),
        ],
        [
            inverse_one, gain_attn, order, w_out, wo_b, ctx_a, ctx_b, grad_two, normed_one,
            after(gu, down_send, up_send), w_up, wu_b,
        ],
        [
            held(here, 2 * half), held(model, 2 * half), wide(here, model), wide(here, model),
            wide(here, model), wide(here, model), held(here, model), held(model, here),
            held(model, here), pltpu.SemaphoreType.DMA((24,)),
        ],
        smem=(2,),
        hbm=(7, 8, 9, 10, 11),
        hbm_outs=(5,),
        us=12,
    )
    grad_contexts = lay(gctx_a, across(gctx_b))
    out_got = across(out_b)

    back = lambda pair, earlier: attention_backward(
        pair, query, key, value, contexts, after(grad_contexts, earlier), lse, segs
    )
    join = lambda one, two: [jnp.concatenate(pair, axis=1) for pair in zip(one, two)]
    down_keep, down_send = next_halves(down_keep, after(down_new, sums_one))
    up_keep, up_send = next_halves(up_keep, after(up_new, sums_one))
    both_keep, both_send = join(down_keep, up_keep), join(down_send, up_send)
    both_new = send_stage(both_send, 1, count, "both")
    grads = back(0, both_send)
    both_keep, both_send = next_halves(both_keep, after(both_new, grads))
    both_new = send_stage(both_send, 2, count, "both")
    grads += back(1, (grads, both_send))
    both_keep, both_new = after((both_keep, both_new), grads)
    exchange = lambda p: last_stages(both_keep[p], both_new[p], count, f"both_exchange{p}")
    both = [exchange(0)]
    grads += back(2, (grads, both_new))
    both_keep, both_new = after((both_keep, both_new), both, grads)
    both.append(exchange(1))

    packed, sums_three, joint = call(
        project_kernel,
        [parts, shape(1, 3 * width), low(2 * here, 3 * width)],
        [tokens, tokens_b, out_a, out_got, order, *after(grads, both[0])],
        [held(model, 2 * here), held(model, 2 * here)],
        smem=(4,),
        us=7,
    )
    last_keep, last_send = halves(packed, None)
    last_new = send_stage(last_send, 0, count, "last")
    both_keep, both_new = after((both_keep, both_new), both, last_send)
    both.append(exchange(2))
    token_part, token_own = call(
        tokens_kernel,
        [low(here, model), shape(here, model)],
        [after(joint, last_send, both[1]), w_query, w_key, w_value, grad_one],
        us=5,
    )
    token_got = across(token_part)
    grad_tokens = token_own + token_got.astype(F32)

    shared = jnp.concatenate([sums_one[:3], sums_two[:3]], axis=0)
    shared, sums_up = after((shared, sums_up), token_own)
    sums_up = sums_up[0, :half] + across(sums_up[0, half:])
    shared = (shared + across(shared)).reshape(-1)
    small = jnp.concatenate(
        [shared, sums_three[0, :width], sums_three[0, 2 * width :], sums_up]
    ).reshape(-1, 128)
    bits = [1 << i for i in range(count.bit_length() - 1)]
    step_small = lambda value, i: value + swap(value, bits[i], count, f"small{i}")

    last_keep, last_send = next_halves(last_keep, after(last_new, token_own))
    last_new = send_stage(last_send, 1, count, "last")
    both = gather_stage(after(both, last_send), 2, count, "both")
    small = step_small(after(small, last_send), 0)
    last_keep, last_send = next_halves(last_keep, after(last_new, both))
    last_new = send_stage(last_send, 2, count, "last")
    both = gather_stage(after(both, last_send), 1, count, "both")
    small = step_small(after(small, last_send), 1)
    last_keep, last_new = after((last_keep, last_new), small)
    last = jnp.split(
        last_stages(
            jnp.concatenate(last_keep), jnp.concatenate(last_new), count, "last_exchange"
        ),
        3,
    )
    both = gather_stage(both, 0, count, "both")
    small = step_small(small, 2)
    last = gather_stage(after(last, small), 2, count, "last")
    last = gather_stage(after(last, both), 1, count, "last")
    for i in range(3, len(bits)):
        small = step_small(after(small, last), i)
    last = gather_stage(last, 0, count, "last")
    grad_w_down, grad_w_up = call(
        unpack_both_kernel,
        [shape(half, model), shape(model, half)],
        [*both, order],
        [wide(model, half)],
        limit=40,
        smem=(3,),
    )
    grad_w_query, grad_w_key, grad_w_value, grad_w_out = call(
        unpack_project_kernel,
        [shape(model, width)] * 3 + [shape(width, model)],
        [*last, order],
        [wide(model, width)],
        limit=40,
        smem=(3,),
    )

    small = small.reshape(-1)
    cuts = [model * i for i in range(1, 7)] + [6 * model + width, 6 * model + 2 * width]
    (
        grad_gain_attn, grad_shift_attn, grad_b_out, grad_gain_ffn, grad_shift_ffn, grad_b_down,
        grad_b_query, grad_b_value, grad_b_up,
    ) = jnp.split(small, cuts)
    return (
        mixed, grad_tokens, grad_w_query, grad_w_key, grad_w_value, grad_b_query, grad_b_value,
        grad_w_out, grad_b_out, grad_gain_attn, grad_shift_attn, grad_w_up, grad_b_up, grad_w_down,
        grad_b_down, grad_gain_ffn, grad_shift_ffn,
    )


def solution(mesh):
    placed = (
        P(("dp", "tensor"), None),
        P(("dp", "tensor")),
        P(None, "tensor"),
        P(None, "tensor"),
        P(None, "tensor"),
        P("tensor"),
        P("tensor"),
        P("tensor", None),
        P(),
        P(),
        P(),
        P(None, "tensor"),
        P("tensor"),
        P("tensor", None),
        P(),
        P(),
        P(),
        P(("dp", "tensor"), None),
    )
    return jax.shard_map(
        shards,
        mesh=mesh,
        in_specs=placed,
        out_specs=(
            P(("dp", "tensor"), None),
            P(("dp", "tensor"), None),
            P(None, "tensor"),
            P(None, "tensor"),
            P(None, "tensor"),
            P("tensor"),
            P("tensor"),
            P("tensor", None),
            P(),
            P(),
            P(),
            P(None, "tensor"),
            P("tensor"),
            P("tensor", None),
            P(),
            P(),
            P(),
        ),
        check_vma=False,
    )
```

time: 307 us -> 260 us (0.85)
  starting transfers between devices: 85.8 us -> 57 us
  local copies, waits for them, and re-layouts: 25.7 us -> 8.99 us
  waiting for transfers between devices: 67 us -> 74.4 us
  matrix products: 5.43 us -> 0 us
    ppermute x67 -> x47, starting transfers between devices: 82.1 us -> 53.2 us  [swap(): return lax.ppermute(value, 'dp', [(i, i ^ bit) for i in range(count)])]
    unnamed x100 -> x72, local copies, waits for them, and re-layouts: 16 us -> 2.55 us
    ppermute x67 -> x47, waiting for transfers between devices: 62.7 us -> 72.2 us  [swap(): return lax.ppermute(value, 'dp', [(i, i ^ bit) for i in range(count)])]
    dot_general x6 -> x0, matrix products: 5.43 us -> none  [nt(): lax.dot_general(left, right, (((1,), (1,)), ((), ())), preferred_element_...]
    reshape x11 -> x0, local copies, waits for them, and re-layouts: 4.91 us -> none  [the longest x10 4.68 us: shards(): row = lambda vector: vector.reshape(1, -1)]
    pallas_call x7, Pallas kernels: 62.9 us -> 66.5 us  [call(): pl.pallas_call(kernel, out_shape=outs, in_specs=[pl.BlockSpec(memory_spac...]
    pallas_call x2 -> x4, Pallas kernels: 39.7 us -> 36.9 us  [the longest x3 20.7 us: attention_backward(): pl.pallas_call(partial(attend_back_kernel, pair=pair, split=split), grid=...]
    convert_element_type x32 -> x20, other arithmetic: 8.26 us -> 6.73 us  [add(): return (left.astype(F32) + right.astype(F32)).astype(BF16)]
  transfers between devices with their start and end apart: 81 -> 61, of which waited for: 33 -> 23; matrix products, arithmetic and copies ran while one was open for 10% -> 7% of each run, Pallas kernels for 25% -> 30%
where the time goes in v2:
time: 260 us; the launch traced here: 256 us
  Pallas kernels  103 us (40%)
  waiting for transfers between devices  74.4 us (29%)
  starting transfers between devices  57 us (22%)
  other arithmetic  10.4 us (4%)
  local copies, waits for them, and re-layouts  8.99 us (3%)
    ppermute x47, waiting for transfers between devices, swap(): return lax.ppermute(value, 'dp', [(i, i ^ bit) for i in range(count)])  72.2 us
    pallas_call x7, Pallas kernels, call(): pl.pallas_call(kernel, out_shape=outs, in_specs=[pl.BlockSpec(memory_spac...  66.5 us
    ppermute x47, starting transfers between devices, swap(): return lax.ppermute(value, 'dp', [(i, i ^ bit) for i in range(count)])  53.2 us
    pallas_call x3, Pallas kernels, attention_backward(): pl.pallas_call(partial(attend_back_kernel, pair=pair, split=split), grid=...  20.7 us
    pallas_call x1, Pallas kernels, attention_forward(): pl.pallas_call(partial(attend_kernel, split=split), grid=(rows,), out_sha...  16.2 us
    convert_element_type x20, other arithmetic, add(): return (left.astype(F32) + right.astype(F32)).astype(BF16)  6.73 us
  transfers between devices with their start and end apart: 61, of which 23 were waited for; matrix products, arithmetic and copies ran while one was open for 7% of the time, Pallas kernels for 30%

profile of v2, /device:TPU:0, one launch (start us, length us, event | category | flops | bytes accessed | tf_op | source)
XLA Modules:
  0.0 256.0 jit_solution(13712209921056326406)
XLA Ops:
  5.1 16.2 %shard_map.314 = (bf16[1024,384]{1,0:T(8,128)(2,1)}, bf16[1024,384]{1,0:T(8,128)(2,1)}, bf16[1024,384]{1,0:T(8,128)(2,1)}, bf16[512,384]{1,0:T(8,128)(2,1)}, bf1...) custom-call(bf16[512,768]{1,0:T(8,128)(2,1)} %refs_0_.9, bf16[512,768]{1,0:T(8,128)(2,1)} %copy-done.2, s32[512]{0:T(512)} %refs_0_.8, ...), custom_call_target="tpu_custom_call" | custom-call | flops 14949999616 | tf_op jit(solution)/shard_map/pallas_call | solution.py:155
  23.9 23.2 %shard_map.315 = (f32[512,1]{1,0:T(8,128)}, f32[8,768]{1,0:T(8,128)}, bf16[512,768]{1,0:T(8,128)(2,1)}, bf16[512,768]{1,0:T(8,128)(2,1)}, f32[512,768]{1,0:T(8,1...) custom-call(bf16[512,768]{1,0:T(8,128)(2,1)} %refs_0_.9, ...), custom_call_target="tpu_custom_call" | custom-call | flops 26449999872 | tf_op jit(solution)/shard_map/pallas_call | solution.py:62
  47.6 13.2 %shard_map.316 = (f32[1,3072]{1,0:T(1,128)}, bf16[512,3072]{1,0:T(8,128)(2,1)}, bf16[3,768,512]{2,1,0:T(8,128)(2,1)}, bf16[3,768,512]{2,1,0:T(8,128)(2,1)}, bf16[3,768,512]{2,1,0:T(8,128)(2,1)}) custom-call(s32[3,16]{1,0:T(4,128)} %broadcast_xor_fusion.order.refs_4_, bf16[512,768]{1,0:T(8,128)(2,1)} %get-tuple-element.143.low_hbm, ...), custom_call_target="tpu_custom_call" | custom-call | flops 13799999488 | tf_op jit(solution)/shard_map/pallas_call | solution.py:62
  61.0 2.5 add_convert_fusion.1
  63.5 3.0 %collective-permute-start.13 = (bf16[384,512]{1,0:T(8,128)(2,1)S(1)}, bf16[384,512]{1,0:T(8,128)(2,1)S(1)}, u32[]{:S(2)}, u32[]{:S(2)}) collective-permute-start(bf16[384,512]{1,0:T(8,128)(2,1)S(1)} %get-tuple-element.260), channel_id=1, source_target_pairs={{0,8},{2,10},{4,12},{6,14},{8,0},{10,2},{12,4},{14,6},{16,24},{18,... | collective-permute-start | bytes 1179656 | tf_op jit(solution)/shard_map/down_send0_2/ppermute | solution.py:563
  66.5 1.5 collective-permute-start.12
  68.0 1.5 collective-permute-start.11
  71.3 5.1 %collective-permute-done.13 = bf16[384,512]{1,0:T(8,128)(2,1)S(1)} collective-permute-done((bf16[384,512]{1,0:T(8,128)(2,1)S(1)}, bf16[384,512]{1,0:T(8,128)(2,1)S(1)}, u32[]{:S(2)}, u32[]{:S(2)}) %collective-permute-start.13) | collective-permute-done | bytes 393248 | tf_op jit(solution)/shard_map/down_send0_2/ppermute | solution.py:563
  76.4 2.0 collective-permute-start.14
  78.4 10.7 %shard_map.317 = (f32[8,768]{1,0:T(8,128)S(1)}, bf16[512,384]{1,0:T(8,128)(2,1)S(1)}, bf16[512,384]{1,0:T(8,128)(2,1)S(1)}, bf16[3,768,128]{2,1,0:T(8,128)(2,1)S...) custom-call(f32[512,1]{1,0:T(8,128)S(1)} %copy-done.21, f32[768]{0:T(1024)S(1)} %copy-done.13, ...), custom_call_target="tpu_custom_call" | custom-call | flops 13799999488 | tf_op jit(solution)/shard_map/pallas_call | solution.py:62
  90.4 2.1 collective-permute-start.18
  92.9 1.6 collective-permute-start.17
  94.5 6.8 %shard_map.318 = (bf16[1024,128]{1,0:T(8,128)(2,1)S(1)}, bf16[1024,128]{1,0:T(8,128)(2,1)S(1)}, bf16[1024,128]{1,0:T(8,128)(2,1)S(1)}) custom-call(bf16[1024,384]{1,0:T(8,128)(2,1)S(1)} %copy-done.17, bf16[1024,384]{1,0:T(8,128)(2,1)S(1)} %copy-done.18, bf16[1024,384]{1,0:T(8,128)(2,1)S(1)} %copy-done.19, f32[1,8,1024]{2,1,0:T(8,128)S(1)} %copy-done.22, ...), custom_call_target="tpu_custom_call" | custom-call | flops 8049999872 | tf_op jit(solution)/shard_map/pallas_call | solution.py:242
  101.6 1.9 collective-permute-done.17
  103.6 1.6 collective-permute-start.22
  105.3 1.6 collective-permute-start.21
  107.5 6.8 %shard_map.319 = (bf16[1024,128]{1,0:T(8,128)(2,1)S(1)}, bf16[1024,128]{1,0:T(8,128)(2,1)S(1)}, bf16[1024,128]{1,0:T(8,128)(2,1)S(1)}) custom-call(bf16[1024,384]{1,0:T(8,128)(2,1)S(1)} %copy-done.17, bf16[1024,384]{1,0:T(8,128)(2,1)S(1)} %copy-done.18, bf16[1024,384]{1,0:T(8,128)(2,1)S(1)} %copy-done.19, f32[1,8,1024]{2,1,0:T(8,128)S(1)} %copy-done.22, ...), custom_call_target="tpu_custom_call" | custom-call | flops 8049999872 | tf_op jit(solution)/shard_map/pallas_call | solution.py:242
  114.4 2.7 %collective-permute-start.23 = (bf16[96,1024]{1,0:T(8,128)(2,1)S(1)}, bf16[96,1024]{1,0:T(8,128)(2,1)S(1)}, u32[]{:S(2)}, u32[]{:S(2)}) collective-permute-start(bf16[96,1024]{1,0:T(8,128)(2,1)S(1)} %add_convert_fusion.19), channel_id=1, source_target_pairs={{0,16},{2,18},{4,20},{6,22},{8,24},{10,26},{12,28},{14,30},{16,0},... | collective-permute-start | bytes 589832 | tf_op jit(solution)/shard_map/both_exchange0/ppermute | solution.py:563
  117.1 7.0 %shard_map.320 = (bf16[1024,128]{1,0:T(8,128)(2,1)S(1)}, bf16[1024,128]{1,0:T(8,128)(2,1)S(1)}, bf16[1024,128]{1,0:T(8,128)(2,1)S(1)}) custom-call(bf16[1024,384]{1,0:T(8,128)(2,1)S(1)} %copy-done.17, bf16[1024,384]{1,0:T(8,128)(2,1)S(1)} %copy-done.18, bf16[1024,384]{1,0:T(8,128)(2,1)S(1)} %copy-done.19, f32[1,8,1024]{2,1,0:T(8,128)S(1)} %copy-done.22, ...), custom_call_target="tpu_custom_call" | custom-call | flops 8049999872 | tf_op jit(solution)/shard_map/pallas_call | solution.py:242
  124.7 6.0 %shard_map.321 = (bf16[3,768,512]{2,1,0:T(8,128)(2,1)}, f32[1,1152]{1,0:T(1,128)S(1)}, bf16[1024,1152]{1,0:T(8,128)(2,1)}) custom-call(bf16[512,768]{1,0:T(8,128)(2,1)S(1)} %copy-done.1, bf16[512,768]{1,0:T(8,128)(2,1)S(1)} %copy-done.3, bf16[3,768,128]{2,1,0:T(8,128)(2,1)S(1)} %get-tuple-element.155.refs_2_, ...), custom_call_target="tpu_custom_call" | custom-call | flops 8049999872 | tf_op jit(solution)/shard_map/pallas_call | solution.py:62
  130.7 2.4 slice_bitcast_fusion
  133.1 3.8 %collective-permute-start.28 = (bf16[384,512]{1,0:T(8,128)(2,1)}, bf16[384,512]{1,0:T(8,128)(2,1)S(1)}, u32[]{:S(2)}, u32[]{:S(2)}) collective-permute-start(bf16[384,512]{1,0:T(8,128)(2,1)} %get-tuple-element.279), channel_id=1, source_target_pairs={{0,8},{2,10},{4,12},{6,14},{8,0},{10,2},{12,4},{14,6},{16,24},{18,... | collective-permute-start | bytes 1179656 | tf_op jit(solution)/shard_map/last_send0_2/ppermute | solution.py:563
  138.6 4.4 %shard_map.322 = (bf16[512,768]{1,0:T(8,128)(2,1)S(1)}, f32[512,768]{1,0:T(8,128)S(1)}) custom-call(bf16[1024,1152]{1,0:T(8,128)(2,1)} %get-tuple-element.207.joint, bf16[768,384]{1,0:T(8,128)(2,1)S(1)} %copy-done.5, bf16[768,384]{1,0:T(8,128)(2,1)S(1)} %copy-done.6, bf16[768,384]{1,0:T(8,128)(2,1)S(1)} %copy-done.7, f32[512,768]{1,0:T(8,128)S(1)} %get-tuple-element.208.grad_one), custom_call_target="tpu_custom_call" | custom-call | flops 5750000128 | tf_op jit(solution)/shard_map/pallas_call | solution.py:62
  145.3 1.3 reshape.152
  146.7 1.9 fusion.6
  148.6 1.5 collective-permute-start.31
  150.6 5.3 %collective-permute-done.32 = bf16[96,1024]{1,0:T(8,128)(2,1)S(1)} collective-permute-done((bf16[96,1024]{1,0:T(8,128)(2,1)S(1)}, bf16[96,1024]{1,0:T(8,128)(2,1)S(1)}, u32[]{:S(2)}, u32[]{:S(2)}) %collective-permute-start.32) | collective-permute-done | bytes 196640 | tf_op jit(solution)/shard_map/both_exchange2/ppermute | solution.py:563
  156.0 1.6 collective-permute-start.34
  157.6 1.5 collective-permute-start.35
  159.2 5.0 %collective-permute-done.33 = bf16[96,1024]{1,0:T(8,128)(2,1)S(1)} collective-permute-done((bf16[96,1024]{1,0:T(8,128)(2,1)S(1)}, bf16[96,1024]{1,0:T(8,128)(2,1)S(1)}, u32[]{:S(2)}, u32[]{:S(2)}) %collective-permute-start.33) | collective-permute-done | bytes 196640 | tf_op jit(solution)/shard_map/both_gather2_0/ppermute | solution.py:563
  164.2 1.5 collective-permute-start.29
  165.8 5.2 %collective-permute-done.29 = bf16[192,512]{1,0:T(8,128)(2,1)S(1)} collective-permute-done((bf16[192,512]{1,0:T(8,128)(2,1)S(1)}, bf16[192,512]{1,0:T(8,128)(2,1)S(1)}, u32[]{:S(2)}, u32[]{:S(2)}) %collective-permute-start.29) | collective-permute-done | bytes 196640 | tf_op jit(solution)/shard_map/last_send1_0/ppermute | solution.py:563
  171.1 1.6 collective-permute-start.38
  175.1 3.1 %collective-permute-done.41 = f32[54,128]{1,0:T(8,128)S(1)} collective-permute-done((f32[54,128]{1,0:T(8,128)S(1)}, f32[54,128]{1,0:T(8,128)S(1)}, u32[]{:S(2)}, u32[]{:S(2)}) %collective-permute-start.41) | collective-permute-done | bytes 27680 | tf_op jit(solution)/shard_map/small0/ppermute | solution.py:563
  178.7 3.6 %collective-permute-done.42 = f32[54,128]{1,0:T(8,128)S(1)} collective-permute-done((f32[54,128]{1,0:T(8,128)S(1)}, f32[54,128]{1,0:T(8,128)S(1)}, u32[]{:S(2)}, u32[]{:S(2)}) %collective-permute-start.42) | collective-permute-done | bytes 27680 | tf_op jit(solution)/shard_map/small1/ppermute | solution.py:563
  182.7 1.7 collective-permute-start.43
  184.9 1.7 collective-permute-start.44
  186.6 12.8 %collective-permute-done.44 = f32[54,128]{1,0:T(8,128)S(1)} collective-permute-done((f32[54,128]{1,0:T(8,128)S(1)}, f32[54,128]{1,0:T(8,128)S(1)}, u32[]{:S(2)}, u32[]{:S(2)}) %collective-permute-start.44) | collective-permute-done | bytes 27680 | tf_op jit(solution)/shard_map/small2/ppermute | solution.py:563
  201.0 1.5 collective-permute-start.46
  203.2 8.3 %collective-permute-done.52 = bf16[192,1024]{1,0:T(8,128)(2,1)S(1)} collective-permute-done((bf16[192,1024]{1,0:T(8,128)(2,1)S(1)}, bf16[192,1024]{1,0:T(8,128)(2,1)S(1)}, u32[]{:S(2)}, u32[]{:S(2)}) %collective-permute-start.52) | collective-permute-done | bytes 393248 | tf_op jit(solution)/shard_map/both_gather1_2/ppermute | solution.py:563
  216.0 10.4 %collective-permute-done.47 = bf16[96,512]{1,0:T(8,128)(2,1)S(1)} collective-permute-done((bf16[96,512]{1,0:T(8,128)(2,1)S(1)}, bf16[96,512]{1,0:T(8,128)(2,1)S(1)}, u32[]{:S(2)}, u32[]{:S(2)}) %collective-permute-start.47) | collective-permute-done | bytes 98336 | tf_op jit(solution)/shard_map/last_gather2_2/ppermute | solution.py:563
  228.6 4.6 %collective-permute-done.54 = bf16[192,512]{1,0:T(8,128)(2,1)S(1)} collective-permute-done((bf16[192,512]{1,0:T(8,128)(2,1)S(1)}, bf16[192,512]{1,0:T(8,128)(2,1)S(1)}, u32[]{:S(2)}, u32[]{:S(2)}) %collective-permute-start.54) | collective-permute-done | bytes 196640 | tf_op jit(solution)/shard_map/last_gather1_0/ppermute | solution.py:563
  233.7 2.3 collective-permute-start.60
  235.9 6.0 %shard_map.324 = (f32[1536,768]{1,0:T(8,128)}, f32[768,1536]{1,0:T(8,128)}) custom-call(bf16[768,1024]{1,0:T(8,128)(2,1)S(1)} %constant_dynamic-update-slice_fusion.6.a_ref, bf16[768,1024]{1,0:T(8,128)(2,1)S(1)} %constant_dynamic-update-slice_fusion.9.b_ref, bf16[768,1024]{1,0:T(8,128)(2,1)S(1)} %constant_dynamic-update-slice_fusion.12.c_ref, ...), custom_call_target="tpu_custom_call" | custom-call | flops 5750000128 | tf_op jit(solution)/shard_map/pallas_call | solution.py:62
  242.9 2.0 collective-permute-start.57
  247.5 2.2 collective-permute-done.59
  250.7 2.0 collective-permute-done.55
  252.7 3.1 %shard_map.323 = (f32[768,384]{1,0:T(8,128)}, f32[768,384]{1,0:T(8,128)}, f32[768,384]{1,0:T(8,128)}, f32[384,768]{1,0:T(8,128)}) custom-call(bf16[768,512]{1,0:T(8,128)(2,1)S(1)} %pad_maximum_fusion.3.a_ref, bf16[768,512]{1,0:T(8,128)(2,1)S(1)} %pad_maximum_fusion.4.b_ref, bf16[768,512]{1,0:T(8,128)(2,1)S(1)} %pad_maximum_fusion.5.c_ref, s32[3,16]{1,0:T(4,128)S(1)} %copy-done), custom_call_target="tpu_custom_call" | custom-call | flops 5750000128 | tf_op jit(solution)/shard_map/pallas_call | solution.py:62
  (218 shorter events, 35.0 us)
Async XLA Ops:
  1.2 22.0 %collective-permute-start.5 = (bf16[768,1536]{1,0:T(8,128)(2,1)}, bf16[768,1536]{1,0:T(8,128)(2,1)}, u32[]{:S(2)}, u32[]{:S(2)}) collective-permute-start(bf16[768,1536]{1,0:T(8,128)(2,1)} %wu_a.3), channel_id=1, source_target_pairs={{0,1},{1,0},{2,3},{3,2},{4,5},{5,4},{6,7},{7,6},{8,9},{9,8},{10,11... | collective-permute-start | bytes 7077896 | tf_op jit(solution)/shard_map/ppermute | solution.py:567
  1.3 21.9 %collective-permute-start.6 = (bf16[1536,768]{1,0:T(8,128)(2,1)}, bf16[1536,768]{1,0:T(8,128)(2,1)}, u32[]{:S(2)}, u32[]{:S(2)}) collective-permute-start(bf16[1536,768]{1,0:T(8,128)(2,1)} %wd_a.3), channel_id=1, source_target_pairs={{0,1},{1,0},{2,3},{3,2},{4,5},{5,4},{6,7},{7,6},{8,9},{9,8},{10,11... | collective-permute-start | bytes 7077896 | tf_op jit(solution)/shard_map/ppermute | solution.py:567
  1.8 21.2 %collective-permute-start.3 = (bf16[384,768]{1,0:T(8,128)(2,1)}, bf16[384,768]{1,0:T(8,128)(2,1)S(1)}, u32[]{:S(2)}, u32[]{:S(2)}) collective-permute-start(bf16[384,768]{1,0:T(8,128)(2,1)} %wo_a.3), channel_id=1, source_target_pairs={{0,1},{1,0},{2,3},{3,2},{4,5},{5,4},{6,7},{7,6},{8,9},{9,8},{10,11... | collective-permute-start | bytes 1769480 | tf_op jit(solution)/shard_map/ppermute | solution.py:567
  47.1 13.9 %collective-permute-start.7 = (bf16[3,768,512]{2,1,0:T(8,128)(2,1)}, bf16[3,768,512]{2,1,0:T(8,128)(2,1)S(1)}, u32[]{:S(2)}, u32[]{:S(2)}) collective-permute-start(bf16[3,768,512]{2,1,0:T(8,128)(2,1)} %get-tuple-element.150), channel_id=1, source_target_pairs={{0,1},{1,0},{2,3},{3,2},{4,5},{5,4},{6,7},{7,6},{8,9},{9,8},{10,11... | collective-permute-start | bytes 7077896 | tf_op jit(solution)/shard_map/ppermute | solution.py:567
  60.8 8.8 %collective-permute-start.8 = (bf16[3,768,512]{2,1,0:T(8,128)(2,1)}, bf16[3,768,512]{2,1,0:T(8,128)(2,1)S(1)}, u32[]{:S(2)}, u32[]{:S(2)}) collective-permute-start(bf16[3,768,512]{2,1,0:T(8,128)(2,1)} %get-tuple-element.153), channel_id=1, source_target_pairs={{0,1},{1,0},{2,3},{3,2},{4,5},{5,4},{6,7},{7,6},{8,9},{9,8},{10,11... | collective-permute-start | bytes 7077896 | tf_op jit(solution)/shard_map/ppermute | solution.py:567
  63.5 12.9 %collective-permute-start.13 = (bf16[384,512]{1,0:T(8,128)(2,1)S(1)}, bf16[384,512]{1,0:T(8,128)(2,1)S(1)}, u32[]{:S(2)}, u32[]{:S(2)}) collective-permute-start(bf16[384,512]{1,0:T(8,128)(2,1)S(1)} %get-tuple-element.260), channel_id=1, source_target_pairs={{0,8},{2,10},{4,12},{6,14},{8,0},{10,2},{12,4},{14,6},{16,24},{18,... | collective-permute-start | bytes 1179656 | tf_op jit(solution)/shard_map/down_send0_2/ppermute | solution.py:563
  66.5 22.6 %collective-permute-start.12 = (bf16[384,512]{1,0:T(8,128)(2,1)S(1)}, bf16[384,512]{1,0:T(8,128)(2,1)S(1)}, u32[]{:S(2)}, u32[]{:S(2)}) collective-permute-start(bf16[384,512]{1,0:T(8,128)(2,1)S(1)} %get-tuple-element.261), channel_id=1, source_target_pairs={{0,4},{2,6},{4,0},{6,2},{8,12},{10,14},{12,8},{14,10},{16,20},{18,... | collective-permute-start | bytes 1179656 | tf_op jit(solution)/shard_map/down_send0_1/ppermute | solution.py:563
  68.0 21.2 %collective-permute-start.11 = (bf16[384,512]{1,0:T(8,128)(2,1)S(1)}, bf16[384,512]{1,0:T(8,128)(2,1)S(1)}, u32[]{:S(2)}, u32[]{:S(2)}) collective-permute-start(bf16[384,512]{1,0:T(8,128)(2,1)S(1)} %get-tuple-element.262), channel_id=1, source_target_pairs={{0,2},{2,0},{4,6},{6,4},{8,10},{10,8},{12,14},{14,12},{16,18},{18,... | collective-permute-start | bytes 1179656 | tf_op jit(solution)/shard_map/down_send0_0/ppermute | solution.py:563
  70.3 19.4 %collective-permute-start.16 = (bf16[384,512]{1,0:T(8,128)(2,1)S(1)}, bf16[384,512]{1,0:T(8,128)(2,1)S(1)}, u32[]{:S(2)}, u32[]{:S(2)}) collective-permute-start(bf16[384,512]{1,0:T(8,128)(2,1)S(1)} %get-tuple-element.266), channel_id=1, source_target_pairs={{0,8},{2,10},{4,12},{6,14},{8,0},{10,2},{12,4},{14,6},{16,24},{18,... | collective-permute-start | bytes 1179656 | tf_op jit(solution)/shard_map/up_send0_2/ppermute | solution.py:563
  70.8 18.9 %collective-permute-start.15 = (bf16[384,512]{1,0:T(8,128)(2,1)S(1)}, bf16[384,512]{1,0:T(8,128)(2,1)S(1)}, u32[]{:S(2)}, u32[]{:S(2)}) collective-permute-start(bf16[384,512]{1,0:T(8,128)(2,1)S(1)} %get-tuple-element.267), channel_id=1, source_target_pairs={{0,4},{2,6},{4,0},{6,2},{8,12},{10,14},{12,8},{14,10},{16,20},{18,... | collective-permute-start | bytes 1179656 | tf_op jit(solution)/shard_map/up_send0_1/ppermute | solution.py:563
  76.4 13.3 %collective-permute-start.14 = (bf16[384,512]{1,0:T(8,128)(2,1)S(1)}, bf16[384,512]{1,0:T(8,128)(2,1)S(1)}, u32[]{:S(2)}, u32[]{:S(2)}) collective-permute-start(bf16[384,512]{1,0:T(8,128)(2,1)S(1)} %get-tuple-element.268), channel_id=1, source_target_pairs={{0,2},{2,0},{4,6},{6,4},{8,10},{10,8},{12,14},{14,12},{16,18},{18,... | collective-permute-start | bytes 1179656 | tf_op jit(solution)/shard_map/up_send0_0/ppermute | solution.py:563
  89.2 35.4 %collective-permute-start.9 = (bf16[3,768,128]{2,1,0:T(8,128)(2,1)S(1)}, bf16[3,768,128]{2,1,0:T(8,128)(2,1)S(1)}, u32[]{:S(2)}, u32[]{:S(2)}) collective-permute-start(bf16[3,768,128]{2,1,0:T(8,128)(2,1)S(1)} %get-tuple-element.156), channel_id=1, source_target_pairs={{0,1},{1,0},{2,3},{3,2},{4,5},{5,4},{6,7},{7,6},{8,9},{9,8},{10,11... | collective-permute-start | bytes 1769480 | tf_op jit(solution)/shard_map/ppermute | solution.py:567
  90.0 11.3 %collective-permute-start.19 = (bf16[192,1024]{1,0:T(8,128)(2,1)S(1)}, bf16[192,1024]{1,0:T(8,128)(2,1)S(1)}, u32[]{:S(2)}, u32[]{:S(2)}) collective-permute-start(bf16[192,1024]{1,0:T(8,128)(2,1)S(1)} %pad_maximum_fusion.8), channel_id=1, source_target_pairs={{0,2},{2,0},{4,6},{6,4},{8,10},{10,8},{12,14},{14,12},{16,18},{18,... | collective-permute-start | bytes 1179656 | tf_op jit(solution)/shard_map/both_send1_2/ppermute | solution.py:563
  90.4 11.2 %collective-permute-start.18 = (bf16[192,1024]{1,0:T(8,128)(2,1)S(1)}, bf16[192,1024]{1,0:T(8,128)(2,1)S(1)}, u32[]{:S(2)}, u32[]{:S(2)}) collective-permute-start(bf16[192,1024]{1,0:T(8,128)(2,1)S(1)} %pad_maximum_fusion.7), channel_id=1, source_target_pairs={{0,8},{2,10},{4,12},{6,14},{8,0},{10,2},{12,4},{14,6},{16,24},{18,... | collective-permute-start | bytes 1179656 | tf_op jit(solution)/shard_map/both_send1_1/ppermute | solution.py:563
  92.9 10.6 %collective-permute-start.17 = (bf16[192,1024]{1,0:T(8,128)(2,1)S(1)}, bf16[192,1024]{1,0:T(8,128)(2,1)S(1)}, u32[]{:S(2)}, u32[]{:S(2)}) collective-permute-start(bf16[192,1024]{1,0:T(8,128)(2,1)S(1)} %pad_maximum_fusion.6), channel_id=1, source_target_pairs={{0,4},{2,6},{4,0},{6,2},{8,12},{10,14},{12,8},{14,10},{16,20},{18,... | collective-permute-start | bytes 1179656 | tf_op jit(solution)/shard_map/both_send1_0/ppermute | solution.py:563
  103.6 10.7 %collective-permute-start.22 = (bf16[96,1024]{1,0:T(8,128)(2,1)S(1)}, bf16[96,1024]{1,0:T(8,128)(2,1)S(1)}, u32[]{:S(2)}, u32[]{:S(2)}) collective-permute-start(bf16[96,1024]{1,0:T(8,128)(2,1)S(1)} %get-tuple-element.283), channel_id=1, source_target_pairs={{0,4},{2,6},{4,0},{6,2},{8,12},{10,14},{12,8},{14,10},{16,20},{18,... | collective-permute-start | bytes 589832 | tf_op jit(solution)/shard_map/both_send2_2/ppermute | solution.py:563
  105.3 9.0 %collective-permute-start.21 = (bf16[96,1024]{1,0:T(8,128)(2,1)S(1)}, bf16[96,1024]{1,0:T(8,128)(2,1)S(1)}, u32[]{:S(2)}, u32[]{:S(2)}) collective-permute-start(bf16[96,1024]{1,0:T(8,128)(2,1)S(1)} %get-tuple-element.285), channel_id=1, source_target_pairs={{0,2},{2,0},{4,6},{6,4},{8,10},{10,8},{12,14},{14,12},{16,18},{18,... | collective-permute-start | bytes 589832 | tf_op jit(solution)/shard_map/both_send2_1/ppermute | solution.py:563
  107.0 7.4 %collective-permute-start.20 = (bf16[96,1024]{1,0:T(8,128)(2,1)S(1)}, bf16[96,1024]{1,0:T(8,128)(2,1)S(1)}, u32[]{:S(2)}, u32[]{:S(2)}) collective-permute-start(bf16[96,1024]{1,0:T(8,128)(2,1)S(1)} %get-tuple-element.287), channel_id=1, source_target_pairs={{0,8},{2,10},{4,12},{6,14},{8,0},{10,2},{12,4},{14,6},{16,24},{18,... | collective-permute-start | bytes 589832 | tf_op jit(solution)/shard_map/both_send2_0/ppermute | solution.py:563
  114.4 9.8 %collective-permute-start.23 = (bf16[96,1024]{1,0:T(8,128)(2,1)S(1)}, bf16[96,1024]{1,0:T(8,128)(2,1)S(1)}, u32[]{:S(2)}, u32[]{:S(2)}) collective-permute-start(bf16[96,1024]{1,0:T(8,128)(2,1)S(1)} %add_convert_fusion.19), channel_id=1, source_target_pairs={{0,16},{2,18},{4,20},{6,22},{8,24},{10,26},{12,28},{14,30},{16,0},... | collective-permute-start | bytes 589832 | tf_op jit(solution)/shard_map/both_exchange0/ppermute | solution.py:563
  124.3 14.2 %collective-permute-start.24 = (bf16[96,1024]{1,0:T(8,128)(2,1)S(1)}, bf16[96,1024]{1,0:T(8,128)(2,1)S(1)}, u32[]{:S(2)}, u32[]{:S(2)}) collective-permute-start(bf16[96,1024]{1,0:T(8,128)(2,1)S(1)} %add_convert_fusion.17), channel_id=1, source_target_pairs={{0,16},{2,18},{4,20},{6,22},{8,24},{10,26},{12,28},{14,30},{16,0},... | collective-permute-start | bytes 589832 | tf_op jit(solution)/shard_map/both_exchange1/ppermute | solution.py:563
  133.1 13.5 %collective-permute-start.28 = (bf16[384,512]{1,0:T(8,128)(2,1)}, bf16[384,512]{1,0:T(8,128)(2,1)S(1)}, u32[]{:S(2)}, u32[]{:S(2)}) collective-permute-start(bf16[384,512]{1,0:T(8,128)(2,1)} %get-tuple-element.279), channel_id=1, source_target_pairs={{0,8},{2,10},{4,12},{6,14},{8,0},{10,2},{12,4},{14,6},{16,24},{18,... | collective-permute-start | bytes 1179656 | tf_op jit(solution)/shard_map/last_send0_2/ppermute | solution.py:563
  136.9 9.8 %collective-permute-start.27 = (bf16[384,512]{1,0:T(8,128)(2,1)}, bf16[384,512]{1,0:T(8,128)(2,1)}, u32[]{:S(2)}, u32[]{:S(2)}) collective-permute-start(bf16[384,512]{1,0:T(8,128)(2,1)} %get-tuple-element.280), channel_id=1, source_target_pairs={{0,4},{2,6},{4,0},{6,2},{8,12},{10,14},{12,8},{14,10},{16,20},{18,... | collective-permute-start | bytes 1179656 | tf_op jit(solution)/shard_map/last_send0_1/ppermute | solution.py:563
  137.4 9.3 %collective-permute-start.26 = (bf16[384,512]{1,0:T(8,128)(2,1)}, bf16[384,512]{1,0:T(8,128)(2,1)}, u32[]{:S(2)}, u32[]{:S(2)}) collective-permute-start(bf16[384,512]{1,0:T(8,128)(2,1)} %get-tuple-element.281), channel_id=1, source_target_pairs={{0,2},{2,0},{4,6},{6,4},{8,10},{10,8},{12,14},{14,12},{16,18},{18,... | collective-permute-start | bytes 1179656 | tf_op jit(solution)/shard_map/last_send0_0/ppermute | solution.py:563
  144.3 11.6 %collective-permute-start.32 = (bf16[96,1024]{1,0:T(8,128)(2,1)S(1)}, bf16[96,1024]{1,0:T(8,128)(2,1)S(1)}, u32[]{:S(2)}, u32[]{:S(2)}) collective-permute-start(bf16[96,1024]{1,0:T(8,128)(2,1)S(1)} %add_convert_fusion.15), channel_id=1, source_target_pairs={{0,16},{2,18},{4,20},{6,22},{8,24},{10,26},{12,28},{14,30},{16,0},... | collective-permute-start | bytes 589832 | tf_op jit(solution)/shard_map/both_exchange2/ppermute | solution.py:563
  148.6 17.3 %collective-permute-start.31 = (bf16[192,512]{1,0:T(8,128)(2,1)S(1)}, bf16[192,512]{1,0:T(8,128)(2,1)S(1)}, u32[]{:S(2)}, u32[]{:S(2)}) collective-permute-start(bf16[192,512]{1,0:T(8,128)(2,1)S(1)} %get-tuple-element.270), channel_id=1, source_target_pairs={{0,2},{2,0},{4,6},{6,4},{8,10},{10,8},{12,14},{14,12},{16,18},{18,... | collective-permute-start | bytes 589832 | tf_op jit(solution)/shard_map/last_send1_2/ppermute | solution.py:563
  150.0 15.8 %collective-permute-start.30 = (bf16[192,512]{1,0:T(8,128)(2,1)S(1)}, bf16[192,512]{1,0:T(8,128)(2,1)S(1)}, u32[]{:S(2)}, u32[]{:S(2)}) collective-permute-start(bf16[192,512]{1,0:T(8,128)(2,1)S(1)} %get-tuple-element.275), channel_id=1, source_target_pairs={{0,8},{2,10},{4,12},{6,14},{8,0},{10,2},{12,4},{14,6},{16,24},{18,... | collective-permute-start | bytes 589832 | tf_op jit(solution)/shard_map/last_send1_1/ppermute | solution.py:563
  155.9 8.3 %collective-permute-start.33 = (bf16[96,1024]{1,0:T(8,128)(2,1)S(1)}, bf16[96,1024]{1,0:T(8,128)(2,1)S(1)}, u32[]{:S(2)}, u32[]{:S(2)}) collective-permute-start(bf16[96,1024]{1,0:T(8,128)(2,1)S(1)} %add_convert_fusion.18), channel_id=1, source_target_pairs={{0,8},{2,10},{4,12},{6,14},{8,0},{10,2},{12,4},{14,6},{16,24},{18,... | collective-permute-start | bytes 589832 | tf_op jit(solution)/shard_map/both_gather2_0/ppermute | solution.py:563
  156.0 9.7 %collective-permute-start.34 = (bf16[96,1024]{1,0:T(8,128)(2,1)S(1)}, bf16[96,1024]{1,0:T(8,128)(2,1)S(1)}, u32[]{:S(2)}, u32[]{:S(2)}) collective-permute-start(bf16[96,1024]{1,0:T(8,128)(2,1)S(1)} %add_convert_fusion.16), channel_id=1, source_target_pairs={{0,2},{2,0},{4,6},{6,4},{8,10},{10,8},{12,14},{14,12},{16,18},{18,... | collective-permute-start | bytes 589832 | tf_op jit(solution)/shard_map/both_gather2_1/ppermute | solution.py:563
  157.6 8.2 %collective-permute-start.35 = (bf16[96,1024]{1,0:T(8,128)(2,1)S(1)}, bf16[96,1024]{1,0:T(8,128)(2,1)S(1)}, u32[]{:S(2)}, u32[]{:S(2)}) collective-permute-start(bf16[96,1024]{1,0:T(8,128)(2,1)S(1)} %add_convert_fusion.14), channel_id=1, source_target_pairs={{0,4},{2,6},{4,0},{6,2},{8,12},{10,14},{12,8},{14,10},{16,20},{18,... | collective-permute-start | bytes 589832 | tf_op jit(solution)/shard_map/both_gather2_2/ppermute | solution.py:563
  171.1 11.5 %collective-permute-start.38 = (bf16[96,512]{1,0:T(8,128)(2,1)S(1)}, bf16[96,512]{1,0:T(8,128)(2,1)S(1)}, u32[]{:S(2)}, u32[]{:S(2)}) collective-permute-start(bf16[96,512]{1,0:T(8,128)(2,1)S(1)} %get-tuple-element.300), channel_id=1, source_target_pairs={{0,4},{2,6},{4,0},{6,2},{8,12},{10,14},{12,8},{14,10},{16,20},{18,... | collective-permute-start | bytes 294920 | tf_op jit(solution)/shard_map/last_send2_2/ppermute | solution.py:563
  172.7 9.8 %collective-permute-start.37 = (bf16[96,512]{1,0:T(8,128)(2,1)S(1)}, bf16[96,512]{1,0:T(8,128)(2,1)S(1)}, u32[]{:S(2)}, u32[]{:S(2)}) collective-permute-start(bf16[96,512]{1,0:T(8,128)(2,1)S(1)} %get-tuple-element.302), channel_id=1, source_target_pairs={{0,2},{2,0},{4,6},{6,4},{8,10},{10,8},{12,14},{14,12},{16,18},{18,... | collective-permute-start | bytes 294920 | tf_op jit(solution)/shard_map/last_send2_1/ppermute | solution.py:563
  174.1 8.5 %collective-permute-start.36 = (bf16[96,512]{1,0:T(8,128)(2,1)S(1)}, bf16[96,512]{1,0:T(8,128)(2,1)S(1)}, u32[]{:S(2)}, u32[]{:S(2)}) collective-permute-start(bf16[96,512]{1,0:T(8,128)(2,1)S(1)} %get-tuple-element.304), channel_id=1, source_target_pairs={{0,8},{2,10},{4,12},{6,14},{8,0},{10,2},{12,4},{14,6},{16,24},{18,... | collective-permute-start | bytes 294920 | tf_op jit(solution)/shard_map/last_send2_0/ppermute | solution.py:563
  178.7 34.3 %collective-permute-start.25 = (bf16[512,768]{1,0:T(8,128)(2,1)S(1)}, bf16[512,768]{1,0:T(8,128)(2,1)S(1)}, u32[]{:S(2)}, u32[]{:S(2)}) collective-permute-start(bf16[512,768]{1,0:T(8,128)(2,1)S(1)} %get-tuple-element.210), channel_id=1, source_target_pairs={{0,1},{1,0},{2,3},{3,2},{4,5},{5,4},{6,7},{7,6},{8,9},{9,8},{10,11... | collective-permute-start | bytes 2359304 | tf_op jit(solution)/shard_map/ppermute | solution.py:567
  182.3 18.7 %collective-permute-start.48 = (bf16[192,1024]{1,0:T(8,128)(2,1)S(1)}, bf16[192,1024]{1,0:T(8,128)(2,1)S(1)}, u32[]{:S(2)}, u32[]{:S(2)}) collective-permute-start(bf16[192,1024]{1,0:T(8,128)(2,1)S(1)} %constant_dynamic-update-slice_fusion), channel_id=1, source_target_pairs={{0,4},{2,6},{4,0},{6,2},{8,12},{10,14},{12,8},{14,10},{16,20},{18,... | collective-permute-start | bytes 1179656 | tf_op jit(solution)/shard_map/both_gather1_0/ppermute | solution.py:563
  182.7 17.6 %collective-permute-start.43 = (bf16[288,512]{1,0:T(8,128)(2,1)S(1)}, bf16[288,512]{1,0:T(8,128)(2,1)S(1)}, u32[]{:S(2)}, u32[]{:S(2)}) collective-permute-start(bf16[288,512]{1,0:T(8,128)(2,1)S(1)} %add_convert_fusion.13), channel_id=1, source_target_pairs={{0,16},{2,18},{4,20},{6,22},{8,24},{10,26},{12,28},{14,30},{16,0},... | collective-permute-start | bytes 884744 | tf_op jit(solution)/shard_map/last_exchange/ppermute | solution.py:563
  184.4 18.1 %collective-permute-start.50 = (bf16[192,1024]{1,0:T(8,128)(2,1)S(1)}, bf16[192,1024]{1,0:T(8,128)(2,1)S(1)}, u32[]{:S(2)}, u32[]{:S(2)}) collective-permute-start(bf16[192,1024]{1,0:T(8,128)(2,1)S(1)} %constant_dynamic-update-slice_fusion.2), channel_id=1, source_target_pairs={{0,8},{2,10},{4,12},{6,14},{8,0},{10,2},{12,4},{14,6},{16,24},{18,... | collective-permute-start | bytes 1179656 | tf_op jit(solution)/shard_map/both_gather1_1/ppermute | solution.py:563
  184.9 14.6 %collective-permute-start.44 = (f32[54,128]{1,0:T(8,128)S(1)}, f32[54,128]{1,0:T(8,128)S(1)}, u32[]{:S(2)}, u32[]{:S(2)}) collective-permute-start(f32[54,128]{1,0:T(8,128)S(1)} %add.235), channel_id=1, source_target_pairs={{0,8},{2,10},{4,12},{6,14},{8,0},{10,2},{12,4},{14,6},{16,24},{18,... | collective-permute-start | bytes 82952 | tf_op jit(solution)/shard_map/small2/ppermute | solution.py:563
  199.5 12.1 %collective-permute-start.52 = (bf16[192,1024]{1,0:T(8,128)(2,1)S(1)}, bf16[192,1024]{1,0:T(8,128)(2,1)S(1)}, u32[]{:S(2)}, u32[]{:S(2)}) collective-permute-start(bf16[192,1024]{1,0:T(8,128)(2,1)S(1)} %constant_dynamic-update-slice_fusion.4), channel_id=1, source_target_pairs={{0,2},{2,0},{4,6},{6,4},{8,10},{10,8},{12,14},{14,12},{16,18},{18,... | collective-permute-start | bytes 1179656 | tf_op jit(solution)/shard_map/both_gather1_2/ppermute | solution.py:563
  200.4 14.4 %collective-permute-start.45 = (bf16[96,512]{1,0:T(8,128)(2,1)S(1)}, bf16[96,512]{1,0:T(8,128)(2,1)S(1)}, u32[]{:S(2)}, u32[]{:S(2)}) collective-permute-start(bf16[96,512]{1,0:T(8,128)(2,1)S(1)} %get-tuple-element.237), channel_id=1, source_target_pairs={{0,8},{2,10},{4,12},{6,14},{8,0},{10,2},{12,4},{14,6},{16,24},{18,... | collective-permute-start | bytes 294920 | tf_op jit(solution)/shard_map/last_gather2_0/ppermute | solution.py:563
  201.0 15.0 %collective-permute-start.46 = (bf16[96,512]{1,0:T(8,128)(2,1)S(1)}, bf16[96,512]{1,0:T(8,128)(2,1)S(1)}, u32[]{:S(2)}, u32[]{:S(2)}) collective-permute-start(bf16[96,512]{1,0:T(8,128)(2,1)S(1)} %get-tuple-element.238), channel_id=1, source_target_pairs={{0,2},{2,0},{4,6},{6,4},{8,10},{10,8},{12,14},{14,12},{16,18},{18,... | collective-permute-start | bytes 294920 | tf_op jit(solution)/shard_map/last_gather2_1/ppermute | solution.py:563
  202.5 24.7 %collective-permute-start.49 = (bf16[384,1024]{1,0:T(8,128)(2,1)S(1)}, bf16[384,1024]{1,0:T(8,128)(2,1)S(1)}, u32[]{:S(2)}, u32[]{:S(2)}) collective-permute-start(bf16[384,1024]{1,0:T(8,128)(2,1)S(1)} %pad_maximum_fusion), channel_id=1, source_target_pairs={{0,2},{2,0},{4,6},{6,4},{8,10},{10,8},{12,14},{14,12},{16,18},{18,... | collective-permute-start | bytes 2359304 | tf_op jit(solution)/shard_map/both_gather0_0/ppermute | solution.py:563
  211.5 15.8 %collective-permute-start.51 = (bf16[384,1024]{1,0:T(8,128)(2,1)S(1)}, bf16[384,1024]{1,0:T(8,128)(2,1)S(1)}, u32[]{:S(2)}, u32[]{:S(2)}) collective-permute-start(bf16[384,1024]{1,0:T(8,128)(2,1)S(1)} %pad_maximum_fusion.1), channel_id=1, source_target_pairs={{0,4},{2,6},{4,0},{6,2},{8,12},{10,14},{12,8},{14,10},{16,20},{18,... | collective-permute-start | bytes 2359304 | tf_op jit(solution)/shard_map/both_gather0_1/ppermute | solution.py:563
  212.9 14.5 %collective-permute-start.53 = (bf16[384,1024]{1,0:T(8,128)(2,1)S(1)}, bf16[384,1024]{1,0:T(8,128)(2,1)S(1)}, u32[]{:S(2)}, u32[]{:S(2)}) collective-permute-start(bf16[384,1024]{1,0:T(8,128)(2,1)S(1)} %pad_maximum_fusion.2), channel_id=1, source_target_pairs={{0,8},{2,10},{4,12},{6,14},{8,0},{10,2},{12,4},{14,6},{16,24},{18,... | collective-permute-start | bytes 2359304 | tf_op jit(solution)/shard_map/both_gather0_2/ppermute | solution.py:563
  214.8 11.6 %collective-permute-start.47 = (bf16[96,512]{1,0:T(8,128)(2,1)S(1)}, bf16[96,512]{1,0:T(8,128)(2,1)S(1)}, u32[]{:S(2)}, u32[]{:S(2)}) collective-permute-start(bf16[96,512]{1,0:T(8,128)(2,1)S(1)} %get-tuple-element.239), channel_id=1, source_target_pairs={{0,4},{2,6},{4,0},{6,2},{8,12},{10,14},{12,8},{14,10},{16,20},{18,... | collective-permute-start | bytes 294920 | tf_op jit(solution)/shard_map/last_gather2_2/ppermute | solution.py:563
  233.7 12.0 %collective-permute-start.60 = (f32[54,128]{1,0:T(8,128)S(1)}, f32[54,128]{1,0:T(8,128)S(1)}, u32[]{:S(2)}, u32[]{:S(2)}) collective-permute-start(f32[54,128]{1,0:T(8,128)S(1)} %add.238), channel_id=1, source_target_pairs={{0,16},{2,18},{4,20},{6,22},{8,24},{10,26},{12,28},{14,30},{16,0},... | collective-permute-start | bytes 82952 | tf_op jit(solution)/shard_map/small3/ppermute | solution.py:563
  241.9 7.8 %collective-permute-start.59 = (bf16[384,512]{1,0:T(8,128)(2,1)S(1)}, bf16[384,512]{1,0:T(8,128)(2,1)S(1)}, u32[]{:S(2)}, u32[]{:S(2)}) collective-permute-start(bf16[384,512]{1,0:T(8,128)(2,1)S(1)} %constant_dynamic-update-slice_fusion.19), channel_id=1, source_target_pairs={{0,8},{2,10},{4,12},{6,14},{8,0},{10,2},{12,4},{14,6},{16,24},{18,... | collective-permute-start | bytes 1179656 | tf_op jit(solution)/shard_map/last_gather0_2/ppermute | solution.py:563
  242.9 7.8 %collective-permute-start.57 = (bf16[384,512]{1,0:T(8,128)(2,1)S(1)}, bf16[384,512]{1,0:T(8,128)(2,1)S(1)}, u32[]{:S(2)}, u32[]{:S(2)}) collective-permute-start(bf16[384,512]{1,0:T(8,128)(2,1)S(1)} %constant_dynamic-update-slice_fusion.17), channel_id=1, source_target_pairs={{0,4},{2,6},{4,0},{6,2},{8,12},{10,14},{12,8},{14,10},{16,20},{18,... | collective-permute-start | bytes 1179656 | tf_op jit(solution)/shard_map/last_gather0_1/ppermute | solution.py:563
  244.9 7.8 %collective-permute-start.55 = (bf16[384,512]{1,0:T(8,128)(2,1)S(1)}, bf16[384,512]{1,0:T(8,128)(2,1)S(1)}, u32[]{:S(2)}, u32[]{:S(2)}) collective-permute-start(bf16[384,512]{1,0:T(8,128)(2,1)S(1)} %constant_dynamic-update-slice_fusion.15), channel_id=1, source_target_pairs={{0,2},{2,0},{4,6},{6,4},{8,10},{10,8},{12,14},{14,12},{16,18},{18,... | collective-permute-start | bytes 1179656 | tf_op jit(solution)/shard_map/last_gather0_0/ppermute | solution.py:563
  (43 other events, 239.0 us)

commit v3 on v2

v3 whole, which is shorter than its diff:
```python
from functools import partial

import jax
import jax.numpy as jnp
from jax import lax
from jax.experimental import pallas as pl
from jax.experimental.pallas import tpu as pltpu
from jax.sharding import PartitionSpec as P

HD = 64
LEN = 1024
EPSILON = 1e-05
MASKED = -1e30
SCALE = HD**-0.5
BLOCKS = 16
PAIR = 2 * HD
MIB = 1 << 20

F32 = jnp.float32
BF16 = jnp.bfloat16


def nn(left, right):
    return lax.dot_general(left, right, (((1,), (0,)), ((), ())), preferred_element_type=F32)


def nt(left, right):
    return lax.dot_general(left, right, (((1,), (1,)), ((), ())), preferred_element_type=F32)


def tn(left, right):
    return lax.dot_general(left, right, (((0,), (0,)), ((), ())), preferred_element_type=F32)


def normalize_parts(hidden):
    average = jnp.mean(hidden, axis=-1, keepdims=True)
    centred = hidden - average
    spread = jnp.mean(centred * centred, axis=-1, keepdims=True)
    inverse = lax.rsqrt(spread + EPSILON)
    return centred * inverse, inverse


def normalize_back(grad_out, normed, inverse, gain):
    scaled = grad_out * gain
    first_mean = jnp.mean(scaled, axis=-1, keepdims=True)
    second_mean = jnp.mean(scaled * normed, axis=-1, keepdims=True)
    return inverse * (scaled - first_mean - normed * second_mean)


def gelu_parts(upper):
    phi = 0.5 + 0.5 * lax.erf(upper * 0.5**0.5)
    bell = jnp.exp(upper * upper * -0.5)
    return upper * phi, phi + upper * bell * 0.3989422804014327


def lasting(us):
    return pl.CostEstimate(flops=int(us * 1.15e9), bytes_accessed=0, transcendentals=0)


def call(kernel, outs, ins, scratch=(), limit=48, smem=(), hbm=(), hbm_outs=(), us=5):
    place = lambda i, far: pl.BlockSpec(memory_space=pl.ANY if i in far else pltpu.VMEM)
    return pl.pallas_call(
        kernel,
        out_shape=outs,
        in_specs=[
            pl.BlockSpec(memory_space=pltpu.SMEM) if i in smem else place(i, hbm)
            for i in range(len(ins))
        ],
        out_specs=[place(i, hbm_outs) for i in range(len(outs))],
        scratch_shapes=list(scratch),
        compiler_params=pltpu.CompilerParams(vmem_limit_bytes=limit * MIB),
        cost_estimate=lasting(us),
    )(*ins)


def shape(*dims, dtype=F32):
    return jax.ShapeDtypeStruct(dims, dtype)


def as_row(ref):
    return ref[...].reshape(1, -1)


def join_segments(refs):
    return jnp.concatenate([as_row(ref).astype(F32) for ref in refs], axis=1)


def as_column(row):
    return jnp.broadcast_to(row, (8, row.shape[1])).T[:, :1]


def pairs(heads):
    return [pl.ds(pair * PAIR, PAIR) for pair in range(heads // 2)]


def split_pair(block):
    owner = lax.broadcasted_iota(jnp.int32, block.shape, 1) // HD
    empty = jnp.zeros_like(block)
    return jnp.concatenate(
        [jnp.where(owner == 0, block, empty), jnp.where(owner == 1, block, empty)], axis=0
    )


def attend_kernel(*refs, split):
    xs, refs = refs[:split], refs[split:]
    segs, refs = refs[:split], refs[split:]
    wq_ref, wk_ref, wv_ref, bq_ref, bv_ref = refs[:5]
    q_ref, k_ref, v_ref, *ctx_refs, lse_ref, bias, vt, ctxt = refs[5:]
    heads = q_ref.shape[1] // HD
    block = 256
    segments = join_segments(segs)
    bias[...] = jnp.where(as_column(segments) == segments, 0.0, MASKED)
    size = LEN // split
    for i, x_ref in enumerate(xs):
        x, rows = x_ref[...], pl.ds(i * size, size)
        q_ref[rows, :] = ((nn(x, wq_ref[...]) + as_row(bq_ref)) * SCALE).astype(BF16)
        k_ref[rows, :] = nn(x, wk_ref[...]).astype(BF16)
        value = (nn(x, wv_ref[...]) + as_row(bv_ref)).astype(BF16)
        v_ref[rows, :] = value
        vt[:, rows] = value.T

    @pl.loop(0, LEN // block)
    def _(j):
        here = pl.ds(pl.multiple_of(j * block, block), block)
        products = [
            nt(k_ref[:, lanes], split_pair(q_ref[here, lanes])) for lanes in pairs(heads)
        ]
        mask = bias[:, here]
        weights, tops, totals = [], [], []
        for head in range(heads):
            start = head % 2 * block
            scores = products[head // 2][:, start : start + block] + mask
            tops.append(jnp.max(scores, axis=0, keepdims=True))
            weight = jnp.exp(scores - tops[-1])
            totals.append(jnp.sum(weight, axis=0, keepdims=True))
            weights.append(weight.astype(BF16))
        for head in range(heads):
            at = pl.ds(head * HD, HD)
            ctxt[at, here] = nn(vt[at, :], weights[head]) * (1.0 / totals[head])
            lse_ref[0, pl.ds(head, 1), here] = tops[head] + jnp.log(totals[head])

    for i, ctx_ref in enumerate(ctx_refs):
        ctx_ref[...] = ctxt[:, pl.ds(i * size, size)].T.astype(BF16)


def attention_forward(xs, segs, w_query, w_key, w_value, b_query, b_value):
    split = len(xs)
    size = LEN // split
    rows, model = xs[0].shape[0] // size, xs[0].shape[1]
    width = w_query.shape[1]
    by_row = pl.BlockSpec((LEN, width), lambda r: (r, 0))
    by_part = pl.BlockSpec((size, width), lambda r: (r, 0))
    whole = lambda *dims: pl.BlockSpec(dims, lambda r: (0,) * len(dims))
    us = 13 * rows
    query, key, value, *contexts, lse = pl.pallas_call(
        partial(attend_kernel, split=split),
        grid=(rows,),
        out_shape=[shape(rows * LEN, width, dtype=BF16)] * 3
        + [shape(rows * size, width, dtype=BF16)] * split
        + [shape(rows, 8, LEN)],
        in_specs=[pl.BlockSpec((size, model), lambda r: (r, 0))] * split
        + [pl.BlockSpec((size,), lambda r: (r,))] * split
        + [
            whole(model, width),
            whole(model, width),
            whole(model, width),
            whole(width),
            whole(width),
        ],
        out_specs=[by_row] * 3
        + [by_part] * split
        + [pl.BlockSpec((1, 8, LEN), lambda r: (r, 0, 0))],
        scratch_shapes=[
            pltpu.VMEM((LEN, LEN), F32),
            pltpu.VMEM((width, LEN), BF16),
            pltpu.VMEM((width, LEN), F32),
        ],
        compiler_params=pltpu.CompilerParams(vmem_limit_bytes=60 * MIB),
        cost_estimate=lasting(us),
    )(*xs, *segs, w_query, w_key, w_value, b_query, b_value)
    return query, key, value, contexts, lse


def attend_back_kernel(
    q_ref, k_ref, v_ref, lse_ref, *refs, pair, split
):
    segs, ctx_refs, dctx_refs = (refs[i * split : (i + 1) * split] for i in range(3))
    dq_ref, dk_ref, dv_ref, kt, dqt, dk_sum, dv_sum, inner, dctx_ref, ctx_ref, seg = refs[
        3 * split :
    ]
    size = LEN // split
    for i in range(split):
        dctx_ref[pl.ds(i * size, size), :] = dctx_refs[i][...]
        ctx_ref[pl.ds(i * size, size), :] = ctx_refs[i][...]
    width = q_ref.shape[1]
    block = 256
    kt[...] = k_ref[...].T
    seg[...] = join_segments(segs)
    column = as_column(seg[...])
    picks = lax.broadcasted_iota(jnp.int32, (8, width), 0) == (
        lax.broadcasted_iota(jnp.int32, (8, width), 1) // HD
    )
    product = ctx_ref[...].astype(F32) * dctx_ref[...].astype(F32)
    inner[...] = lax.dot_general(
        picks.astype(F32), product, (((1,), (1,)), ((), ())),
        precision=lax.Precision.HIGHEST, preferred_element_type=F32,
    )
    dk_sum[...] = jnp.zeros_like(dk_sum)
    dv_sum[...] = jnp.zeros_like(dv_sum)

    @pl.loop(0, LEN // block)
    def _(j):
        here = pl.ds(pl.multiple_of(j * block, block), block)
        allowed = column == seg[:, here]
        queries, grads = split_pair(q_ref[here, :]), split_pair(dctx_ref[here, :])
        products, slopes = nt(k_ref[...], queries), nt(v_ref[...], grads)
        weights, changes = [], []
        for side in range(2):
            at = slice(side * block, (side + 1) * block)
            scores = jnp.where(allowed, products[:, at], MASKED)
            weight = jnp.exp(scores - lse_ref[0, 2 * pair + side : 2 * pair + side + 1, here])
            change = weight * (slopes[:, at] - inner[side : side + 1, here])
            weights.append(weight.astype(BF16))
            changes.append(change.astype(BF16))
        dv_sum[...] += nn(jnp.concatenate(weights, axis=1), grads)
        dk_sum[...] += nn(jnp.concatenate(changes, axis=1), queries)
        for side in range(2):
            at = slice(side * HD, (side + 1) * HD)
            dqt[at, here] = nn(kt[at, :], changes[side]) * SCALE

    dq_ref[...] = dqt[...].T.astype(BF16)
    dk_ref[...] = dk_sum[...].astype(BF16)
    dv_ref[...] = dv_sum[...].astype(BF16)


def attention_backward(pair, query, key, value, contexts, grads, lse, segs):
    rows, split = query.shape[0] // LEN, len(contexts)
    columns = pl.BlockSpec((LEN, PAIR), lambda r: (r, pair))
    part = pl.BlockSpec((LEN // split, PAIR), lambda r: (r, pair))
    own = pl.BlockSpec((LEN, PAIR), lambda r: (r, 0))
    us = 7 * rows
    return pl.pallas_call(
        partial(attend_back_kernel, pair=pair, split=split),
        grid=(rows,),
        out_shape=[shape(rows * LEN, PAIR, dtype=BF16)] * 3,
        in_specs=[columns] * 3
        + [
            pl.BlockSpec((1, 8, LEN), lambda r: (r, 0, 0)),
        ]
        + [pl.BlockSpec((LEN // split,), lambda r: (r,))] * split
        + [part] * (2 * split),
        out_specs=[own] * 3,
        scratch_shapes=[
            pltpu.VMEM((PAIR, LEN), BF16),
            pltpu.VMEM((PAIR, LEN), F32),
            pltpu.VMEM((LEN, PAIR), F32),
            pltpu.VMEM((LEN, PAIR), F32),
            pltpu.VMEM((8, LEN), F32),
            pltpu.VMEM((LEN, PAIR), BF16),
            pltpu.VMEM((LEN, PAIR), BF16),
            pltpu.VMEM((1, LEN), F32),
        ],
        compiler_params=pltpu.CompilerParams(vmem_limit_bytes=24 * MIB),
        cost_estimate=lasting(us),
    )(query, key, value, lse, *segs, *contexts, *grads)


def rearrange(order, source, target):
    third = source.shape[0] // 3
    size = third // BLOCKS
    for p in range(3):
        for place in range(BLOCKS):
            rows = pl.ds(pl.multiple_of(p * third + order[p, place] * size, 16), size)
            target[pl.ds(p * third + place * size, size), :] = source[rows, :]


class Copies:
    def __init__(self, sems):
        self.sems, self.used, self.open = sems, 0, []

    def start(self, source, target):
        copy = pltpu.make_async_copy(source, target, self.sems.at[self.used])
        self.used += 1
        copy.start()
        return copy

    def store(self, source, target):
        self.open.append(self.start(source, target))

    def drain(self):
        for copy in self.open:
            copy.wait()


def as_lines(row, cols):
    return jnp.concatenate(
        [row[:, i : i + cols] for i in range(0, row.shape[1], cols)], axis=0
    )


def split_small(values):
    high = values.astype(BF16)
    return jnp.concatenate([high, (values - high.astype(F32)).astype(BF16)], axis=0)


def layer_kernel(
    x_ref, ctx_a, ctx_b, wo_a, wo_b, b_out, gain_one, shift_one, b_down, gain_two, shift_two,
    bu_a, bu_b, order, wu_a, wu_b, wd_a, wd_b, cot_hbm,
    sums_ref, gctx_a, gctx_b, out_a, out_b, mixed_hbm, one_hbm, down_a, down_b, up_a, up_b,
    wu, wd, cot, mixed, after_buf, normed_buf, inverse_buf, slope, grad_buf, low_buf, act,
    flipped, moved, parts, total, sems,
):
    rows, model = x_ref.shape
    half = wu_a.shape[1]
    chunk = 512
    copies = Copies(sems)
    ups, downs = [], []
    for side, up in enumerate((wu_a, wu_b)):
        for start in range(0, half, chunk):
            to = pl.ds(side * half + start, chunk)
            ups.append(copies.start(up.at[:, pl.ds(start, chunk)], wu.at[:, to]))
    for side, down in enumerate((wd_a, wd_b)):
        downs.append(copies.start(down, wd.at[pl.ds(side * half, half), :]))
    cot_copy = copies.start(cot_hbm, cot)
    b_out, gain_one, shift_one, b_down, gain_two, shift_two = map(
        as_row, (b_out, gain_one, shift_one, b_down, gain_two, shift_two)
    )
    biases = [as_row(bu_a), as_row(bu_b)]

    hidden = nn(ctx_a[...], wo_a[...]) + nn(ctx_b[...], wo_b[...])
    normed, inverse = normalize_parts(x_ref[...].astype(F32) + hidden + b_out)
    normed_buf[...] = normed
    inverse_buf[...] = inverse
    after_buf[...] = (normed * gain_one + shift_one).astype(BF16)

    def raise_up(i):
        ups[i].wait()
        here = pl.ds(i * chunk, chunk)
        start = i * chunk % half
        bias = biases[i * chunk // half][:, start : start + chunk]
        return nn(after_buf[...], wu[:, here]) + bias

    count = 2 * half // chunk
    upper = raise_up(0)
    for i in range(count):
        following = raise_up(i + 1) if i + 1 < count else None
        here = pl.ds(i * chunk, chunk)
        active, steep = gelu_parts(upper)
        act[:, here] = active.astype(BF16)
        slope[:, here] = steep.astype(BF16)
        upper = following
    for copy in downs:
        copy.wait()
    total[...] = nn(act[...], wd[...])
    cot_copy.wait()

    after = normed_buf[...] * gain_one + shift_one
    normed, inverse = normalize_parts(after + total[...] + b_down)
    mixed[...] = (normed * gain_two + shift_two).astype(BF16)
    copies.store(mixed, mixed_hbm)
    outer = cot[...].astype(F32)
    grad = normalize_back(outer, normed, inverse, gain_two)
    grad_buf[...] = grad
    low_buf[...] = grad.astype(BF16)
    add_up = lambda values: jnp.sum(values, axis=0, keepdims=True)
    sums_two = [add_up(outer * normed), add_up(outer), add_up(grad)]

    flipped[...] = grad_buf[...].T.astype(BF16)
    rearrange(order, flipped, moved)
    for side, out in ((1, down_b), (0, down_a)):
        parts[side] = nn(moved[...], act[:, pl.ds(side * half, half)]).astype(BF16)
        copies.store(parts.at[side], out)
    flipped[...] = after_buf[...].T
    rearrange(order, flipped, moved)
    sums_up = [None, None]
    for side, out in ((1, up_b), (0, up_a)):
        here = pl.ds(side * half, half)
        pulled = nt(low_buf[...], wd[here, :])
        slope[:, here] = (pulled * slope[:, here].astype(F32)).astype(BF16)
        sums_up[side] = add_up(slope[:, here].astype(F32))
        parts[2 + side] = nn(moved[...], slope[:, here]).astype(BF16)
        copies.store(parts.at[2 + side], out)
    total[...] = nt(slope[...], wu[...])

    after = grad_buf[...] + total[...]
    normed = normed_buf[...]
    grad = normalize_back(after, normed, inverse_buf[...], gain_one)
    grad_buf[...] = grad
    copies.store(grad_buf, one_hbm)
    low_buf[...] = grad.astype(BF16)
    gctx_b[...] = nt(low_buf[...], wo_b[...]).astype(BF16)
    gctx_a[...] = nt(low_buf[...], wo_a[...]).astype(BF16)
    flipped[...] = grad_buf[...].T.astype(BF16)
    rearrange(order, flipped, moved)
    out_b[pl.ds(0, model), :] = nn(moved[...], ctx_b[...]).astype(BF16)
    out_a[...] = nn(moved[...], ctx_a[...]).astype(BF16)

    cols = ctx_a.shape[1] // 3
    sums = [add_up(after * normed), add_up(after), add_up(grad), *sums_two]
    shared = as_lines(jnp.concatenate(sums, axis=1), cols)
    own, other = (as_lines(part, cols) for part in sums_up)
    sums_ref[...] = jnp.concatenate([shared, own], axis=0)
    rider = split_small(jnp.concatenate([shared, other], axis=0))
    lines = rider.shape[0] // 3
    for i in range(3):
        out_b[pl.ds(model, lines), pl.ds(i * cols, cols)] = rider[i * lines : (i + 1) * lines]
    copies.drain()


SMALL = 16


def project_kernel(*refs):
    x_a, x_b, out_a, out_b, sums_ref, order = refs[:6]
    grads, outs = refs[6:15], refs[15:]
    keeps, sends, (small, joint, flipped, moved) = outs[:3], outs[3:6], outs[6:]
    width = joint.shape[1] // 3
    cols = width // 3
    here, model = x_a.shape
    half = keeps[0].shape[0]
    flipped[:, pl.ds(0, here)] = x_a[...].T
    flipped[:, pl.ds(here, here)] = x_b[...].T
    for i, grad in enumerate(grads):
        at = pl.ds(i % 3 * width + i // 3 * PAIR, PAIR)
        joint[:, at] = grad[...]
    rearrange(order, flipped, moved)
    product = nn(moved[...], joint[...]).astype(BF16)
    other = (out_a[...].astype(F32) + out_b[pl.ds(0, model), :].astype(F32)).astype(BF16)
    for p in range(3):
        for i, out in enumerate((keeps[p], sends[p])):
            rows = slice((2 * p + i) * half, (2 * p + i + 1) * half)
            out[pl.ds(0, half), pl.ds(0, 3 * width)] = product[rows]
            out[pl.ds(0, half), pl.ds(3 * width, width)] = other[rows]
    sums = jnp.sum(joint[...].astype(F32), axis=0, keepdims=True)
    lines = out_b.shape[0] - model
    rider = [out_b[pl.ds(model, lines), pl.ds(i * cols, cols)] for i in range(3)]
    rider = jnp.concatenate(rider, axis=0).astype(F32)
    count = sums_ref.shape[0]
    shared = sums_ref[...] + (rider[:count] + rider[count:])
    per = small.shape[1] // cols
    small[...] = jnp.zeros_like(small)
    for i in range(count):
        small[pl.ds(i // per, 1), pl.ds(i % per * cols, cols)] = shared[i : i + 1]
    rows = count // per
    small[pl.ds(rows, 1), pl.ds(0, width)] = sums[:, :width]
    small[pl.ds(rows + 1, 1), pl.ds(0, width)] = sums[:, 2 * width :]
    sends[0][pl.ds(half, SMALL), :] = jnp.zeros((SMALL, sends[0].shape[1]), BF16)
    high = split_small(small[...])
    for i in range(2):
        sends[0][pl.ds(half, SMALL), pl.ds(i * small.shape[1], small.shape[1])] = high[
            i * SMALL : (i + 1) * SMALL
        ]


def tokens_kernel(joint, w_query, w_key, w_value, grad_one, part_ref, own_ref):
    rows, width = own_ref.shape[0], w_query.shape[1]
    for first, out_ref in ((rows, part_ref), (0, own_ref)):
        total = grad_one[...] if first == 0 else 0.0
        for i, weight in enumerate((w_query, w_key, w_value)):
            part = joint[pl.ds(first, rows), pl.ds(i * width, width)]
            total = total + nt(part, weight[...])
        out_ref[...] = total.astype(out_ref.dtype)


def unpack(order, lows, highs, put):
    third = 2 * lows[0].shape[0]
    size = third // BLOCKS
    for p, halves_of_part in enumerate(zip(lows, highs)):
        for place in range(BLOCKS):
            rows = pl.ds(pl.multiple_of(p * third + order[p, place] * size, 8), size)
            side, at = divmod(place, BLOCKS // 2)
            put(rows, halves_of_part[side][pl.ds(at * size, size), :].astype(F32))


def unpack_both_kernel(*refs):
    lows, highs, (order, down_ref, up_ref, natural) = refs[:3], refs[3:6], refs[6:]
    half = up_ref.shape[1]

    def put(rows, values):
        natural[rows, :] = values[:, :half]
        up_ref[rows, :] = values[:, half:]

    unpack(order, lows, highs, put)
    step = 512
    for start in range(0, half, step):
        here = pl.ds(start, step)
        down_ref[here, :] = natural[:, here].T


def unpack_project_kernel(*refs):
    lows, highs, refs = refs[:3], refs[3:6], refs[6:]
    order, q_ref, k_ref, v_ref, out_ref, natural = refs
    width = q_ref.shape[1]

    def put(rows, values):
        for i, ref in enumerate((q_ref, k_ref, v_ref, natural)):
            ref[rows, :] = values[:, i * width : (i + 1) * width]

    unpack(order, lows, highs, put)
    out_ref[...] = natural[...].T


def swap(value, bit, count, name="swap"):
    with jax.named_scope(name):
        return lax.ppermute(value, "dp", [(i, i ^ bit) for i in range(count)])


def across(value):
    return lax.ppermute(value, "tensor", [(0, 1), (1, 0)])


def add(left, right):
    return (left.astype(F32) + right.astype(F32)).astype(BF16)


STAGES = ((1, 2, 4, 8), (2, 4, 1, 8), (4, 1, 2, 8))


def block_order():
    mine = lax.rem(lax.axis_index("dp"), BLOCKS // 2)
    rows = []
    for bits in STAGES:
        rows.append(
            [
                sum(bit for i, bit in enumerate(bits) if place >> (len(bits) - 1 - i) & 1)
                for place in range(BLOCKS)
            ]
        )
    return jnp.bitwise_xor(jnp.array(rows, jnp.int32), mine.astype(jnp.int32))


def halves(own, other):
    half = own.shape[0] // 6
    cut = lambda at: add(own[at * half : (at + 1) * half], other[at * half : (at + 1) * half])
    return [cut(2 * p) for p in range(3)], [cut(2 * p + 1) for p in range(3)]


def send_stage(sends, step, count, name):
    return [
        swap(sends[p], STAGES[p][step], count, f"{name}_send{step}_{p}") for p in range(3)
    ]


def next_halves(keeps, gots):
    half = keeps[0].shape[0] // 2
    cut = lambda side: [
        add(keeps[p][side * half : (side + 1) * half], gots[p][side * half : (side + 1) * half])
        for p in range(3)
    ]
    return cut(0), cut(1)


def with_rider(rows, small):
    high = split_small(small)
    rider = jnp.concatenate([high[:SMALL], high[SMALL:]], axis=1)
    rider = jnp.pad(rider, ((0, 0), (0, rows.shape[1] - rider.shape[1])))
    return jnp.concatenate([rows, rider], axis=0)


def take_small(got, rows, small):
    rider, width = got[rows:].astype(F32), small.shape[1]
    return got[:rows], small + (rider[:, :width] + rider[:, width : 2 * width])


def halves_and_small(keeps, gots, small):
    first, small = take_small(gots[0], keeps[0].shape[0], small)
    keeps, sends = next_halves(keeps, [first, *gots[1:]])
    return keeps, [with_rider(sends[0], small), *sends[1:]], small


def gather_stage(values, step, count, name):
    return [
        swap(values[p], STAGES[p][step], count, f"{name}_gather{step}_{p}") for p in range(3)
    ]


def after(values, *earlier):
    return lax.optimization_barrier((values, *earlier))[0]


def shards(
    tokens, segment_ids, w_query, w_key, w_value, b_query, b_value, w_out, b_out, gain_attn,
    shift_attn, w_up, b_up, w_down, b_down, gain_ffn, shift_ffn, cotangent,
):
    count = lax.axis_size("dp")
    here, model = tokens.shape
    width, half = w_query.shape[1], w_up.shape[1]
    row = lambda vector: vector.reshape(1, -1)

    tokens_b = across(tokens)
    segments_b, bu_b = across(segment_ids), across(b_up)
    wo_b, wu_b, wd_b = map(across, after((w_out, w_up, w_down), tokens_b))
    order = block_order()
    one_row = here < LEN
    lay = lambda own, other: (
        [own, other] if one_row else [jnp.concatenate([own, other], axis=0)]
    )
    segs = lay(segment_ids, segments_b)
    query, key, value, contexts, lse = attention_forward(
        lay(tokens, tokens_b), after(segs, order), w_query, w_key, w_value, b_query, b_value
    )
    if one_row:
        ctx_a, ctx_b = contexts
    else:
        ctx_a, ctx_b = contexts[0][:here], contexts[0][here:]
    ctx_b = across(ctx_b)

    low = lambda *dims: shape(*dims, dtype=BF16)
    held = lambda *dims: pltpu.VMEM(dims, BF16)
    wide = lambda *dims: pltpu.VMEM(dims, F32)
    lines = (6 * model + half) // (width // 3)
    size = min(here, LEN // 2)

    def layer(at):
        cut = lambda value: value[at : at + size]
        return call(
            layer_kernel,
            [
                shape(lines, width // 3), low(size, width), low(size, width), low(model, width),
                low(model + 2 * lines // 3, width), low(size, model), shape(size, model),
            ] + [low(model, half)] * 4,
            [
                cut(tokens), cut(ctx_a), cut(ctx_b), w_out, wo_b, b_out, gain_attn, shift_attn,
                b_down, gain_ffn, shift_ffn, b_up, bu_b, order, w_up, wu_b, w_down, wd_b,
                cut(cotangent),
            ],
            [
                held(model, 2 * half), held(2 * half, model), held(size, model), held(size, model),
                held(size, model), wide(size, model), wide(size, 1), held(size, 2 * half),
                wide(size, model), held(size, model), held(size, 2 * half), held(model, size),
                held(model, size), held(4, model, half), wide(size, model),
                pltpu.SemaphoreType.DMA((20,)),
            ],
            limit=60,
            smem=(13,),
            hbm=(14, 15, 16, 17, 18),
            hbm_outs=range(5, 11),
            us=35,
        )

    blocks = [layer(at) for at in range(0, here, size)]
    if len(blocks) == 1:
        small_sums, gctx_a, gctx_b, out_a, out_b, mixed, grad_one, *weights = blocks[0]
    else:
        small_sums, gctx_a, gctx_b, out_a, out_b, mixed, grad_one, *weights = (
            jnp.concatenate(each, axis=0)
            if i in (1, 2, 5, 6)
            else sum(part.astype(F32) for part in each).astype(each[0].dtype)
            for i, each in enumerate(zip(*blocks))
        )
    down_a, down_b, up_a, up_b = weights
    grad_contexts = lay(gctx_a, across(gctx_b))
    down_b, up_b, out_b = after((down_b, up_b, out_b), grad_contexts)
    down_got, up_got, out_got = across(down_b), across(up_b), across(out_b)

    back = lambda pair, earlier: attention_backward(
        pair, query, key, value, contexts, after(grad_contexts, earlier), lse, segs
    )
    grads = back(0, grad_contexts)
    down_got, up_got = after((down_got, up_got), grads)
    down_keep, down_send = halves(down_a, down_got)
    up_keep, up_send = halves(up_a, up_got)
    join = lambda one, two: [jnp.concatenate(pair, axis=1) for pair in zip(one, two)]
    both_keep, both_send = join(down_keep, up_keep), join(down_send, up_send)
    both_new = send_stage(both_send, 0, count, "both")

    grads += back(1, (grads, both_send))
    grads += back(2, grads)
    both_keep, both_send = next_halves(both_keep, after(both_new, grads))
    both_new = send_stage(both_send, 1, count, "both")
    grads = after(grads, both_send)
    sixth = low(model // 6, 4 * width)
    *last, small, joint = call(
        project_kernel,
        [sixth] * 3
        + [low(model // 6 + SMALL, 4 * width), sixth, sixth]
        + [shape(SMALL, half // 3), low(2 * here, 3 * width)],
        [
            tokens, tokens_b, out_a, out_got, small_sums, order, *grads,
        ],
        [held(model, 2 * here), held(model, 2 * here)],
        smem=(5,),
        us=7,
    )
    last_keep, last_send = last[:3], last[3:]
    both_keep, both_send = next_halves(both_keep, after(both_new, last))
    both_new = send_stage(both_send, 2, count, "both")
    last_send = after(last_send, both_send)
    last_new = send_stage(last_send, 0, count, "last")
    token_part, token_own = call(
        tokens_kernel,
        [low(here, model), shape(here, model)],
        [after(joint, last_send), w_query, w_key, w_value, grad_one],
        us=5,
    )
    token_got = across(token_part)

    join_rows = lambda one, two: [jnp.concatenate(pair, axis=0) for pair in zip(one, two)]
    meet = lambda keeps, gots: jnp.concatenate([add(k, g) for k, g in zip(keeps, gots)], axis=0)
    apart = lambda value: [
        value[i * value.shape[0] // 3 : (i + 1) * value.shape[0] // 3] for i in range(3)
    ]
    extras = [BLOCKS // 2 << i for i in range((count // (BLOCKS // 2)).bit_length() - 1)]
    both_value = meet(both_keep, after(both_new, token_own))
    both_got = swap(both_value, extras[0], count, "both_exchange")

    last_keep, last_send, small = halves_and_small(last_keep, after(last_new, both_value), small)
    last_new = send_stage(last_send, 1, count, "last")
    last_keep, last_send, small = halves_and_small(last_keep, last_new, small)
    last_new = send_stage(last_send, 2, count, "last")
    grad_tokens = token_own + after(token_got, last_send).astype(F32)
    first, small = take_small(last_new[0], last_keep[0].shape[0], small)
    last_value = meet(last_keep, [first, *last_new[1:]])
    rider = with_rider(last_value, small)
    last_got = swap(rider, extras[0], count, "last_exchange")

    both_value = add(both_value, after(both_got, rider))
    for extra in extras[1:]:
        both_value = add(both_value, swap(both_value, extra, count))
    both = apart(both_value)
    both = join_rows(both, gather_stage(both, 2, count, "both"))
    both_new = gather_stage(both, 1, count, "both")

    last_got, small = take_small(after(last_got, both), last_value.shape[0], small)
    last_value = add(last_value, last_got)
    for extra in extras[1:]:
        got = swap(with_rider(last_value, small), extra, count)
        got, small = take_small(got, last_value.shape[0], small)
        last_value = add(last_value, got)
    last = apart(last_value)
    last_new = gather_stage(last, 2, count, "last")
    both = join_rows(both, after(both_new, last))
    last = join_rows(last, after(last_new, both))
    last_new = gather_stage(last, 1, count, "last")
    both = after(both, last)
    both_new = gather_stage(both, 0, count, "both")
    last = join_rows(last, after(last_new, both))
    last_new = gather_stage(last, 0, count, "last")
    grad_w_down, grad_w_up = call(
        unpack_both_kernel,
        [shape(half, model), shape(model, half)],
        [*both, *after(both_new, last), order],
        [wide(model, half)],
        limit=40,
        smem=(6,),
    )
    last_new = after(last_new, grad_w_down)
    grad_w_query, grad_w_key, grad_w_value, grad_w_out = call(
        unpack_project_kernel,
        [shape(model, width)] * 3 + [shape(width, model)],
        [*last, *last_new, order],
        [wide(model, width)],
        limit=32,
        smem=(6,),
    )
    small = after(small, last)

    flat = small.reshape(-1)
    (
        grad_gain_attn, grad_shift_attn, grad_b_out, grad_gain_ffn, grad_shift_ffn, grad_b_down,
        grad_b_up,
    ) = jnp.split(flat[: 6 * model + half], [model * i for i in range(1, 7)])
    others = small[(6 * model + half) // small.shape[1] :]
    grad_b_query, grad_b_value = others[0, :width], others[1, :width]
    return (
        mixed, grad_tokens, grad_w_query, grad_w_key, grad_w_value, grad_b_query, grad_b_value,
        grad_w_out, grad_b_out, grad_gain_attn, grad_shift_attn, grad_w_up, grad_b_up, grad_w_down,
        grad_b_down, grad_gain_ffn, grad_shift_ffn,
    )


def solution(mesh):
    placed = (
        P(("dp", "tensor"), None),
        P(("dp", "tensor")),
        P(None, "tensor"),
        P(None, "tensor"),
        P(None, "tensor"),
        P("tensor"),
        P("tensor"),
        P("tensor", None),
        P(),
        P(),
        P(),
        P(None, "tensor"),
        P("tensor"),
        P("tensor", None),
        P(),
        P(),
        P(),
        P(("dp", "tensor"), None),
    )
    return jax.shard_map(
        shards,
        mesh=mesh,
        in_specs=placed,
        out_specs=(
            P(("dp", "tensor"), None),
            P(("dp", "tensor"), None),
            P(None, "tensor"),
            P(None, "tensor"),
            P(None, "tensor"),
            P("tensor"),
            P("tensor"),
            P("tensor", None),
            P(),
            P(),
            P(),
            P(None, "tensor"),
            P("tensor"),
            P("tensor", None),
            P(),
            P(),
            P(),
        ),
        check_vma=False,
    )
```

time: 260 us -> 230 us (0.88)
  Pallas kernels: 103 us -> 91.5 us
  waiting for transfers between devices: 74.4 us -> 66 us
  starting transfers between devices: 57 us -> 51.3 us
  other arithmetic: 10.4 us -> 6.25 us
    ppermute x47 -> x38, waiting for transfers between devices: 72.2 us -> 56.3 us  [swap(): return lax.ppermute(value, 'dp', [(i, i ^ bit) for i in range(count)])]
    pallas_call x7 -> x5, Pallas kernels: 66.5 us -> 54.6 us  [call(): pl.pallas_call(kernel, out_shape=outs, in_specs=[pl.BlockSpec(memory_spac...]
    ppermute x14 -> x12, waiting for transfers between devices: 2.2 us -> 9.73 us  [across(): return lax.ppermute(value, 'tensor', [(0, 1), (1, 0)])]
    ppermute x47 -> x38, starting transfers between devices: 53.2 us -> 47.7 us  [swap(): return lax.ppermute(value, 'dp', [(i, i ^ bit) for i in range(count)])]
    convert_element_type x20 -> x21, other arithmetic: 6.73 us -> 2.93 us  [add(): return (left.astype(F32) + right.astype(F32)).astype(BF16)]
  transfers between devices with their start and end apart: 61 -> 50, of which waited for: 23 -> 29; matrix products, arithmetic and copies ran while one was open for 7% -> 5% of each run, Pallas kernels for 30% -> 24%
where the time goes in v3:
time: 230 us; the launch traced here: 225 us
  Pallas kernels  91.5 us (40%)
  waiting for transfers between devices  66 us (29%)
  starting transfers between devices  51.3 us (22%)
  local copies, waits for them, and re-layouts  8.6 us (4%)
  other arithmetic  6.25 us (3%)
    ppermute x38, waiting for transfers between devices, swap(): return lax.ppermute(value, 'dp', [(i, i ^ bit) for i in range(count)])  56.3 us
    pallas_call x5, Pallas kernels, call(): pl.pallas_call(kernel, out_shape=outs, in_specs=[pl.BlockSpec(memory_spac...  54.6 us
    ppermute x38, starting transfers between devices, swap(): return lax.ppermute(value, 'dp', [(i, i ^ bit) for i in range(count)])  47.7 us
    pallas_call x3, Pallas kernels, attention_backward(): pl.pallas_call(partial(attend_back_kernel, pair=pair, split=split), grid=...  20.8 us
    pallas_call x1, Pallas kernels, attention_forward(): pl.pallas_call(partial(attend_kernel, split=split), grid=(rows,), out_sha...  16.2 us
    ppermute x12, waiting for transfers between devices, across(): return lax.ppermute(value, 'tensor', [(0, 1), (1, 0)])  9.73 us
  transfers between devices with their start and end apart: 50, of which 29 were waited for; matrix products, arithmetic and copies ran while one was open for 5% of the time, Pallas kernels for 24%

profile of v3, /device:TPU:0, one launch (start us, length us, event | category | flops | bytes accessed | tf_op | source)
XLA Modules:
  0.0 225.4 jit_solution(12087555457970942859)
XLA Ops:
  1.2 2.1 collective-permute-done.refs_1_
  5.4 4.6 %collective-permute-done.1.refs_3_.refs_1_ = s32[512]{0:T(512)S(1)} collective-permute-done((s32[512]{0:T(512)}, s32[512]{0:T(512)S(1)}, u32[]{:S(2)}, u32[]{:S(2)}) %collective-permute-start.1) | collective-permute-done | bytes 2080 | tf_op jit(solution)/shard_map/ppermute | solution.py:509
  10.6 16.2 %shard_map.314 = (bf16[1024,384]{1,0:T(8,128)(2,1)}, bf16[1024,384]{1,0:T(8,128)(2,1)}, bf16[1024,384]{1,0:T(8,128)(2,1)}, bf16[512,384]{1,0:T(8,128)(2,1)}, bf1...) custom-call(bf16[512,768]{1,0:T(8,128)(2,1)} %refs_0_.9, bf16[512,768]{1,0:T(8,128)(2,1)} %copy-done.21, s32[512]{0:T(512)} %refs_0_.8, ...), custom_call_target="tpu_custom_call" | custom-call | flops 14949999616 | tf_op jit(solution)/shard_map/pallas_call | solution.py:155
  28.8 1.4 copy-done.20
  30.3 33.3 %shard_map.315 = (f32[48,128]{1,0:T(8,128)}, bf16[512,384]{1,0:T(8,128)(2,1)}, bf16[512,384]{1,0:T(8,128)(2,1)}, bf16[768,384]{1,0:T(8,128)(2,1)}, bf16[800,384]...) custom-call(bf16[512,768]{1,0:T(8,128)(2,1)} %refs_0_.9, ...), custom_call_target="tpu_custom_call" | custom-call | flops 40249999360 | tf_op jit(solution)/shard_map/pallas_call | solution.py:62
  64.0 1.6 collective-permute-done.7.refs_5_
  67.5 7.0 %shard_map.316 = (bf16[1024,128]{1,0:T(8,128)(2,1)S(1)}, bf16[1024,128]{1,0:T(8,128)(2,1)S(1)}, bf16[1024,128]{1,0:T(8,128)(2,1)S(1)}) custom-call(bf16[1024,384]{1,0:T(8,128)(2,1)S(1)} %copy-done.9, bf16[1024,384]{1,0:T(8,128)(2,1)S(1)} %copy-done.10, bf16[1024,384]{1,0:T(8,128)(2,1)S(1)} %copy-done.11, f32[1,8,1024]{2,1,0:T(8,128)S(1)} %copy-done.15, ...), custom_call_target="tpu_custom_call" | custom-call | flops 8049999872 | tf_op jit(solution)/shard_map/pallas_call | solution.py:242
  76.9 2.7 %collective-permute-start.11 = (bf16[128,3072]{1,0:T(8,128)(2,1)S(1)}, bf16[128,3072]{1,0:T(8,128)(2,1)S(1)}, u32[]{:S(2)}, u32[]{:S(2)}) collective-permute-start(bf16[128,3072]{1,0:T(8,128)(2,1)S(1)} %pad_maximum_fusion), channel_id=1, source_target_pairs={{0,2},{2,0},{4,6},{6,4},{8,10},{10,8},{12,14},{14,12},{16,18},{18,... | collective-permute-start | bytes 2359304 | tf_op jit(solution)/shard_map/both_send0_0/ppermute | solution.py:505
  79.7 1.6 collective-permute-start.12
  81.4 1.6 collective-permute-start.13
  83.0 6.8 %shard_map.317 = (bf16[1024,128]{1,0:T(8,128)(2,1)S(1)}, bf16[1024,128]{1,0:T(8,128)(2,1)S(1)}, bf16[1024,128]{1,0:T(8,128)(2,1)S(1)}) custom-call(bf16[1024,384]{1,0:T(8,128)(2,1)S(1)} %copy-done.9, bf16[1024,384]{1,0:T(8,128)(2,1)S(1)} %copy-done.10, bf16[1024,384]{1,0:T(8,128)(2,1)S(1)} %copy-done.11, f32[1,8,1024]{2,1,0:T(8,128)S(1)} %copy-done.15, ...), custom_call_target="tpu_custom_call" | custom-call | flops 8049999872 | tf_op jit(solution)/shard_map/pallas_call | solution.py:242
  89.8 7.0 %shard_map.318 = (bf16[1024,128]{1,0:T(8,128)(2,1)S(1)}, bf16[1024,128]{1,0:T(8,128)(2,1)S(1)}, bf16[1024,128]{1,0:T(8,128)(2,1)S(1)}) custom-call(bf16[1024,384]{1,0:T(8,128)(2,1)S(1)} %copy-done.9, bf16[1024,384]{1,0:T(8,128)(2,1)S(1)} %copy-done.10, bf16[1024,384]{1,0:T(8,128)(2,1)S(1)} %copy-done.11, f32[1,8,1024]{2,1,0:T(8,128)S(1)} %copy-done.15, ...), custom_call_target="tpu_custom_call" | custom-call | flops 8049999872 | tf_op jit(solution)/shard_map/pallas_call | solution.py:242
  97.7 1.6 collective-permute-done.12
  99.3 1.4 collective-permute-done.13
  101.7 1.7 collective-permute-start.15
  104.2 5.9 %shard_map.319 = (bf16[128,1536]{1,0:T(8,128)(2,1)S(1)}, bf16[128,1536]{1,0:T(8,128)(2,1)S(1)}, bf16[128,1536]{1,0:T(8,128)(2,1)S(1)}, bf16[144,1536]{1,0:T(8,12...) custom-call(bf16[512,768]{1,0:T(8,128)(2,1)} %refs_0_.9, ...), custom_call_target="tpu_custom_call" | custom-call | flops 8049999872 | tf_op jit(solution)/shard_map/pallas_call | solution.py:62
  111.4 1.6 collective-permute-done.14
  113.7 1.5 collective-permute-start.22
  115.8 1.6 collective-permute-start.19
  117.3 1.5 collective-permute-start.20
  118.9 4.3 %shard_map.320 = (bf16[512,768]{1,0:T(8,128)(2,1)S(1)}, f32[512,768]{1,0:T(8,128)S(1)}) custom-call(bf16[1024,1152]{1,0:T(8,128)(2,1)} %get-tuple-element.188.joint, bf16[768,384]{1,0:T(8,128)(2,1)S(1)} %copy-done.1, bf16[768,384]{1,0:T(8,128)(2,1)S(1)} %copy-done.2, bf16[768,384]{1,0:T(8,128)(2,1)S(1)} %copy-done.3, f32[512,768]{1,0:T(8,128)S(1)} %copy-done.8), custom_call_target="tpu_custom_call" | custom-call | flops 5750000128 | tf_op jit(solution)/shard_map/pallas_call | solution.py:62
  124.1 2.6 %collective-permute-start.31 = (bf16[96,3072]{1,0:T(8,128)(2,1)S(1)}, bf16[96,3072]{1,0:T(8,128)(2,1)S(1)}, u32[]{:S(2)}, u32[]{:S(2)}) collective-permute-start(bf16[96,3072]{1,0:T(8,128)(2,1)S(1)} %pad_maximum_fusion.6), channel_id=1, source_target_pairs={{0,16},{2,18},{4,20},{6,22},{8,24},{10,26},{12,28},{14,30},{16,0},... | collective-permute-start | bytes 1769480 | tf_op jit(solution)/shard_map/both_exchange/ppermute | solution.py:505
  127.4 5.6 %collective-permute-done.18 = bf16[144,1536]{1,0:T(8,128)(2,1)S(1)} collective-permute-done((bf16[144,1536]{1,0:T(8,128)(2,1)S(1)}, bf16[144,1536]{1,0:T(8,128)(2,1)S(1)}, u32[]{:S(2)}, u32[]{:S(2)}) %collective-permute-start.18) | collective-permute-done | bytes 442400 | tf_op jit(solution)/shard_map/last_send0_0/ppermute | solution.py:505
  134.7 4.4 %collective-permute-done.26 = bf16[64,1536]{1,0:T(8,128)(2,1)S(1)} collective-permute-done((bf16[64,1536]{1,0:T(8,128)(2,1)S(1)}, bf16[64,1536]{1,0:T(8,128)(2,1)S(1)}, u32[]{:S(2)}, u32[]{:S(2)}) %collective-permute-start.26) | collective-permute-done | bytes 196640 | tf_op jit(solution)/shard_map/last_send1_2/ppermute | solution.py:505
  139.7 4.5 %collective-permute-done.25 = bf16[64,1536]{1,0:T(8,128)(2,1)S(1)} collective-permute-done((bf16[64,1536]{1,0:T(8,128)(2,1)S(1)}, bf16[64,1536]{1,0:T(8,128)(2,1)S(1)}, u32[]{:S(2)}, u32[]{:S(2)}) %collective-permute-start.25) | collective-permute-done | bytes 196640 | tf_op jit(solution)/shard_map/last_send1_1/ppermute | solution.py:505
  144.3 1.5 collective-permute-start.28
  146.0 2.5 %collective-permute-start.27 = (bf16[48,1536]{1,0:T(8,128)(2,1)S(1)}, bf16[48,1536]{1,0:T(8,128)(2,1)S(1)}, u32[]{:S(2)}, u32[]{:S(2)}) collective-permute-start(bf16[48,1536]{1,0:T(8,128)(2,1)S(1)} %pad_maximum_fusion.21), channel_id=1, source_target_pairs={{0,8},{2,10},{4,12},{6,14},{8,0},{10,2},{12,4},{14,6},{16,24},{18,... | collective-permute-start | bytes 442376 | tf_op jit(solution)/shard_map/last_send2_0/ppermute | solution.py:505
  149.1 7.5 %collective-permute-done.27 = bf16[48,1536]{1,0:T(8,128)(2,1)S(1)} collective-permute-done((bf16[48,1536]{1,0:T(8,128)(2,1)S(1)}, bf16[48,1536]{1,0:T(8,128)(2,1)S(1)}, u32[]{:S(2)}, u32[]{:S(2)}) %collective-permute-start.27) | collective-permute-done | bytes 147488 | tf_op jit(solution)/shard_map/last_send2_0/ppermute | solution.py:505
  159.4 1.4 collective-permute-start.33
  160.9 2.5 %collective-permute-start.32 = (bf16[32,3072]{1,0:T(8,128)(2,1)S(1)}, bf16[32,3072]{1,0:T(8,128)(2,1)S(1)}, u32[]{:S(2)}, u32[]{:S(2)}) collective-permute-start(bf16[32,3072]{1,0:T(8,128)(2,1)S(1)} %get-tuple-element.264), channel_id=1, source_target_pairs={{0,8},{2,10},{4,12},{6,14},{8,0},{10,2},{12,4},{14,6},{16,24},{18,... | collective-permute-start | bytes 589832 | tf_op jit(solution)/shard_map/both_gather2_0/ppermute | solution.py:505
  163.9 1.5 collective-permute-start.40
  165.7 4.1 %collective-permute-start.39 = (bf16[64,3072]{1,0:T(8,128)(2,1)S(1)}, bf16[64,3072]{1,0:T(8,128)(2,1)S(1)}, u32[]{:S(2)}, u32[]{:S(2)}) collective-permute-start(bf16[64,3072]{1,0:T(8,128)(2,1)S(1)} %pad_maximum_fusion.11), channel_id=1, source_target_pairs={{0,8},{2,10},{4,12},{6,14},{8,0},{10,2},{12,4},{14,6},{16,24},{18,... | collective-permute-start | bytes 1179656 | tf_op jit(solution)/shard_map/both_gather1_1/ppermute | solution.py:505
  169.8 2.3 %collective-permute-done.32 = bf16[32,3072]{1,0:T(8,128)(2,1)S(1)} collective-permute-done((bf16[32,3072]{1,0:T(8,128)(2,1)S(1)}, bf16[32,3072]{1,0:T(8,128)(2,1)S(1)}, u32[]{:S(2)}, u32[]{:S(2)}) %collective-permute-start.32) | collective-permute-done | bytes 196640 | tf_op jit(solution)/shard_map/both_gather2_0/ppermute | solution.py:505
  172.2 1.5 collective-permute-start.38
  173.7 3.1 %collective-permute-done.30 = bf16[112,1536]{1,0:T(8,128)(2,1)S(1)} collective-permute-done((bf16[112,1536]{1,0:T(8,128)(2,1)S(1)}, bf16[112,1536]{1,0:T(8,128)(2,1)S(1)}, u32[]{:S(2)}, u32[]{:S(2)}) %collective-permute-start.30) | collective-permute-done | bytes 344096 | tf_op jit(solution)/shard_map/last_exchange/ppermute | solution.py:505
  176.9 1.5 collective-permute-start.37
  178.4 1.5 collective-permute-start.36
  180.0 4.4 %collective-permute-done.39 = bf16[64,3072]{1,0:T(8,128)(2,1)S(1)} collective-permute-done((bf16[64,3072]{1,0:T(8,128)(2,1)S(1)}, bf16[64,3072]{1,0:T(8,128)(2,1)S(1)}, u32[]{:S(2)}, u32[]{:S(2)}) %collective-permute-start.39) | collective-permute-done | bytes 393248 | tf_op jit(solution)/shard_map/both_gather1_1/ppermute | solution.py:505
  185.5 1.5 collective-permute-start.43
  187.0 1.5 collective-permute-start.41
  189.7 3.7 %collective-permute-done.43 = bf16[64,1536]{1,0:T(8,128)(2,1)S(1)} collective-permute-done((bf16[64,1536]{1,0:T(8,128)(2,1)S(1)}, bf16[64,1536]{1,0:T(8,128)(2,1)S(1)}, u32[]{:S(2)}, u32[]{:S(2)}) %collective-permute-start.43) | collective-permute-done | bytes 196640 | tf_op jit(solution)/shard_map/last_gather1_2/ppermute | solution.py:505
  194.9 2.1 collective-permute-start.46
  197.0 1.6 collective-permute-start.45
  203.4 4.8 %collective-permute-done.47.refs_3_ = bf16[128,3072]{1,0:T(8,128)(2,1)} collective-permute-done((bf16[128,3072]{1,0:T(8,128)(2,1)S(1)}, bf16[128,3072]{1,0:T(8,128)(2,1)}, u32[]{:S(2)}, u32[]{:S(2)}) %collective-permute-start.47) | collective-permute-done | bytes 786464 | tf_op jit(solution)/shard_map/both_gather0_0/ppermute | solution.py:505
  209.0 2.8 %collective-permute-done.48.refs_4_ = bf16[128,3072]{1,0:T(8,128)(2,1)} collective-permute-done((bf16[128,3072]{1,0:T(8,128)(2,1)S(1)}, bf16[128,3072]{1,0:T(8,128)(2,1)}, u32[]{:S(2)}, u32[]{:S(2)}) %collective-permute-start.48) | collective-permute-done | bytes 786464 | tf_op jit(solution)/shard_map/both_gather0_1/ppermute | solution.py:505
  211.8 2.0 collective-permute-done.49.refs_5_
  213.9 7.2 %shard_map.321 = (f32[1536,768]{1,0:T(8,128)}, f32[768,1536]{1,0:T(8,128)}) custom-call(bf16[128,3072]{1,0:T(8,128)(2,1)S(1)} %pad_maximum_fusion.3.refs_0_, bf16[128,3072]{1,0:T(8,128)(2,1)S(1)} %pad_maximum_fusion.4.refs_1_, bf16[128,3072]{1,0:T(8,128)(2,1)S(1)} %pad_maximum_fusion.5.refs_2_, bf16[128,3072]{1,0:T(8,128)(2,1)} %collective-permute-done.47.refs_3_, ...), custom_call_target="tpu_custom_call" | custom-call | flops 5750000128 | tf_op jit(solution)/shard_map/pallas_call | solution.py:62
  221.1 3.9 %shard_map.322 = (f32[768,384]{1,0:T(8,128)}, f32[768,384]{1,0:T(8,128)}, f32[768,384]{1,0:T(8,128)}, f32[384,768]{1,0:T(8,128)}) custom-call(bf16[128,1536]{1,0:T(8,128)(2,1)S(1)} %pad_maximum_fusion.13.refs_0_, bf16[128,1536]{1,0:T(8,128)(2,1)S(1)} %pad_maximum_fusion.14.refs_1_, bf16[128,1536]{1,0:T(8,128)(2,1)S(1)} %pad_maximum_fusion.15.refs_2_, ...), custom_call_target="tpu_custom_call" | custom-call | flops 5750000128 | tf_op jit(solution)/shard_map/pallas_call | solution.py:62
  (171 shorter events, 32.8 us)
Async XLA Ops:
  0.7 2.6 %collective-permute-start = (bf16[512,768]{1,0:T(8,128)(2,1)}, bf16[512,768]{1,0:T(8,128)(2,1)S(1)}, u32[]{:S(2)}, u32[]{:S(2)}) collective-permute-start(bf16[512,768]{1,0:T(8,128)(2,1)} %refs_0_.9), channel_id=1, source_target_pairs={{0,1},{1,0},{2,3},{3,2},{4,5},{5,4},{6,7},{7,6},{8,9},{9,8},{10,11... | collective-permute-start | bytes 2359304 | tf_op jit(solution)/shard_map/ppermute | solution.py:509
  3.3 25.5 %collective-permute-start.5 = (bf16[768,1536]{1,0:T(8,128)(2,1)}, bf16[768,1536]{1,0:T(8,128)(2,1)S(1)}, u32[]{:S(2)}, u32[]{:S(2)}) collective-permute-start(bf16[768,1536]{1,0:T(8,128)(2,1)} %wu_a.1), channel_id=1, source_target_pairs={{0,1},{1,0},{2,3},{3,2},{4,5},{5,4},{6,7},{7,6},{8,9},{9,8},{10,11... | collective-permute-start | bytes 7077896 | tf_op jit(solution)/shard_map/ppermute | solution.py:509
  3.7 25.1 %collective-permute-start.6 = (bf16[1536,768]{1,0:T(8,128)(2,1)}, bf16[1536,768]{1,0:T(8,128)(2,1)}, u32[]{:S(2)}, u32[]{:S(2)}) collective-permute-start(bf16[1536,768]{1,0:T(8,128)(2,1)} %wd_a.1), channel_id=1, source_target_pairs={{0,1},{1,0},{2,3},{3,2},{4,5},{5,4},{6,7},{7,6},{8,9},{9,8},{10,11... | collective-permute-start | bytes 7077896 | tf_op jit(solution)/shard_map/ppermute | solution.py:509
  3.8 6.2 %collective-permute-start.1 = (s32[512]{0:T(512)}, s32[512]{0:T(512)S(1)}, u32[]{:S(2)}, u32[]{:S(2)}) collective-permute-start(s32[512]{0:T(512)} %refs_0_.8), channel_id=1, source_target_pairs={{0,1},{1,0},{2,3},{3,2},{4,5},{5,4},{6,7},{7,6},{8,9},{9,8},{10,11... | collective-permute-start | bytes 6152 | tf_op jit(solution)/shard_map/ppermute | solution.py:509
  10.1 18.7 %collective-permute-start.3 = (bf16[384,768]{1,0:T(8,128)(2,1)}, bf16[384,768]{1,0:T(8,128)(2,1)}, u32[]{:S(2)}, u32[]{:S(2)}) collective-permute-start(bf16[384,768]{1,0:T(8,128)(2,1)} %wo_a.1), channel_id=1, source_target_pairs={{0,1},{1,0},{2,3},{3,2},{4,5},{5,4},{6,7},{7,6},{8,9},{9,8},{10,11... | collective-permute-start | bytes 1769480 | tf_op jit(solution)/shard_map/ppermute | solution.py:509
  63.6 2.0 collective-permute-start.7
  65.6 8.9 %collective-permute-start.9 = (bf16[768,1536]{1,0:T(8,128)(2,1)}, bf16[768,1536]{1,0:T(8,128)(2,1)S(1)}, u32[]{:S(2)}, u32[]{:S(2)}) collective-permute-start(bf16[768,1536]{1,0:T(8,128)(2,1)} %get-tuple-element.148), channel_id=1, source_target_pairs={{0,1},{1,0},{2,3},{3,2},{4,5},{5,4},{6,7},{7,6},{8,9},{9,8},{10,11... | collective-permute-start | bytes 7077896 | tf_op jit(solution)/shard_map/ppermute | solution.py:509
  66.0 8.6 %collective-permute-start.10 = (bf16[768,1536]{1,0:T(8,128)(2,1)}, bf16[768,1536]{1,0:T(8,128)(2,1)S(1)}, u32[]{:S(2)}, u32[]{:S(2)}) collective-permute-start(bf16[768,1536]{1,0:T(8,128)(2,1)} %get-tuple-element.149), channel_id=1, source_target_pairs={{0,1},{1,0},{2,3},{3,2},{4,5},{5,4},{6,7},{7,6},{8,9},{9,8},{10,11... | collective-permute-start | bytes 7077896 | tf_op jit(solution)/shard_map/ppermute | solution.py:509
  66.1 38.0 %collective-permute-start.8 = (bf16[800,384]{1,0:T(8,128)(2,1)}, bf16[800,384]{1,0:T(8,128)(2,1)S(1)}, u32[]{:S(2)}, u32[]{:S(2)}) collective-permute-start(bf16[800,384]{1,0:T(8,128)(2,1)} %get-tuple-element.136), channel_id=1, source_target_pairs={{0,1},{1,0},{2,3},{3,2},{4,5},{5,4},{6,7},{7,6},{8,9},{9,8},{10,11... | collective-permute-start | bytes 1843208 | tf_op jit(solution)/shard_map/ppermute | solution.py:509
  76.9 20.8 %collective-permute-start.11 = (bf16[128,3072]{1,0:T(8,128)(2,1)S(1)}, bf16[128,3072]{1,0:T(8,128)(2,1)S(1)}, u32[]{:S(2)}, u32[]{:S(2)}) collective-permute-start(bf16[128,3072]{1,0:T(8,128)(2,1)S(1)} %pad_maximum_fusion), channel_id=1, source_target_pairs={{0,2},{2,0},{4,6},{6,4},{8,10},{10,8},{12,14},{14,12},{16,18},{18,... | collective-permute-start | bytes 2359304 | tf_op jit(solution)/shard_map/both_send0_0/ppermute | solution.py:505
  79.7 19.6 %collective-permute-start.12 = (bf16[128,3072]{1,0:T(8,128)(2,1)S(1)}, bf16[128,3072]{1,0:T(8,128)(2,1)S(1)}, u32[]{:S(2)}, u32[]{:S(2)}) collective-permute-start(bf16[128,3072]{1,0:T(8,128)(2,1)S(1)} %pad_maximum_fusion.1), channel_id=1, source_target_pairs={{0,4},{2,6},{4,0},{6,2},{8,12},{10,14},{12,8},{14,10},{16,20},{18,... | collective-permute-start | bytes 2359304 | tf_op jit(solution)/shard_map/both_send0_1/ppermute | solution.py:505
  81.4 19.3 %collective-permute-start.13 = (bf16[128,3072]{1,0:T(8,128)(2,1)S(1)}, bf16[128,3072]{1,0:T(8,128)(2,1)S(1)}, u32[]{:S(2)}, u32[]{:S(2)}) collective-permute-start(bf16[128,3072]{1,0:T(8,128)(2,1)S(1)} %pad_maximum_fusion.2), channel_id=1, source_target_pairs={{0,8},{2,10},{4,12},{6,14},{8,0},{10,2},{12,4},{14,6},{16,24},{18,... | collective-permute-start | bytes 2359304 | tf_op jit(solution)/shard_map/both_send0_2/ppermute | solution.py:505
  100.9 10.0 %collective-permute-start.16 = (bf16[64,3072]{1,0:T(8,128)(2,1)S(1)}, bf16[64,3072]{1,0:T(8,128)(2,1)S(1)}, u32[]{:S(2)}, u32[]{:S(2)}) collective-permute-start(bf16[64,3072]{1,0:T(8,128)(2,1)S(1)} %get-tuple-element.251), channel_id=1, source_target_pairs={{0,2},{2,0},{4,6},{6,4},{8,10},{10,8},{12,14},{14,12},{16,18},{18,... | collective-permute-start | bytes 1179656 | tf_op jit(solution)/shard_map/both_send1_2/ppermute | solution.py:505
  101.7 9.7 %collective-permute-start.15 = (bf16[64,3072]{1,0:T(8,128)(2,1)S(1)}, bf16[64,3072]{1,0:T(8,128)(2,1)S(1)}, u32[]{:S(2)}, u32[]{:S(2)}) collective-permute-start(bf16[64,3072]{1,0:T(8,128)(2,1)S(1)} %get-tuple-element.253), channel_id=1, source_target_pairs={{0,8},{2,10},{4,12},{6,14},{8,0},{10,2},{12,4},{14,6},{16,24},{18,... | collective-permute-start | bytes 1179656 | tf_op jit(solution)/shard_map/both_send1_1/ppermute | solution.py:505
  103.6 9.4 %collective-permute-start.14 = (bf16[64,3072]{1,0:T(8,128)(2,1)S(1)}, bf16[64,3072]{1,0:T(8,128)(2,1)S(1)}, u32[]{:S(2)}, u32[]{:S(2)}) collective-permute-start(bf16[64,3072]{1,0:T(8,128)(2,1)S(1)} %get-tuple-element.255), channel_id=1, source_target_pairs={{0,4},{2,6},{4,0},{6,2},{8,12},{10,14},{12,8},{14,10},{16,20},{18,... | collective-permute-start | bytes 1179656 | tf_op jit(solution)/shard_map/both_send1_0/ppermute | solution.py:505
  113.1 10.1 %collective-permute-start.23 = (bf16[32,3072]{1,0:T(8,128)(2,1)S(1)}, bf16[32,3072]{1,0:T(8,128)(2,1)S(1)}, u32[]{:S(2)}, u32[]{:S(2)}) collective-permute-start(bf16[32,3072]{1,0:T(8,128)(2,1)S(1)} %add_convert_fusion.32), channel_id=1, source_target_pairs={{0,4},{2,6},{4,0},{6,2},{8,12},{10,14},{12,8},{14,10},{16,20},{18,... | collective-permute-start | bytes 589832 | tf_op jit(solution)/shard_map/both_send2_2/ppermute | solution.py:505
  113.7 10.2 %collective-permute-start.22 = (bf16[32,3072]{1,0:T(8,128)(2,1)S(1)}, bf16[32,3072]{1,0:T(8,128)(2,1)S(1)}, u32[]{:S(2)}, u32[]{:S(2)}) collective-permute-start(bf16[32,3072]{1,0:T(8,128)(2,1)S(1)} %add_convert_fusion.33), channel_id=1, source_target_pairs={{0,2},{2,0},{4,6},{6,4},{8,10},{10,8},{12,14},{14,12},{16,18},{18,... | collective-permute-start | bytes 589832 | tf_op jit(solution)/shard_map/both_send2_1/ppermute | solution.py:505
  115.3 8.6 %collective-permute-start.21 = (bf16[32,3072]{1,0:T(8,128)(2,1)S(1)}, bf16[32,3072]{1,0:T(8,128)(2,1)S(1)}, u32[]{:S(2)}, u32[]{:S(2)}) collective-permute-start(bf16[32,3072]{1,0:T(8,128)(2,1)S(1)} %add_convert_fusion.34), channel_id=1, source_target_pairs={{0,8},{2,10},{4,12},{6,14},{8,0},{10,2},{12,4},{14,6},{16,24},{18,... | collective-permute-start | bytes 589832 | tf_op jit(solution)/shard_map/both_send2_0/ppermute | solution.py:505
  115.8 11.0 %collective-permute-start.19 = (bf16[128,1536]{1,0:T(8,128)(2,1)S(1)}, bf16[128,1536]{1,0:T(8,128)(2,1)S(1)}, u32[]{:S(2)}, u32[]{:S(2)}) collective-permute-start(bf16[128,1536]{1,0:T(8,128)(2,1)S(1)} %get-tuple-element.186), channel_id=1, source_target_pairs={{0,4},{2,6},{4,0},{6,2},{8,12},{10,14},{12,8},{14,10},{16,20},{18,... | collective-permute-start | bytes 1179656 | tf_op jit(solution)/shard_map/last_send0_1/ppermute | solution.py:505
  117.3 10.1 %collective-permute-start.20 = (bf16[128,1536]{1,0:T(8,128)(2,1)S(1)}, bf16[128,1536]{1,0:T(8,128)(2,1)S(1)}, u32[]{:S(2)}, u32[]{:S(2)}) collective-permute-start(bf16[128,1536]{1,0:T(8,128)(2,1)S(1)} %get-tuple-element.187), channel_id=1, source_target_pairs={{0,8},{2,10},{4,12},{6,14},{8,0},{10,2},{12,4},{14,6},{16,24},{18,... | collective-permute-start | bytes 1179656 | tf_op jit(solution)/shard_map/last_send0_2/ppermute | solution.py:505
  123.2 9.9 %collective-permute-start.18 = (bf16[144,1536]{1,0:T(8,128)(2,1)S(1)}, bf16[144,1536]{1,0:T(8,128)(2,1)S(1)}, u32[]{:S(2)}, u32[]{:S(2)}) collective-permute-start(bf16[144,1536]{1,0:T(8,128)(2,1)S(1)} %get-tuple-element.185), channel_id=1, source_target_pairs={{0,2},{2,0},{4,6},{6,4},{8,10},{10,8},{12,14},{14,12},{16,18},{18,... | collective-permute-start | bytes 1327112 | tf_op jit(solution)/shard_map/last_send0_0/ppermute | solution.py:505
  123.8 25.2 %collective-permute-start.17 = (bf16[512,768]{1,0:T(8,128)(2,1)S(1)}, bf16[512,768]{1,0:T(8,128)(2,1)S(1)}, u32[]{:S(2)}, u32[]{:S(2)}) collective-permute-start(bf16[512,768]{1,0:T(8,128)(2,1)S(1)} %get-tuple-element.191), channel_id=1, source_target_pairs={{0,1},{1,0},{2,3},{3,2},{4,5},{5,4},{6,7},{7,6},{8,9},{9,8},{10,11... | collective-permute-start | bytes 2359304 | tf_op jit(solution)/shard_map/ppermute | solution.py:509
  124.1 32.6 %collective-permute-start.31 = (bf16[96,3072]{1,0:T(8,128)(2,1)S(1)}, bf16[96,3072]{1,0:T(8,128)(2,1)S(1)}, u32[]{:S(2)}, u32[]{:S(2)}) collective-permute-start(bf16[96,3072]{1,0:T(8,128)(2,1)S(1)} %pad_maximum_fusion.6), channel_id=1, source_target_pairs={{0,16},{2,18},{4,20},{6,22},{8,24},{10,26},{12,28},{14,30},{16,0},... | collective-permute-start | bytes 1769480 | tf_op jit(solution)/shard_map/both_exchange/ppermute | solution.py:505
  133.4 5.7 %collective-permute-start.26 = (bf16[64,1536]{1,0:T(8,128)(2,1)S(1)}, bf16[64,1536]{1,0:T(8,128)(2,1)S(1)}, u32[]{:S(2)}, u32[]{:S(2)}) collective-permute-start(bf16[64,1536]{1,0:T(8,128)(2,1)S(1)} %get-tuple-element.259), channel_id=1, source_target_pairs={{0,2},{2,0},{4,6},{6,4},{8,10},{10,8},{12,14},{14,12},{16,18},{18,... | collective-permute-start | bytes 589832 | tf_op jit(solution)/shard_map/last_send1_2/ppermute | solution.py:505
  133.5 10.8 %collective-permute-start.25 = (bf16[64,1536]{1,0:T(8,128)(2,1)S(1)}, bf16[64,1536]{1,0:T(8,128)(2,1)S(1)}, u32[]{:S(2)}, u32[]{:S(2)}) collective-permute-start(bf16[64,1536]{1,0:T(8,128)(2,1)S(1)} %get-tuple-element.261), channel_id=1, source_target_pairs={{0,8},{2,10},{4,12},{6,14},{8,0},{10,2},{12,4},{14,6},{16,24},{18,... | collective-permute-start | bytes 589832 | tf_op jit(solution)/shard_map/last_send1_1/ppermute | solution.py:505
  134.1 11.8 %collective-permute-start.24 = (bf16[80,1536]{1,0:T(8,128)(2,1)S(1)}, bf16[80,1536]{1,0:T(8,128)(2,1)S(1)}, u32[]{:S(2)}, u32[]{:S(2)}) collective-permute-start(bf16[80,1536]{1,0:T(8,128)(2,1)S(1)} %pad_maximum_fusion.17), channel_id=1, source_target_pairs={{0,4},{2,6},{4,0},{6,2},{8,12},{10,14},{12,8},{14,10},{16,20},{18,... | collective-permute-start | bytes 737288 | tf_op jit(solution)/shard_map/last_send1_0/ppermute | solution.py:505
  139.2 9.4 %collective-permute-start.29 = (bf16[32,1536]{1,0:T(8,128)(2,1)S(1)}, bf16[32,1536]{1,0:T(8,128)(2,1)S(1)}, u32[]{:S(2)}, u32[]{:S(2)}) collective-permute-start(bf16[32,1536]{1,0:T(8,128)(2,1)S(1)} %add_convert_fusion.41), channel_id=1, source_target_pairs={{0,4},{2,6},{4,0},{6,2},{8,12},{10,14},{12,8},{14,10},{16,20},{18,... | collective-permute-start | bytes 294920 | tf_op jit(solution)/shard_map/last_send2_2/ppermute | solution.py:505
  144.3 4.7 %collective-permute-start.28 = (bf16[32,1536]{1,0:T(8,128)(2,1)S(1)}, bf16[32,1536]{1,0:T(8,128)(2,1)S(1)}, u32[]{:S(2)}, u32[]{:S(2)}) collective-permute-start(bf16[32,1536]{1,0:T(8,128)(2,1)S(1)} %add_convert_fusion.42), channel_id=1, source_target_pairs={{0,2},{2,0},{4,6},{6,4},{8,10},{10,8},{12,14},{14,12},{16,18},{18,... | collective-permute-start | bytes 294920 | tf_op jit(solution)/shard_map/last_send2_1/ppermute | solution.py:505
  146.0 10.6 %collective-permute-start.27 = (bf16[48,1536]{1,0:T(8,128)(2,1)S(1)}, bf16[48,1536]{1,0:T(8,128)(2,1)S(1)}, u32[]{:S(2)}, u32[]{:S(2)}) collective-permute-start(bf16[48,1536]{1,0:T(8,128)(2,1)S(1)} %pad_maximum_fusion.21), channel_id=1, source_target_pairs={{0,8},{2,10},{4,12},{6,14},{8,0},{10,2},{12,4},{14,6},{16,24},{18,... | collective-permute-start | bytes 442376 | tf_op jit(solution)/shard_map/last_send2_0/ppermute | solution.py:505
  156.9 6.9 %collective-permute-start.34 = (bf16[32,3072]{1,0:T(8,128)(2,1)S(1)}, bf16[32,3072]{1,0:T(8,128)(2,1)S(1)}, u32[]{:S(2)}, u32[]{:S(2)}) collective-permute-start(bf16[32,3072]{1,0:T(8,128)(2,1)S(1)} %get-tuple-element.262), channel_id=1, source_target_pairs={{0,4},{2,6},{4,0},{6,2},{8,12},{10,14},{12,8},{14,10},{16,20},{18,... | collective-permute-start | bytes 589832 | tf_op jit(solution)/shard_map/both_gather2_2/ppermute | solution.py:505
  158.8 18.0 %collective-permute-start.30 = (bf16[112,1536]{1,0:T(8,128)(2,1)S(1)}, bf16[112,1536]{1,0:T(8,128)(2,1)S(1)}, u32[]{:S(2)}, u32[]{:S(2)}) collective-permute-start(bf16[112,1536]{1,0:T(8,128)(2,1)S(1)} %pad_maximum_fusion.16), channel_id=1, source_target_pairs={{0,16},{2,18},{4,20},{6,22},{8,24},{10,26},{12,28},{14,30},{16,0},... | collective-permute-start | bytes 1032200 | tf_op jit(solution)/shard_map/last_exchange/ppermute | solution.py:505
  159.4 6.3 %collective-permute-start.33 = (bf16[32,3072]{1,0:T(8,128)(2,1)S(1)}, bf16[32,3072]{1,0:T(8,128)(2,1)S(1)}, u32[]{:S(2)}, u32[]{:S(2)}) collective-permute-start(bf16[32,3072]{1,0:T(8,128)(2,1)S(1)} %get-tuple-element.263), channel_id=1, source_target_pairs={{0,2},{2,0},{4,6},{6,4},{8,10},{10,8},{12,14},{14,12},{16,18},{18,... | collective-permute-start | bytes 589832 | tf_op jit(solution)/shard_map/both_gather2_1/ppermute | solution.py:505
  160.9 11.3 %collective-permute-start.32 = (bf16[32,3072]{1,0:T(8,128)(2,1)S(1)}, bf16[32,3072]{1,0:T(8,128)(2,1)S(1)}, u32[]{:S(2)}, u32[]{:S(2)}) collective-permute-start(bf16[32,3072]{1,0:T(8,128)(2,1)S(1)} %get-tuple-element.264), channel_id=1, source_target_pairs={{0,8},{2,10},{4,12},{6,14},{8,0},{10,2},{12,4},{14,6},{16,24},{18,... | collective-permute-start | bytes 589832 | tf_op jit(solution)/shard_map/both_gather2_0/ppermute | solution.py:505
  163.9 16.1 %collective-permute-start.40 = (bf16[64,3072]{1,0:T(8,128)(2,1)S(1)}, bf16[64,3072]{1,0:T(8,128)(2,1)S(1)}, u32[]{:S(2)}, u32[]{:S(2)}) collective-permute-start(bf16[64,3072]{1,0:T(8,128)(2,1)S(1)} %pad_maximum_fusion.12), channel_id=1, source_target_pairs={{0,2},{2,0},{4,6},{6,4},{8,10},{10,8},{12,14},{14,12},{16,18},{18,... | collective-permute-start | bytes 1179656 | tf_op jit(solution)/shard_map/both_gather1_2/ppermute | solution.py:505
  165.7 18.7 %collective-permute-start.39 = (bf16[64,3072]{1,0:T(8,128)(2,1)S(1)}, bf16[64,3072]{1,0:T(8,128)(2,1)S(1)}, u32[]{:S(2)}, u32[]{:S(2)}) collective-permute-start(bf16[64,3072]{1,0:T(8,128)(2,1)S(1)} %pad_maximum_fusion.11), channel_id=1, source_target_pairs={{0,8},{2,10},{4,12},{6,14},{8,0},{10,2},{12,4},{14,6},{16,24},{18,... | collective-permute-start | bytes 1179656 | tf_op jit(solution)/shard_map/both_gather1_1/ppermute | solution.py:505
  172.2 12.2 %collective-permute-start.38 = (bf16[64,3072]{1,0:T(8,128)(2,1)S(1)}, bf16[64,3072]{1,0:T(8,128)(2,1)S(1)}, u32[]{:S(2)}, u32[]{:S(2)}) collective-permute-start(bf16[64,3072]{1,0:T(8,128)(2,1)S(1)} %pad_maximum_fusion.10), channel_id=1, source_target_pairs={{0,4},{2,6},{4,0},{6,2},{8,12},{10,14},{12,8},{14,10},{16,20},{18,... | collective-permute-start | bytes 1179656 | tf_op jit(solution)/shard_map/both_gather1_0/ppermute | solution.py:505
  176.9 7.7 %collective-permute-start.37 = (bf16[32,1536]{1,0:T(8,128)(2,1)S(1)}, bf16[32,1536]{1,0:T(8,128)(2,1)S(1)}, u32[]{:S(2)}, u32[]{:S(2)}) collective-permute-start(bf16[32,1536]{1,0:T(8,128)(2,1)S(1)} %get-tuple-element.265), channel_id=1, source_target_pairs={{0,4},{2,6},{4,0},{6,2},{8,12},{10,14},{12,8},{14,10},{16,20},{18,... | collective-permute-start | bytes 294920 | tf_op jit(solution)/shard_map/last_gather2_2/ppermute | solution.py:505
  178.4 6.2 %collective-permute-start.36 = (bf16[32,1536]{1,0:T(8,128)(2,1)S(1)}, bf16[32,1536]{1,0:T(8,128)(2,1)S(1)}, u32[]{:S(2)}, u32[]{:S(2)}) collective-permute-start(bf16[32,1536]{1,0:T(8,128)(2,1)S(1)} %get-tuple-element.266), channel_id=1, source_target_pairs={{0,2},{2,0},{4,6},{6,4},{8,10},{10,8},{12,14},{14,12},{16,18},{18,... | collective-permute-start | bytes 294920 | tf_op jit(solution)/shard_map/last_gather2_1/ppermute | solution.py:505
  179.9 5.5 %collective-permute-start.35 = (bf16[32,1536]{1,0:T(8,128)(2,1)S(1)}, bf16[32,1536]{1,0:T(8,128)(2,1)S(1)}, u32[]{:S(2)}, u32[]{:S(2)}) collective-permute-start(bf16[32,1536]{1,0:T(8,128)(2,1)S(1)} %get-tuple-element.267), channel_id=1, source_target_pairs={{0,8},{2,10},{4,12},{6,14},{8,0},{10,2},{12,4},{14,6},{16,24},{18,... | collective-permute-start | bytes 294920 | tf_op jit(solution)/shard_map/last_gather2_0/ppermute | solution.py:505
  185.5 7.9 %collective-permute-start.43 = (bf16[64,1536]{1,0:T(8,128)(2,1)S(1)}, bf16[64,1536]{1,0:T(8,128)(2,1)S(1)}, u32[]{:S(2)}, u32[]{:S(2)}) collective-permute-start(bf16[64,1536]{1,0:T(8,128)(2,1)S(1)} %pad_maximum_fusion.20), channel_id=1, source_target_pairs={{0,2},{2,0},{4,6},{6,4},{8,10},{10,8},{12,14},{14,12},{16,18},{18,... | collective-permute-start | bytes 589832 | tf_op jit(solution)/shard_map/last_gather1_2/ppermute | solution.py:505
  187.0 6.9 %collective-permute-start.42 = (bf16[64,1536]{1,0:T(8,128)(2,1)S(1)}, bf16[64,1536]{1,0:T(8,128)(2,1)S(1)}, u32[]{:S(2)}, u32[]{:S(2)}) collective-permute-start(bf16[64,1536]{1,0:T(8,128)(2,1)S(1)} %pad_maximum_fusion.19), channel_id=1, source_target_pairs={{0,8},{2,10},{4,12},{6,14},{8,0},{10,2},{12,4},{14,6},{16,24},{18,... | collective-permute-start | bytes 589832 | tf_op jit(solution)/shard_map/last_gather1_1/ppermute | solution.py:505
  187.0 7.8 %collective-permute-start.41 = (bf16[64,1536]{1,0:T(8,128)(2,1)S(1)}, bf16[64,1536]{1,0:T(8,128)(2,1)S(1)}, u32[]{:S(2)}, u32[]{:S(2)}) collective-permute-start(bf16[64,1536]{1,0:T(8,128)(2,1)S(1)} %pad_maximum_fusion.18), channel_id=1, source_target_pairs={{0,4},{2,6},{4,0},{6,2},{8,12},{10,14},{12,8},{14,10},{16,20},{18,... | collective-permute-start | bytes 589832 | tf_op jit(solution)/shard_map/last_gather1_0/ppermute | solution.py:505
  188.6 19.6 %collective-permute-start.47 = (bf16[128,3072]{1,0:T(8,128)(2,1)S(1)}, bf16[128,3072]{1,0:T(8,128)(2,1)}, u32[]{:S(2)}, u32[]{:S(2)}) collective-permute-start(bf16[128,3072]{1,0:T(8,128)(2,1)S(1)} %pad_maximum_fusion.3.refs_0_), channel_id=1, source_target_pairs={{0,2},{2,0},{4,6},{6,4},{8,10},{10,8},{12,14},{14,12},{16,18},{18,... | collective-permute-start | bytes 2359304 | tf_op jit(solution)/shard_map/both_gather0_0/ppermute | solution.py:505
  189.2 22.7 %collective-permute-start.48 = (bf16[128,3072]{1,0:T(8,128)(2,1)S(1)}, bf16[128,3072]{1,0:T(8,128)(2,1)}, u32[]{:S(2)}, u32[]{:S(2)}) collective-permute-start(bf16[128,3072]{1,0:T(8,128)(2,1)S(1)} %pad_maximum_fusion.4.refs_1_), channel_id=1, source_target_pairs={{0,4},{2,6},{4,0},{6,2},{8,12},{10,14},{12,8},{14,10},{16,20},{18,... | collective-permute-start | bytes 2359304 | tf_op jit(solution)/shard_map/both_gather0_1/ppermute | solution.py:505
  193.4 20.5 %collective-permute-start.49 = (bf16[128,3072]{1,0:T(8,128)(2,1)S(1)}, bf16[128,3072]{1,0:T(8,128)(2,1)}, u32[]{:S(2)}, u32[]{:S(2)}) collective-permute-start(bf16[128,3072]{1,0:T(8,128)(2,1)S(1)} %pad_maximum_fusion.5.refs_2_), channel_id=1, source_target_pairs={{0,8},{2,10},{4,12},{6,14},{8,0},{10,2},{12,4},{14,6},{16,24},{18,... | collective-permute-start | bytes 2359304 | tf_op jit(solution)/shard_map/both_gather0_2/ppermute | solution.py:505
  194.9 26.1 %collective-permute-start.46 = (bf16[128,1536]{1,0:T(8,128)(2,1)S(1)}, bf16[128,1536]{1,0:T(8,128)(2,1)}, u32[]{:S(2)}, u32[]{:S(2)}) collective-permute-start(bf16[128,1536]{1,0:T(8,128)(2,1)S(1)} %pad_maximum_fusion.15.refs_2_), channel_id=1, source_target_pairs={{0,8},{2,10},{4,12},{6,14},{8,0},{10,2},{12,4},{14,6},{16,24},{18,... | collective-permute-start | bytes 1179656 | tf_op jit(solution)/shard_map/last_gather0_2/ppermute | solution.py:505
  197.0 24.0 %collective-permute-start.45 = (bf16[128,1536]{1,0:T(8,128)(2,1)S(1)}, bf16[128,1536]{1,0:T(8,128)(2,1)}, u32[]{:S(2)}, u32[]{:S(2)}) collective-permute-start(bf16[128,1536]{1,0:T(8,128)(2,1)S(1)} %pad_maximum_fusion.14.refs_1_), channel_id=1, source_target_pairs={{0,4},{2,6},{4,0},{6,2},{8,12},{10,14},{12,8},{14,10},{16,20},{18,... | collective-permute-start | bytes 1179656 | tf_op jit(solution)/shard_map/last_gather0_1/ppermute | solution.py:505
  208.2 12.9 %collective-permute-start.44 = (bf16[128,1536]{1,0:T(8,128)(2,1)S(1)}, bf16[128,1536]{1,0:T(8,128)(2,1)S(1)}, u32[]{:S(2)}, u32[]{:S(2)}) collective-permute-start(bf16[128,1536]{1,0:T(8,128)(2,1)S(1)} %pad_maximum_fusion.13.refs_0_), channel_id=1, source_target_pairs={{0,2},{2,0},{4,6},{6,4},{8,10},{10,8},{12,14},{14,12},{16,18},{18,... | collective-permute-start | bytes 1179656 | tf_op jit(solution)/shard_map/last_gather0_0/ppermute | solution.py:505
  (27 other events, 395.4 us)
